TPU v7x, 32 devices: a whole 2x2x4 slice. The times are simulated.
32 devices in a mesh: pipe: 2 (over x), expert: 4 (over y, core), dp: 4 (over z).
Axes of the slice: x: 2, y: 2, z: 4, core: 2. Of those that a mesh axis runs over, the one named last changes fastest.
Arguments:
- carry_forward: bfloat16 [2, 64, 7168], P('pipe', 'expert', 'dp'), may hold values from -6 to 6
- carry_cotangent: bfloat16 [2, 64, 7168], P('pipe', 'expert', 'dp'), may hold values from -6 to 6
- saved_input: bfloat16 [2, 64, 7168], P('pipe', 'expert', 'dp'), may hold values from -6 to 6
- routes_forward: int32 [2, 64, 1], P('pipe', 'expert'), may hold values from 0 to 1; in each aligned block of 16 rows (0 to 15, 16 to 31, ..., all dimensions but the last counted through in order) at most 10 rows name the same one
- gates_forward: bfloat16 [2, 64, 1], P('pipe', 'expert'), may hold values from 0.049804688 to 0.59765625
- routes_backward: int32 [2, 64, 1], P('pipe', 'expert'), may hold values from 0 to 1; in each aligned block of 16 rows (0 to 15, 16 to 31, ..., all dimensions but the last counted through in order) at most 10 rows name the same one
- gates_backward: bfloat16 [2, 64, 1], P('pipe', 'expert'), may hold values from 0.049804688 to 0.59765625
- w_gate: bfloat16 [2, 4, 7168, 512], P('pipe', 'expert', 'dp'), may hold values from -0.0625 to 0.0625
- w_up: bfloat16 [2, 4, 7168, 512], P('pipe', 'expert', 'dp'), may hold values from -0.0625 to 0.0625
- w_down: bfloat16 [2, 4, 512, 7168], P('pipe', 'expert', None, 'dp'), may hold values from -0.1875 to 0.1875
Outputs:
- forward_out: bfloat16 [2, 64, 7168], P('pipe', 'expert', 'dp')
- backward_out: bfloat16 [2, 64, 7168], P('pipe', 'expert', 'dp')
Inputs may be any that keep to these rules, and one draw needn't show every extreme that they name: `routes_forward`: within each section, the 16 tokens of one index of expert name any one expert at most 10 times; in some such blocks an expert is named exactly 10 times. A token names 1 different experts. `routes_backward`: as for routes_forward.
All inputs are finite; a program needn't handle non-finite values.
Results may differ from a plain program's by a relative error of at most 0.0032.
Values may be sent and summed in bfloat16 or wider, within the bound.
No kernel may reach another device: no remote copies, remote signals or barrier semaphores. Data moves between devices by JAX's collectives and lax.ppermute only.
A program may use at most 64 MiB of HBM per device.

v0:
```python
import jax
import jax.numpy as jnp
from jax import lax
from jax.sharding import PartitionSpec as P


def from_behind(x, axis, by):
    peers = lax.axis_size(axis)
    return lax.ppermute(x, axis, [(i, (i + by) % peers) for i in range(peers)])


def tables(routes, gates, experts, capacity):
    kinds = jnp.arange(experts, dtype=jnp.int32)
    onehot = (routes[:, :, None] == kinds).astype(jnp.int32).reshape(-1, experts)
    before = jnp.cumsum(onehot, axis=0) - onehot
    slot = jnp.sum(before * onehot, axis=1).reshape(routes.shape)
    index = routes * capacity + slot
    columns = jnp.arange(experts * capacity, dtype=jnp.int32)
    hit = index[:, :, None] == columns
    place = jnp.sum(hit.astype(jnp.float32), axis=1).astype(jnp.bfloat16)
    weigh = jnp.sum(jnp.where(hit, gates.astype(jnp.float32)[:, :, None], 0.0), axis=1).astype(
        jnp.bfloat16
    )
    return (place, weigh)


def scatter_rows(table, rows, experts, capacity):
    sent = jnp.einsum("tj,td->jd", table, rows, preferred_element_type=jnp.float32).astype(
        jnp.bfloat16
    )
    sent = sent.reshape(experts, capacity, rows.shape[1])
    return jnp.repeat(sent, 2, axis=0).reshape(2 * experts * capacity, rows.shape[1])


def widen(table, experts, capacity):
    wide = table.reshape(table.shape[0], experts, capacity)
    return jnp.repeat(wide, 2, axis=1).reshape(table.shape[0], 2 * experts * capacity)


def backward_terms(gate_b, upper_b, dhid):
    sigma = jax.nn.sigmoid(gate_b)
    active = gate_b * sigma
    slope = sigma * (1.0 + gate_b * (1.0 - sigma))
    dgate = (dhid * upper_b * slope).astype(jnp.bfloat16)
    dupper = (dhid * active).astype(jnp.bfloat16)
    return (dgate, dupper)


def input_grad(dgate, dupper, w_g, w_u):
    half_grad = jnp.einsum("rh,dh->rd", dgate, w_g, preferred_element_type=jnp.float32)
    half_grad = half_grad + jnp.einsum("rh,dh->rd", dupper, w_u, preferred_element_type=jnp.float32)
    return half_grad.astype(jnp.bfloat16)


def local(
    carry_forward,
    carry_cotangent,
    saved_input,
    routes_forward,
    gates_forward,
    routes_backward,
    gates_backward,
    w_gate,
    w_up,
    w_down,
):
    experts = lax.axis_size("expert") // 2
    tok_rows = carry_forward.shape[1]
    topk = routes_forward.shape[2]
    capacity = min(tok_rows, max(6, tok_rows * topk // experts + 2))
    stacked = jnp.concatenate((carry_forward, carry_cotangent), axis=0)
    arrived = from_behind(stacked, "pipe", 1)
    x_fwd = arrived[0]
    c_bwd = arrived[1]
    x_bwd = saved_input[0]
    place_f, weigh_f = tables(routes_forward[0], gates_forward[0], experts, capacity)
    place_b, weigh_b = tables(routes_backward[0], gates_backward[0], experts, capacity)
    send_f = scatter_rows(place_f, x_fwd, experts, capacity)
    send_b = scatter_rows(place_b, x_bwd, experts, capacity)
    send_c = scatter_rows(weigh_b, c_bwd, experts, capacity)
    rows_f, rows_b, grads_b = (
        lax.all_to_all(send_f, "expert", split_axis=0, concat_axis=0, tiled=True),
        lax.all_to_all(send_b, "expert", split_axis=0, concat_axis=0, tiled=True),
        lax.all_to_all(send_c, "expert", split_axis=0, concat_axis=0, tiled=True),
    )
    w_g = w_gate[0, 0]
    w_u = w_up[0, 0]
    w_d = w_down[0, 0]
    part_gf = jnp.dot(rows_f, w_g, preferred_element_type=jnp.float32)
    part_uf = jnp.dot(rows_f, w_u, preferred_element_type=jnp.float32)
    part_gb = jnp.dot(rows_b, w_g, preferred_element_type=jnp.float32)
    part_ub = jnp.dot(rows_b, w_u, preferred_element_type=jnp.float32)
    part_dh = jnp.einsum("rd,hd->rh", grads_b, w_d, preferred_element_type=jnp.float32)
    gate_f, upper_f, gate_b, upper_b, dhid = (
        lax.psum_scatter(part_gf, "dp", scatter_dimension=1, tiled=True),
        lax.psum_scatter(part_uf, "dp", scatter_dimension=1, tiled=True),
        lax.psum_scatter(part_gb, "dp", scatter_dimension=1, tiled=True),
        lax.psum_scatter(part_ub, "dp", scatter_dimension=1, tiled=True),
        lax.psum_scatter(part_dh, "dp", scatter_dimension=1, tiled=True),
    )
    hidden = (jax.nn.silu(gate_f) * upper_f).astype(jnp.bfloat16)
    dgate, dupper = backward_terms(gate_b, upper_b, dhid)
    hidden, dgate, dupper = (
        lax.all_gather(hidden, "dp", axis=1, tiled=True),
        lax.all_gather(dgate, "dp", axis=1, tiled=True),
        lax.all_gather(dupper, "dp", axis=1, tiled=True),
    )
    out_f = jnp.dot(hidden, w_d, preferred_element_type=jnp.float32).astype(jnp.bfloat16)
    half_grad = input_grad(dgate, dupper, w_g, w_u)
    back_f, back_b = (
        lax.all_to_all(out_f, "expert", split_axis=0, concat_axis=0, tiled=True),
        lax.all_to_all(half_grad, "expert", split_axis=0, concat_axis=0, tiled=True),
    )
    result_f = x_fwd.astype(jnp.float32) + jnp.dot(
        widen(weigh_f, experts, capacity), back_f, preferred_element_type=jnp.float32
    )
    result_b = c_bwd.astype(jnp.float32) + jnp.dot(
        widen(place_b, experts, capacity), back_b, preferred_element_type=jnp.float32
    )
    return (result_f.astype(jnp.bfloat16)[None], result_b.astype(jnp.bfloat16)[None])


def solution(mesh):
    placed = (
        P("pipe", "expert", "dp"),
        P("pipe", "expert", "dp"),
        P("pipe", "expert", "dp"),
        P("pipe", "expert", None),
        P("pipe", "expert", None),
        P("pipe", "expert", None),
        P("pipe", "expert", None),
        P("pipe", "expert", "dp", None),
        P("pipe", "expert", "dp", None),
        P("pipe", "expert", None, "dp"),
    )
    return jax.shard_map(
        local,
        mesh=mesh,
        in_specs=placed,
        out_specs=(P("pipe", "expert", "dp"), P("pipe", "expert", "dp")),
        check_vma=False,
    )
```

profile of v0, /device:TPU:0, one launch (start us, length us, event | category | flops | bytes accessed | tf_op | source)
XLA Modules:
  0.0 176.8 jit_solution(17535556467476079711)
XLA Ops:
  7.2 1.0 pad_maximum_fusion
  8.2 3.0 %collective-permute-start = (bf16[2,16,1792]{2,1,0:T(8,128)(2,1)S(1)}, bf16[2,16,1792]{2,1,0:T(8,128)(2,1)S(1)}, u32[]{:S(2)}, u32[]{:S(2)}) collective-permute-start(bf16[2,16,1792]{2,1,0:T(8,128)(2,1)S(1)} %pad_maximum_fusion), channel_id=1, source_target_pairs={{0,16},{16,0},{1,17},{17,1},{2,18},{18,2},{3,19},{19,3},{4,20},{20... | collective-permute-start | bytes 344072 | tf_op jit(solution)/shard_map/ppermute | solution.py:9
  11.9 0.8 select_reduce_fusion
  13.4 1.1 convolution_convert_fusion.1
  15.3 3.4 %all-to-all-start.3 = ((bf16[4,10,1792]{2,1,0:T(8,128)(2,1)}), bf16[4,10,1792]{2,1,0:T(8,128)(2,1)S(1)}, u32[]{:S(2)}, u32[]{:S(2)}) async-start(bf16[4,10,1792]{2,1,0:T(8,128)(2,1)} %bitcast.16), calls=%async_computation.6 | async-start | bytes 458752 | tf_op jit(solution)/shard_map/all_to_all | solution.py:83
  19.4 0.8 select_reduce_fusion.1
  22.0 2.3 %all-to-all-done.3 = bf16[4,10,1792]{2,1,0:T(8,128)(2,1)S(1)} async-done(((bf16[4,10,1792]{2,1,0:T(8,128)(2,1)}), bf16[4,10,1792]{2,1,0:T(8,128)(2,1)S(1)}, u32[]{:S(2)}, u32[]{:S(2)}) %all-to-all-start.3) | async-done | bytes 143392 | tf_op jit(solution)/shard_map/all_to_all | solution.py:83
  25.0 3.4 %all-to-all-start = ((bf16[4,10,1792]{2,1,0:T(8,128)(2,1)}), bf16[4,10,1792]{2,1,0:T(8,128)(2,1)S(1)}, u32[]{:S(2)}, u32[]{:S(2)}) async-start(bf16[4,10,1792]{2,1,0:T(8,128)(2,1)} %bitcast.4), calls=%async_computation | async-start | bytes 458752 | tf_op jit(solution)/shard_map/all_to_all | solution.py:82
  28.8 5.2 %all-to-all-done = bf16[4,10,1792]{2,1,0:T(8,128)(2,1)S(1)} async-done(((bf16[4,10,1792]{2,1,0:T(8,128)(2,1)}), bf16[4,10,1792]{2,1,0:T(8,128)(2,1)S(1)}, u32[]{:S(2)}, u32[]{:S(2)}) %all-to-all-start) | async-done | bytes 143392 | tf_op jit(solution)/shard_map/all_to_all | solution.py:82
  34.1 2.6 %fusion.7 = f32[40,512]{1,0:T(8,128)} fusion(bf16[40,1792]{1,0:T(8,128)(2,1)S(1)} %all_to_all.42, bf16[1,1,1792,512]{3,2,1,0:T(8,128)(2,1)} %param.18), kind=kOutput, calls=%fused_computation.12 | convolution fusion | flops 73400320 | bytes 2060288 | tf_op jit(solution)/shard_map/dot_general | solution.py:90
  36.8 1.1 fusion.13
  37.9 1.1 fusion.11
  40.0 3.4 %all-to-all-start.2 = ((bf16[4,10,1792]{2,1,0:T(8,128)(2,1)}), bf16[4,10,1792]{2,1,0:T(8,128)(2,1)S(1)}, u32[]{:S(2)}, u32[]{:S(2)}) async-start(bf16[4,10,1792]{2,1,0:T(8,128)(2,1)} %bitcast.13), calls=%async_computation.4 | async-start | bytes 458752 | tf_op jit(solution)/shard_map/all_to_all | solution.py:84
  43.4 2.6 %fusion.5 = f32[40,512]{1,0:T(8,128)} fusion(bf16[40,1792]{1,0:T(8,128)(2,1)S(1)} %all_to_all.51, bf16[1,1,1792,512]{3,2,1,0:T(8,128)(2,1)} %param.18), kind=kOutput, calls=%fused_computation.10 | convolution fusion | flops 73400320 | bytes 2060288 | tf_op jit(solution)/shard_map/dot_general | solution.py:92
  46.1 3.0 %all-to-all-done.2 = bf16[4,10,1792]{2,1,0:T(8,128)(2,1)S(1)} async-done(((bf16[4,10,1792]{2,1,0:T(8,128)(2,1)}), bf16[4,10,1792]{2,1,0:T(8,128)(2,1)S(1)}, u32[]{:S(2)}, u32[]{:S(2)}) %all-to-all-start.2) | async-done | bytes 143392 | tf_op jit(solution)/shard_map/all_to_all | solution.py:84
  49.1 2.8 %fusion.1 = f32[40,512]{1,0:T(8,128)} fusion(bf16[40,1792]{1,0:T(8,128)(2,1)S(1)} %all_to_all.48, bf16[1,1,512,1792]{3,2,1,0:T(8,128)(2,1)} %param.19), kind=kOutput, calls=%fused_computation.6 | convolution fusion | flops 73400320 | bytes 2060288 | tf_op jit(solution)/shard_map/rd,hd->rh/dot_general | solution.py:93
  51.9 3.4 %reduce-scatter.8.cloned.1.call-done = f32[40,128]{1,0:T(8,128)} async-done(((f32[40,512]{1,0:T(8,128)}), f32[40,128]{1,0:T(8,128)}) %reduce-scatter.8.cloned.1.call-update) | async-done | bytes 20496 | tf_op jit(solution)/shard_map/reduce_scatter | solution.py:96
  55.3 19.8 %reduce-scatter.6.cloned.1.call-done = f32[40,128]{1,0:T(8,128)} async-done(((f32[40,512]{1,0:T(8,128)}), f32[40,128]{1,0:T(8,128)}) %reduce-scatter.6.cloned.1.call-update) | async-done | bytes 20496 | tf_op jit(solution)/shard_map/reduce_scatter | solution.py:95
  75.1 0.8 multiply_convert_fusion.2
  75.9 11.9 %all_gather.9 = bf16[40,512]{1,0:T(8,128)(2,1)S(1)} all-gather(bf16[40,128]{1,0:T(8,128)(2,1)S(1)} %multiply_convert_fusion.2), channel_id=1, replica_groups=mesh['pipe'=2,'expert'=4,'dp'=4] {'dp'}, dimensions={1}, use_global_device_ids=true | all-gather | bytes 51200 | tf_op jit(solution)/shard_map/all_gather | solution.py:104
  87.8 1.9 %convolution_convert_fusion = bf16[40,1792]{1,0:T(8,128)(2,1)S(1)} fusion(bf16[40,512]{1,0:T(8,128)(2,1)S(1)} %all_gather.9, bf16[1,1,512,1792]{3,2,1,0:T(8,128)(2,1)} %param.19), kind=kOutput, calls=%fused_computation.2 | convolution fusion | flops 73472000 | bytes 2019328 | tf_op jit(solution)/shard_map/dot_general | solution.py:108
  90.4 3.4 %all-to-all-start.1 = ((bf16[4,10,1792]{2,1,0:T(8,128)(2,1)}), bf16[4,10,1792]{2,1,0:T(8,128)(2,1)S(1)}, u32[]{:S(2)}, u32[]{:S(2)}) async-start(bf16[4,10,1792]{2,1,0:T(8,128)(2,1)} %all_to_all.43), calls=%async_computation.3 | async-start | bytes 458752 | tf_op jit(solution)/shard_map/all_to_all | solution.py:111
  93.8 0.9 reduce-scatter.14.cloned.1.call-done
  94.7 19.5 %reduce-scatter.12.cloned.1.call-done = f32[40,128]{1,0:T(8,128)} async-done(((f32[40,512]{1,0:T(8,128)}), f32[40,128]{1,0:T(8,128)}) %reduce-scatter.12.cloned.1.call-update) | async-done | bytes 20496 | tf_op jit(solution)/shard_map/reduce_scatter | solution.py:98
  114.2 19.4 %reduce-scatter.10.cloned.1.call-done = f32[40,128]{1,0:T(8,128)} async-done(((f32[40,512]{1,0:T(8,128)}), f32[40,128]{1,0:T(8,128)}) %reduce-scatter.10.cloned.1.call-update) | async-done | bytes 20496 | tf_op jit(solution)/shard_map/reduce_scatter | solution.py:99
  133.7 0.9 multiply_convert_fusion
  134.6 11.9 %all_gather.10 = bf16[40,512]{1,0:T(8,128)(2,1)S(1)} all-gather(bf16[40,128]{1,0:T(8,128)(2,1)S(1)} %get-tuple-element.5), channel_id=1, replica_groups=mesh['pipe'=2,'expert'=4,'dp'=4] {'dp'}, dimensions={1}, use_global_device_ids=true | all-gather | bytes 51200 | tf_op jit(solution)/shard_map/all_gather | solution.py:105
  147.1 11.9 %all_gather.11 = bf16[40,512]{1,0:T(8,128)(2,1)S(1)} all-gather(bf16[40,128]{1,0:T(8,128)(2,1)S(1)} %get-tuple-element.4), channel_id=1, replica_groups=mesh['pipe'=2,'expert'=4,'dp'=4] {'dp'}, dimensions={1}, use_global_device_ids=true | all-gather | bytes 51200 | tf_op jit(solution)/shard_map/all_gather | solution.py:106
  159.6 0.8 all_to_all.52
  160.4 3.4 %all-to-all-start.4 = ((bf16[4,10,1792]{2,1,0:T(8,128)(2,1)}), bf16[4,10,1792]{2,1,0:T(8,128)(2,1)S(1)}, u32[]{:S(2)}, u32[]{:S(2)}) async-start(bf16[4,10,1792]{2,1,0:T(8,128)(2,1)} %all_to_all.52), calls=%async_computation.9 | async-start | bytes 458752 | tf_op jit(solution)/shard_map/all_to_all | solution.py:112
  164.0 5.4 %all-to-all-done.4 = bf16[4,10,1792]{2,1,0:T(8,128)(2,1)S(1)} async-done(((bf16[4,10,1792]{2,1,0:T(8,128)(2,1)}), bf16[4,10,1792]{2,1,0:T(8,128)(2,1)S(1)}, u32[]{:S(2)}, u32[]{:S(2)}) %all-to-all-start.4) | async-done | bytes 143392 | tf_op jit(solution)/shard_map/all_to_all | solution.py:112
  169.5 0.8 fusion.16
  (48 shorter events, 9.3 us)
Async XLA Ops:
  7.2 29.6 %copy-start = (bf16[1,1,1792,512]{3,2,1,0:T(8,128)(2,1)S(1)}, bf16[1,1,1792,512]{3,2,1,0:T(8,128)(2,1)}, u32[]{:S(2)}) copy-start(bf16[1,1,1792,512]{3,2,1,0:T(8,128)(2,1)} %param.17) | copy-start | bytes 5505028
  8.2 13.5 %collective-permute-start = (bf16[2,16,1792]{2,1,0:T(8,128)(2,1)S(1)}, bf16[2,16,1792]{2,1,0:T(8,128)(2,1)S(1)}, u32[]{:S(2)}, u32[]{:S(2)}) collective-permute-start(bf16[2,16,1792]{2,1,0:T(8,128)(2,1)S(1)} %pad_maximum_fusion), channel_id=1, source_target_pairs={{0,16},{16,0},{1,17},{17,1},{2,18},{18,2},{3,19},{19,3},{4,20},{20... | collective-permute-start | bytes 344072 | tf_op jit(solution)/shard_map/ppermute | solution.py:9
  15.3 9.0 %all-to-all-start.3 = ((bf16[4,10,1792]{2,1,0:T(8,128)(2,1)}), bf16[4,10,1792]{2,1,0:T(8,128)(2,1)S(1)}, u32[]{:S(2)}, u32[]{:S(2)}) async-start(bf16[4,10,1792]{2,1,0:T(8,128)(2,1)} %bitcast.16), calls=%async_computation.6 | async-start | bytes 458752 | tf_op jit(solution)/shard_map/all_to_all | solution.py:83
  25.0 9.0 %all-to-all-start = ((bf16[4,10,1792]{2,1,0:T(8,128)(2,1)}), bf16[4,10,1792]{2,1,0:T(8,128)(2,1)S(1)}, u32[]{:S(2)}, u32[]{:S(2)}) async-start(bf16[4,10,1792]{2,1,0:T(8,128)(2,1)} %bitcast.4), calls=%async_computation | async-start | bytes 458752 | tf_op jit(solution)/shard_map/all_to_all | solution.py:82
  28.4 26.9 %reduce-scatter.8.cloned.1.call-start = ((), (), s32[]{:S(2)}) async-start(), calls=%async_computation.11 | async-start | bytes 102400 | tf_op jit(solution)/shard_map/reduce_scatter | solution.py:96
  36.7 2.3 %copy-start.2 = (bf16[1,16,1]{1,2,0:T(2,128)(2,1)S(1)}, bf16[1,16,1]{1,2,0:T(2,128)(2,1)}, u32[]{:S(2)}) copy-start(bf16[1,16,1]{1,2,0:T(2,128)(2,1)} %param.16) | copy-start | bytes 100
  36.7 38.4 %reduce-scatter.6.cloned.1.call-start = ((), (), s32[]{:S(2)}) async-start(), calls=%async_computation.10 | async-start | bytes 102400 | tf_op jit(solution)/shard_map/reduce_scatter | solution.py:95
  37.8 56.9 %reduce-scatter.14.cloned.1.call-start = ((), (), s32[]{:S(2)}) async-start(), calls=%async_computation.14 | async-start | bytes 102400 | tf_op jit(solution)/shard_map/reduce_scatter | solution.py:97
  40.0 9.0 %all-to-all-start.2 = ((bf16[4,10,1792]{2,1,0:T(8,128)(2,1)}), bf16[4,10,1792]{2,1,0:T(8,128)(2,1)S(1)}, u32[]{:S(2)}, u32[]{:S(2)}) async-start(bf16[4,10,1792]{2,1,0:T(8,128)(2,1)} %bitcast.13), calls=%async_computation.4 | async-start | bytes 458752 | tf_op jit(solution)/shard_map/all_to_all | solution.py:84
  43.4 70.8 %reduce-scatter.12.cloned.1.call-start = ((), (), s32[]{:S(2)}) async-start(), calls=%async_computation.13 | async-start | bytes 102400 | tf_op jit(solution)/shard_map/reduce_scatter | solution.py:98
  46.0 87.6 %reduce-scatter.10.cloned.1.call-start = ((), (), s32[]{:S(2)}) async-start(), calls=%async_computation.12 | async-start | bytes 102400 | tf_op jit(solution)/shard_map/reduce_scatter | solution.py:99
  90.4 70.0 %all-to-all-start.1 = ((bf16[4,10,1792]{2,1,0:T(8,128)(2,1)}), bf16[4,10,1792]{2,1,0:T(8,128)(2,1)S(1)}, u32[]{:S(2)}, u32[]{:S(2)}) async-start(bf16[4,10,1792]{2,1,0:T(8,128)(2,1)} %all_to_all.43), calls=%async_computation.3 | async-start | bytes 458752 | tf_op jit(solution)/shard_map/all_to_all | solution.py:111
  133.7 25.3 %copy-start.1 = (bf16[1,1,1792,512]{3,2,1,0:T(8,128)(2,1)S(1)}, bf16[1,1,1792,512]{3,2,1,0:T(8,128)(2,1)}, u32[]{:S(2)}) copy-start(bf16[1,1,1792,512]{3,2,1,0:T(8,128)(2,1)} %param.18) | copy-start | bytes 5505028
  160.4 9.0 %all-to-all-start.4 = ((bf16[4,10,1792]{2,1,0:T(8,128)(2,1)}), bf16[4,10,1792]{2,1,0:T(8,128)(2,1)S(1)}, u32[]{:S(2)}, u32[]{:S(2)}) async-start(bf16[4,10,1792]{2,1,0:T(8,128)(2,1)} %all_to_all.52), calls=%async_computation.9 | async-start | bytes 458752 | tf_op jit(solution)/shard_map/all_to_all | solution.py:112
Sparse Core Ops, SparseCore 0:
  36.8 18.4 reduce-scatter.7
  57.7 17.3 reduce-scatter.5
  77.3 17.3 reduce-scatter.13
  96.9 17.3 reduce-scatter.11
  116.3 17.2 reduce-scatter.9
where the time goes:
time: 178 us; the launch traced here: 177 us
  waiting for transfers between devices  79.1 us (44%)
  blocking collectives  35.7 us (20%)
  starting transfers between devices  20.1 us (11%)
  matrix products  15.7 us (9%)
  between operations  14 us (8%)
  other arithmetic  8.03 us (5%)
  local copies, waits for them, and re-layouts  4.16 us (2%)
    reduce_scatter x1, waiting for transfers between devices, local(): lax.psum_scatter(part_gf, 'dp', scatter_dimension=1, tiled=True)  19.8 us
    reduce_scatter x1, waiting for transfers between devices, local(): lax.psum_scatter(part_ub, 'dp', scatter_dimension=1, tiled=True)  19.5 us
    reduce_scatter x1, waiting for transfers between devices, local(): lax.psum_scatter(part_dh, 'dp', scatter_dimension=1, tiled=True)  19.4 us
    all_gather x1, blocking collectives, local(): lax.all_gather(hidden, 'dp', axis=1, tiled=True)  11.9 us
    all_gather x1, blocking collectives, local(): lax.all_gather(dupper, 'dp', axis=1, tiled=True)  11.9 us
    all_gather x1, blocking collectives, local(): lax.all_gather(dgate, 'dp', axis=1, tiled=True)  11.9 us
    all_to_all x1, waiting for transfers between devices, local(): lax.all_to_all(half_grad, 'expert', split_axis=0, concat_axis=0, tiled=True)  5.44 us
    all_to_all x1, waiting for transfers between devices, local(): lax.all_to_all(send_f, 'expert', split_axis=0, concat_axis=0, tiled=True)  5.23 us
  transfers between devices with their start and end apart: 11, of which 9 were waited for; matrix products, arithmetic and copies ran while one was open for 12% of the time, Pallas kernels for 0%

commit v1 on v0

v1 whole, which is shorter than its diff:
```python
import functools

import jax
import jax.numpy as jnp
from jax import lax
from jax.experimental import pallas as pl
from jax.experimental.pallas import tpu as pltpu
from jax.sharding import PartitionSpec as P

BF16 = jnp.bfloat16
F32 = jnp.float32
LANES = 128
VMEM_LIMIT = 24 * 1024 * 1024


def in_vmem(x):
    return pltpu.with_memory_space_constraint(x, pltpu.VMEM)


def kernel_call(body, out_shape, flops, bytes_accessed):
    return pl.pallas_call(
        body,
        out_shape=out_shape,
        compiler_params=pltpu.CompilerParams(vmem_limit_bytes=VMEM_LIMIT),
        cost_estimate=pl.CostEstimate(flops=flops, bytes_accessed=bytes_accessed, transcendentals=0),
    )


def swap(x, axis, bit):
    peers = lax.axis_size(axis)
    return lax.ppermute(x, axis, [(i, i ^ bit) for i in range(peers)])


def onward(x, bit):
    sections = lax.axis_size("pipe")
    peers = lax.axis_size("expert")
    pairs = [
        (s * peers + i, (s + 1) % sections * peers + (i ^ bit))
        for s in range(sections)
        for i in range(peers)
    ]
    return lax.ppermute(x, ("pipe", "expert"), pairs)


def pack_kernel(topk, x_ref, c_ref, b_ref, rf_ref, gf_ref, rb_ref, gb_ref, moved_ref, saved_ref):
    rows, width = x_ref.shape
    moved_ref[:rows, :] = x_ref[...]
    moved_ref[rows:, :] = c_ref[...]
    saved_ref[:, :width] = b_ref[...]
    lane = lax.broadcasted_iota(jnp.int32, (rows, LANES), 1)
    notes = jnp.zeros((rows, LANES), F32)
    for group, ref in enumerate((rf_ref, gf_ref, rb_ref, gb_ref)):
        values = ref[...].astype(F32)
        for choice in range(topk):
            notes = jnp.where(lane == group * topk + choice, values[:, choice : choice + 1], notes)
    saved_ref[:, width:] = notes.astype(BF16)


def places(notes, first, topk, expert, rows):
    tokens = notes.shape[1]
    hit = (notes[first : first + topk] == expert).astype(F32)
    named = jnp.sum(hit, axis=0, keepdims=True)
    weight = jnp.sum(hit * notes[first + topk : first + 2 * topk], axis=0, keepdims=True)
    earlier = lax.broadcasted_iota(jnp.int32, (tokens, tokens), 0) < lax.broadcasted_iota(
        jnp.int32, (tokens, tokens), 1
    )
    rank = jnp.dot(
        jnp.broadcast_to(named, (8, tokens)).astype(BF16),
        earlier.astype(BF16),
        preferred_element_type=F32,
    )[:1]
    row = lax.broadcasted_iota(jnp.int32, (rows, tokens), 0).astype(F32)
    place = jnp.where((row == rank) & (named > 0.0), 1.0, 0.0)
    return place, place * weight


def up_kernel(groups, topk, rows, *refs):
    moved = refs[: 2 * groups]
    saved = refs[2 * groups : 4 * groups]
    w_g_ref, w_u_ref, w_d_ref, part_ref, place_f_ref, place_b_ref = refs[4 * groups :]
    held = moved[0].shape[0] // 2
    width = moved[0].shape[1]
    expert = (lax.axis_index("expert") // 2).astype(F32)
    notes = jnp.concatenate([r[:, width:] for r in saved], axis=0).astype(F32).T
    place_f, _ = places(notes, 0, topk, expert, rows)
    place_b, weigh_b = places(notes, 2 * topk, topk, expert, rows)
    place_f_ref[...] = place_f.astype(BF16)
    place_b_ref[...] = place_b.astype(BF16)
    x_f = jnp.concatenate([r[:held, :] for r in moved], axis=0)
    c_b = jnp.concatenate([r[held:, :] for r in moved], axis=0)
    x_b = jnp.concatenate([r[:, :width] for r in saved], axis=0)
    rows_f = jnp.dot(place_f.astype(BF16), x_f, preferred_element_type=F32)
    rows_b = jnp.dot(place_b.astype(BF16), x_b, preferred_element_type=F32)
    grads_b = jnp.dot(weigh_b.astype(BF16), c_b, preferred_element_type=F32).astype(BF16)
    both = jnp.concatenate([rows_f, rows_b], axis=0).astype(BF16)
    gate = jnp.dot(both, w_g_ref[...], preferred_element_type=F32)
    upper = jnp.dot(both, w_u_ref[...], preferred_element_type=F32)
    dhid = lax.dot_general(grads_b, w_d_ref[...], (((1,), (1,)), ((), ())), preferred_element_type=F32)
    part_ref[...] = jnp.concatenate([gate, upper, dhid], axis=0).astype(BF16)


def down_kernel(
    groups, rows, a_ref, b_ref, place_f_ref, place_b_ref, w_g_ref, w_u_ref, w_d_ref, own_ref, other_ref
):
    total = a_ref[...].astype(F32) + b_ref[...].astype(F32)
    gate_f, gate_b, upper_f, upper_b, dhid = [total[i * rows : (i + 1) * rows] for i in range(5)]
    hidden = (gate_f * jax.nn.sigmoid(gate_f) * upper_f).astype(BF16)
    sigma = jax.nn.sigmoid(gate_b)
    slope = sigma * (1.0 + gate_b * (1.0 - sigma))
    dgate = (dhid * upper_b * slope).astype(BF16)
    dupper = (dhid * (gate_b * sigma)).astype(BF16)
    turned = (((1,), (1,)), ((), ()))
    out_f = jnp.dot(hidden, w_d_ref[...], preferred_element_type=F32).astype(BF16)
    grad = lax.dot_general(dgate, w_g_ref[...], turned, preferred_element_type=F32)
    grad = grad + lax.dot_general(dupper, w_u_ref[...], turned, preferred_element_type=F32)
    grad = grad.astype(BF16)
    back = (((0,), (0,)), ((), ()))
    full_f = lax.dot_general(place_f_ref[...], out_f, back, preferred_element_type=F32).astype(BF16)
    full_b = lax.dot_general(place_b_ref[...], grad, back, preferred_element_type=F32).astype(BF16)
    held = own_ref.shape[1] // 2
    for d in range(groups):
        for ref, at in ((own_ref, d * held), (other_ref, (groups + d) * held)):
            ref[d, :held, :] = full_f[at : at + held]
            ref[d, held:, :] = full_b[at : at + held]


def final_kernel(groups, moved_ref, rf_ref, gf_ref, own_ref, other_ref, *refs):
    came = refs[: groups - 1]
    out_f_ref, out_b_ref = refs[groups - 1 :]
    held = out_f_ref.shape[0]
    mine = lax.axis_index("expert") // 2
    routes_f = rf_ref[...]
    gates_f = gf_ref[...].astype(F32)
    result_f = moved_ref[:held, :].astype(F32)
    result_b = moved_ref[held:, :].astype(F32)
    for d in range(groups):
        if d == 0:
            halves = own_ref[0].astype(F32) + other_ref[0].astype(F32)
        else:
            halves = came[d - 1][...].astype(F32)
        weight = jnp.sum(jnp.where(routes_f == (mine ^ d), gates_f, 0.0), axis=1, keepdims=True)
        result_f = result_f + weight * halves[:held]
        result_b = result_b + halves[held:]
    out_f_ref[...] = result_f.astype(BF16)
    out_b_ref[...] = result_b.astype(BF16)


def local(
    carry_forward,
    carry_cotangent,
    saved_input,
    routes_forward,
    gates_forward,
    routes_backward,
    gates_backward,
    w_gate,
    w_up,
    w_down,
):
    peers = lax.axis_size("expert")
    experts = peers // 2
    groups = peers // 2
    held, width = carry_forward.shape[1:]
    hidden = w_gate.shape[3]
    topk = routes_forward.shape[2]
    capacity = min(held, max(6, held * topk // experts + 2))
    rows = -(-peers * capacity // 8) * 8
    tokens = peers * held
    w_g = in_vmem(w_gate[0, 0])
    w_u = in_vmem(w_up[0, 0])
    w_d = in_vmem(w_down[0, 0])
    weight_bytes = 6 * width * hidden

    moved, saved = kernel_call(
        functools.partial(pack_kernel, topk),
        (
            jax.ShapeDtypeStruct((2 * held, width), BF16),
            jax.ShapeDtypeStruct((held, width + LANES), BF16),
        ),
        0,
        6 * held * width,
    )(
        carry_forward[0],
        carry_cotangent[0],
        saved_input[0],
        routes_forward[0],
        gates_forward[0],
        routes_backward[0],
        gates_backward[0],
    )
    saved_all = [saved] + [swap(saved, "expert", 2 * d) for d in range(1, groups)]
    moved_all = [onward(moved, 2 * d) for d in range(groups)]
    saved_all = saved_all + [swap(x, "expert", 1) for x in saved_all]
    moved_all = moved_all + [swap(x, "expert", 1) for x in moved_all]
    part, place_f, place_b = kernel_call(
        functools.partial(up_kernel, groups, topk, rows),
        (
            jax.ShapeDtypeStruct((5 * rows, hidden), BF16),
            jax.ShapeDtypeStruct((rows, tokens), BF16),
            jax.ShapeDtypeStruct((rows, tokens), BF16),
        ),
        10 * rows * width * hidden,
        weight_bytes,
    )(*moved_all, *saved_all, w_g, w_u, w_d)
    bit = lax.axis_size("dp") // 2
    while bit > 1:
        part = (part.astype(F32) + swap(part, "dp", bit).astype(F32)).astype(BF16)
        bit //= 2
    other_part = swap(part, "dp", 1)
    own, other = kernel_call(
        functools.partial(down_kernel, groups, rows),
        (
            jax.ShapeDtypeStruct((groups, 2 * held, width), BF16),
            jax.ShapeDtypeStruct((groups, 2 * held, width), BF16),
        ),
        6 * rows * width * hidden,
        weight_bytes,
    )(part, other_part, place_f, place_b, w_g, w_u, w_d)
    other = swap(other, "expert", 1)
    came = []
    for d in range(1, groups):
        halves = (own[d].astype(F32) + other[d].astype(F32)).astype(BF16)
        came.append(swap(halves, "expert", 2 * d))
    result_f, result_b = kernel_call(
        functools.partial(final_kernel, groups),
        (
            jax.ShapeDtypeStruct((held, width), BF16),
            jax.ShapeDtypeStruct((held, width), BF16),
        ),
        0,
        20 * held * width,
    )(moved_all[0], routes_forward[0], gates_forward[0], own, other, *came)
    return (result_f[None], result_b[None])


def solution(mesh):
    placed = (
        P("pipe", "expert", "dp"),
        P("pipe", "expert", "dp"),
        P("pipe", "expert", "dp"),
        P("pipe", "expert", None),
        P("pipe", "expert", None),
        P("pipe", "expert", None),
        P("pipe", "expert", None),
        P("pipe", "expert", "dp", None),
        P("pipe", "expert", "dp", None),
        P("pipe", "expert", None, "dp"),
    )
    return jax.shard_map(
        local,
        mesh=mesh,
        in_specs=placed,
        out_specs=(P("pipe", "expert", "dp"), P("pipe", "expert", "dp")),
        check_vma=False,
    )
```

time: 178 us -> 52.3 us (0.29)
  waiting for transfers between devices: 79.1 us -> 27.9 us
  blocking collectives: 35.7 us -> 0 us
  matrix products: 15.7 us -> 0 us
  between operations: 14 us -> 0.69 us
  starting transfers between devices: 20.1 us -> 9.3 us
  other arithmetic: 8.03 us -> 0.08 us
  local copies, waits for them, and re-layouts: 4.16 us -> 9.92 us
  Pallas kernels: 0 us -> 3.97 us
    reduce_scatter x5 -> x0, waiting for transfers between devices: 63 us -> none  [the longest x1 19.8 us: local(): lax.psum_scatter(part_gf, 'dp', scatter_dimension=1, tiled=True)]
    all_gather x3 -> x0, blocking collectives: 35.7 us -> none  [the longest x1 11.9 us: local(): lax.all_gather(hidden, 'dp', axis=1, tiled=True)]
    ppermute x1 -> x11, waiting for transfers between devices: 0.01 us -> 27.9 us  [the longest x9 22.7 us: swap(): return lax.ppermute(x, axis, [(i, i ^ bit) for i in range(peers)])]
    all_to_all x5 -> x0, starting transfers between devices: 16.9 us -> none  [the longest x1 3.39 us: local(): lax.all_to_all(half_grad, 'expert', split_axis=0, concat_axis=0, tiled=True)]
    all_to_all x5 -> x0, waiting for transfers between devices: 15.9 us -> none  [the longest x1 5.44 us: local(): lax.all_to_all(half_grad, 'expert', split_axis=0, concat_axis=0, tiled=True)]
    dot_general x13 -> x0, matrix products: 15.7 us -> none  [the longest x1 2.78 us: local(): jnp.einsum('rd,hd->rh', grads_b, w_d, preferred_element_type=jnp.float32)]
    unnamed x6 -> x18, local copies, waits for them, and re-layouts: 0.02 us -> 6.96 us
    ppermute x1 -> x11, starting transfers between devices: 3 us -> 9.3 us  [the longest x9 4.87 us: swap(): return lax.ppermute(x, axis, [(i, i ^ bit) for i in range(peers)])]
  transfers between devices with their start and end apart: 11 -> 11, of which waited for: 9 -> 8; matrix products, arithmetic and copies ran while one was open for 12% -> 0% of each run, Pallas kernels for 0% -> 0%
where the time goes in v1:
time: 52.3 us; the launch traced here: 51.9 us
  waiting for transfers between devices  27.9 us (53%)
  local copies, waits for them, and re-layouts  9.92 us (19%)
  starting transfers between devices  9.3 us (18%)
  Pallas kernels  3.97 us (8%)
  between operations  0.69 us (1%)
    ppermute x9, waiting for transfers between devices, swap(): return lax.ppermute(x, axis, [(i, i ^ bit) for i in range(peers)])  22.7 us
    unnamed x18, local copies, waits for them, and re-layouts  6.96 us
    ppermute x2, waiting for transfers between devices, onward(): return lax.ppermute(x, ('pipe', 'expert'), pairs)  5.21 us
    ppermute x9, starting transfers between devices, swap(): return lax.ppermute(x, axis, [(i, i ^ bit) for i in range(peers)])  4.87 us
    ppermute x2, starting transfers between devices, onward(): return lax.ppermute(x, ('pipe', 'expert'), pairs)  4.44 us
    pallas_call x1, Pallas kernels, local(): kernel_call(functools.partial(down_kernel, groups, rows), (jax.ShapeDtype...  1.72 us
    pallas_call x1, Pallas kernels, local(): kernel_call(functools.partial(up_kernel, groups, topk, rows), (jax.ShapeD...  1.43 us
  transfers between devices with their start and end apart: 11, of which 8 were waited for; matrix products, arithmetic and copies ran while one was open for 0% of the time, Pallas kernels for 0%

profile of v1, /device:TPU:0, one launch (start us, length us, event | category | flops | bytes accessed | tf_op | source)
XLA Modules:
  0.0 51.9 jit_solution(11041314754165393691)
XLA Ops:
  0.6 0.7 %copy.13.gf_ref = bf16[16,1]{1,0:T(8,128)(2,1)S(1)} copy(bf16[16,1]{0,1:T(2,128)(2,1)} %bitcast.23) | data formatting | bytes 64 | tf_op jit(solution)/shard_map/squeeze | solution.py:187
  1.4 0.7 %copy.15.gb_ref = bf16[16,1]{1,0:T(8,128)(2,1)S(1)} copy(bf16[16,1]{0,1:T(2,128)(2,1)} %bitcast.24) | data formatting | bytes 64 | tf_op jit(solution)/shard_map/squeeze | solution.py:189
  2.1 0.7 %copy.12.rf_ref = s32[16,1]{1,0:T(8,128)S(1)} copy(s32[16,1]{0,1:T(1,128)} %bitcast.25) | data formatting | bytes 128 | tf_op jit(solution)/shard_map/squeeze | solution.py:186
  2.9 0.7 %copy.14.rb_ref = s32[16,1]{1,0:T(8,128)S(1)} copy(s32[16,1]{0,1:T(1,128)} %bitcast.26) | data formatting | bytes 128 | tf_op jit(solution)/shard_map/squeeze | solution.py:188
  3.6 0.8 %copy-done.6 = bf16[1,16,1792]{2,1,0:T(8,128)(2,1)S(1)} copy-done((bf16[1,16,1792]{2,1,0:T(8,128)(2,1)S(1)}, bf16[1,16,1792]{2,1,0:T(8,128)(2,1)}, u32[]{:S(2)}) %copy-start.6) | copy-done | bytes 57368
  4.4 0.8 %copy-done.7 = bf16[1,16,1792]{2,1,0:T(8,128)(2,1)S(1)} copy-done((bf16[1,16,1792]{2,1,0:T(8,128)(2,1)S(1)}, bf16[1,16,1792]{2,1,0:T(8,128)(2,1)}, u32[]{:S(2)}) %copy-start.7) | copy-done | bytes 57368
  5.2 0.8 %copy-done.8 = bf16[1,16,1792]{2,1,0:T(8,128)(2,1)S(1)} copy-done((bf16[1,16,1792]{2,1,0:T(8,128)(2,1)S(1)}, bf16[1,16,1792]{2,1,0:T(8,128)(2,1)}, u32[]{:S(2)}) %copy-start.8) | copy-done | bytes 57368
  6.0 0.1 shard_map.113
  6.1 3.9 %collective-permute-start.1 = (bf16[32,1792]{1,0:T(8,128)(2,1)S(1)}, bf16[32,1792]{1,0:T(8,128)(2,1)S(1)}, u32[]{:S(2)}, u32[]{:S(2)}) collective-permute-start(bf16[32,1792]{1,0:T(8,128)(2,1)S(1)} %get-tuple-element.11), channel_id=1, source_target_pairs={{0,24},{4,28},{8,16},{12,20},{16,8},{20,12},{24,0},{28,4},{1,25},{... | collective-permute-start | bytes 344072 | tf_op jit(solution)/shard_map/ppermute | solution.py:42
  10.0 0.5 %collective-permute-start = (bf16[32,1792]{1,0:T(8,128)(2,1)S(1)}, bf16[32,1792]{1,0:T(8,128)(2,1)S(1)}, u32[]{:S(2)}, u32[]{:S(2)}) collective-permute-start(bf16[32,1792]{1,0:T(8,128)(2,1)S(1)} %get-tuple-element.11), channel_id=1, source_target_pairs={{0,16},{4,20},{8,24},{12,28},{16,0},{20,4},{24,8},{28,12},{1,17},{... | collective-permute-start | bytes 344072 | tf_op jit(solution)/shard_map/ppermute | solution.py:42
  10.6 0.1 collective-permute-start.4
  10.7 3.3 %collective-permute-done.1.refs_1_ = bf16[32,1792]{1,0:T(8,128)(2,1)S(1)} collective-permute-done((bf16[32,1792]{1,0:T(8,128)(2,1)S(1)}, bf16[32,1792]{1,0:T(8,128)(2,1)S(1)}, u32[]{:S(2)}, u32[]{:S(2)}) %collective-permute-start.1) | collective-permute-done | bytes 114720 | tf_op jit(solution)/shard_map/ppermute | solution.py:42
  14.0 1.9 %collective-permute-done.refs_0_.moved_ref = bf16[32,1792]{1,0:T(8,128)(2,1)S(1)} collective-permute-done((bf16[32,1792]{1,0:T(8,128)(2,1)S(1)}, bf16[32,1792]{1,0:T(8,128)(2,1)S(1)}, u32[]{:S(2)}, u32[]{:S(2)}) %collective-permute-start) | collective-permute-done | bytes 114720 | tf_op jit(solution)/shard_map/ppermute | solution.py:42
  15.9 0.5 collective-permute-start.5
  16.4 0.0 collective-permute-start.6
  16.4 0.9 %collective-permute-done.5.refs_6_ = bf16[16,1920]{1,0:T(8,128)(2,1)S(1)} collective-permute-done((bf16[16,1920]{1,0:T(8,128)(2,1)S(1)}, bf16[16,1920]{1,0:T(8,128)(2,1)S(1)}, u32[]{:S(2)}, u32[]{:S(2)}) %collective-permute-start.5) | collective-permute-done | bytes 61472 | tf_op jit(solution)/shard_map/ppermute | solution.py:31
  17.3 0.3 collective-permute-done.6.refs_7_
  17.7 1.5 %copy-done = bf16[1,1,1792,512]{3,2,1,0:T(8,128)(2,1)S(1)} copy-done((bf16[1,1,1792,512]{3,2,1,0:T(8,128)(2,1)S(1)}, bf16[1,1,1792,512]{3,2,1,0:T(8,128)(2,1)}, u32[]{:S(2)}) %copy-start) | copy-done | bytes 1835032
  19.2 1.5 %copy-done.2 = bf16[1,1,1792,512]{3,2,1,0:T(8,128)(2,1)S(1)} copy-done((bf16[1,1,1792,512]{3,2,1,0:T(8,128)(2,1)S(1)}, bf16[1,1,1792,512]{3,2,1,0:T(8,128)(2,1)}, u32[]{:S(2)}) %copy-start.2) | copy-done | bytes 1835032
  20.7 1.5 %copy-done.4 = bf16[1,1,512,1792]{3,2,1,0:T(8,128)(2,1)S(1)} copy-done((bf16[1,1,512,1792]{3,2,1,0:T(8,128)(2,1)S(1)}, bf16[1,1,512,1792]{3,2,1,0:T(8,128)(2,1)}, u32[]{:S(2)}) %copy-start.4) | copy-done | bytes 1835032
  22.2 1.4 %shard_map.114 = (bf16[200,512]{1,0:T(8,128)(2,1)S(1)}, bf16[40,64]{1,0:T(8,128)(2,1)S(1)}, bf16[40,64]{1,0:T(8,128)(2,1)S(1)}) custom-call(bf16[32,1792]{1,0:T(8,128)(2,1)S(1)} %collective-permute-done.refs_0_.moved_ref, bf16[32,1792]{1,0:T(8,128)(2,1)S(1)} %collective-permute-done.1.refs_1_, bf16[32,1792]{1,0:T(8,128)(2,1)S(1)} %collective-permute-done.2.refs_2_, ...), custom_call_target="tpu_custom_call" | custom-call | flops 367001600 | bytes 5505024 | tf_op jit(solution)/shard_map/pallas_call | solution.py:195
  23.6 2.7 %collective-permute-start.7 = (bf16[200,512]{1,0:T(8,128)(2,1)S(1)}, bf16[200,512]{1,0:T(8,128)(2,1)S(1)}, u32[]{:S(2)}, u32[]{:S(2)}) collective-permute-start(bf16[200,512]{1,0:T(8,128)(2,1)S(1)} %get-tuple-element.13), channel_id=1, source_target_pairs={{0,2},{1,3},{2,0},{3,1},{4,6},{5,7},{6,4},{7,5},{8,10},{9,11},{10,... | collective-permute-start | bytes 614408 | tf_op jit(solution)/shard_map/ppermute | solution.py:31
  26.3 9.8 %collective-permute-done.7 = bf16[200,512]{1,0:T(8,128)(2,1)S(1)} collective-permute-done((bf16[200,512]{1,0:T(8,128)(2,1)S(1)}, bf16[200,512]{1,0:T(8,128)(2,1)S(1)}, u32[]{:S(2)}, u32[]{:S(2)}) %collective-permute-start.7) | collective-permute-done | bytes 204832 | tf_op jit(solution)/shard_map/ppermute | solution.py:31
  36.1 0.1 add_convert_fusion.a_ref
  36.2 0.7 %collective-permute-start.8 = (bf16[200,512]{1,0:T(8,128)(2,1)S(1)}, bf16[200,512]{1,0:T(8,128)(2,1)S(1)}, u32[]{:S(2)}, u32[]{:S(2)}) collective-permute-start(bf16[200,512]{1,0:T(8,128)(2,1)S(1)} %add_convert_fusion.a_ref), channel_id=1, source_target_pairs={{0,1},{1,0},{2,3},{3,2},{4,5},{5,4},{6,7},{7,6},{8,9},{9,8},{10,11... | collective-permute-start | bytes 614408 | tf_op jit(solution)/shard_map/ppermute | solution.py:31
  36.9 5.6 %collective-permute-done.8.b_ref = bf16[200,512]{1,0:T(8,128)(2,1)S(1)} collective-permute-done((bf16[200,512]{1,0:T(8,128)(2,1)S(1)}, bf16[200,512]{1,0:T(8,128)(2,1)S(1)}, u32[]{:S(2)}, u32[]{:S(2)}) %collective-permute-start.8) | collective-permute-done | bytes 204832 | tf_op jit(solution)/shard_map/ppermute | solution.py:31
  42.6 1.7 %shard_map.115 = (bf16[2,32,1792]{2,1,0:T(8,128)(2,1)S(1)}, bf16[2,32,1792]{2,1,0:T(8,128)(2,1)S(1)}) custom-call(bf16[200,512]{1,0:T(8,128)(2,1)S(1)} %add_convert_fusion.a_ref, bf16[200,512]{1,0:T(8,128)(2,1)S(1)} %collective-permute-done.8.b_ref, bf16[40,64]{1,0:T(8,128)(2,1)S(1)} %get-tuple-element.14.place_f_ref, ...), custom_call_target="tpu_custom_call" | custom-call | flops 220200960 | bytes 5505024 | tf_op jit(solution)/shard_map/pallas_call | solution.py:210
  44.3 0.1 collective-permute-start.9
  44.4 1.5 %collective-permute-done.9.other_ref = bf16[2,32,1792]{2,1,0:T(8,128)(2,1)S(1)} collective-permute-done((bf16[2,32,1792]{2,1,0:T(8,128)(2,1)S(1)}, bf16[2,32,1792]{2,1,0:T(8,128)(2,1)S(1)}, u32[]{:S(2)}, u32[]{:S(2)}) %collective-permute-start.9) | collective-permute-done | bytes 229408 | tf_op jit(solution)/shard_map/ppermute | solution.py:31
  45.9 0.8 %collective-permute-start.10 = (bf16[32,1792]{1,0:T(8,128)(2,1)S(1)}, bf16[32,1792]{1,0:T(8,128)(2,1)S(1)}, u32[]{:S(2)}, u32[]{:S(2)}) collective-permute-start(bf16[32,1792]{1,0:T(8,128)(2,1)S(1)} %fusion), channel_id=1, source_target_pairs={{0,8},{4,12},{8,0},{12,4},{1,9},{5,13},{9,1},{13,5},{2,10},{6,14},... | collective-permute-start | bytes 344072 | tf_op jit(solution)/shard_map/ppermute | solution.py:31
  46.6 4.5 %collective-permute-done.10.refs_0_ = bf16[32,1792]{1,0:T(8,128)(2,1)S(1)} collective-permute-done((bf16[32,1792]{1,0:T(8,128)(2,1)S(1)}, bf16[32,1792]{1,0:T(8,128)(2,1)S(1)}, u32[]{:S(2)}, u32[]{:S(2)}) %collective-permute-start.10) | collective-permute-done | bytes 114720 | tf_op jit(solution)/shard_map/ppermute | solution.py:31
  51.1 0.7 %shard_map.116 = (bf16[16,1792]{1,0:T(8,128)(2,1)}, bf16[16,1792]{1,0:T(8,128)(2,1)}) custom-call(bf16[32,1792]{1,0:T(8,128)(2,1)S(1)} %collective-permute-done.refs_0_.moved_ref, s32[16,1]{1,0:T(8,128)S(1)} %copy.12.rf_ref, bf16[16,1]{1,0:T(8,128)(2,1)S(1)} %copy.13.gf_ref, bf16[2,32,1792]{2,1,0:T(8,128)(2,1)S(1)} %get-tuple-element.16.own_ref, ...), custom_call_target="tpu_custom_call" | custom-call | bytes 573440 | tf_op jit(solution)/shard_map/pallas_call | solution.py:224
  (18 shorter events, 0.1 us)
Async XLA Ops:
  3.6 0.8 %copy-start.6 = (bf16[1,16,1792]{2,1,0:T(8,128)(2,1)S(1)}, bf16[1,16,1792]{2,1,0:T(8,128)(2,1)}, u32[]{:S(2)}) copy-start(bf16[1,16,1792]{2,1,0:T(8,128)(2,1)} %param.10) | copy-start | bytes 172036
  4.4 0.8 %copy-start.7 = (bf16[1,16,1792]{2,1,0:T(8,128)(2,1)S(1)}, bf16[1,16,1792]{2,1,0:T(8,128)(2,1)}, u32[]{:S(2)}) copy-start(bf16[1,16,1792]{2,1,0:T(8,128)(2,1)} %param.11) | copy-start | bytes 172036
  5.2 0.8 %copy-start.8 = (bf16[1,16,1792]{2,1,0:T(8,128)(2,1)S(1)}, bf16[1,16,1792]{2,1,0:T(8,128)(2,1)}, u32[]{:S(2)}) copy-start(bf16[1,16,1792]{2,1,0:T(8,128)(2,1)} %param.12) | copy-start | bytes 172036
  6.1 7.9 %collective-permute-start.1 = (bf16[32,1792]{1,0:T(8,128)(2,1)S(1)}, bf16[32,1792]{1,0:T(8,128)(2,1)S(1)}, u32[]{:S(2)}, u32[]{:S(2)}) collective-permute-start(bf16[32,1792]{1,0:T(8,128)(2,1)S(1)} %get-tuple-element.11), channel_id=1, source_target_pairs={{0,24},{4,28},{8,16},{12,20},{16,8},{20,12},{24,0},{28,4},{1,25},{... | collective-permute-start | bytes 344072 | tf_op jit(solution)/shard_map/ppermute | solution.py:42
  10.0 5.9 %collective-permute-start = (bf16[32,1792]{1,0:T(8,128)(2,1)S(1)}, bf16[32,1792]{1,0:T(8,128)(2,1)S(1)}, u32[]{:S(2)}, u32[]{:S(2)}) collective-permute-start(bf16[32,1792]{1,0:T(8,128)(2,1)S(1)} %get-tuple-element.11), channel_id=1, source_target_pairs={{0,16},{4,20},{8,24},{12,28},{16,0},{20,4},{24,8},{28,12},{1,17},{... | collective-permute-start | bytes 344072 | tf_op jit(solution)/shard_map/ppermute | solution.py:42
  10.6 5.8 %collective-permute-start.4 = (bf16[16,1920]{1,0:T(8,128)(2,1)S(1)}, bf16[16,1920]{1,0:T(8,128)(2,1)S(1)}, u32[]{:S(2)}, u32[]{:S(2)}) collective-permute-start(bf16[16,1920]{1,0:T(8,128)(2,1)S(1)} %get-tuple-element.12.refs_4_), channel_id=1, source_target_pairs={{0,8},{4,12},{8,0},{12,4},{1,9},{5,13},{9,1},{13,5},{2,10},{6,14},... | collective-permute-start | bytes 184328 | tf_op jit(solution)/shard_map/ppermute | solution.py:31
  14.0 3.6 %collective-permute-start.3 = (bf16[32,1792]{1,0:T(8,128)(2,1)S(1)}, bf16[32,1792]{1,0:T(8,128)(2,1)S(1)}, u32[]{:S(2)}, u32[]{:S(2)}) collective-permute-start(bf16[32,1792]{1,0:T(8,128)(2,1)S(1)} %collective-permute-done.1.refs_1_), channel_id=1, source_target_pairs={{0,4},{4,0},{8,12},{12,8},{1,5},{5,1},{9,13},{13,9},{2,6},{6,2},{1... | collective-permute-start | bytes 344072 | tf_op jit(solution)/shard_map/ppermute | solution.py:31
  15.9 1.8 %collective-permute-start.2 = (bf16[32,1792]{1,0:T(8,128)(2,1)S(1)}, bf16[32,1792]{1,0:T(8,128)(2,1)S(1)}, u32[]{:S(2)}, u32[]{:S(2)}) collective-permute-start(bf16[32,1792]{1,0:T(8,128)(2,1)S(1)} %collective-permute-done.refs_0_.moved_ref), channel_id=1, source_target_pairs={{0,4},{4,0},{8,12},{12,8},{1,5},{5,1},{9,13},{13,9},{2,6},{6,2},{1... | collective-permute-start | bytes 344072 | tf_op jit(solution)/shard_map/ppermute | solution.py:31
  15.9 1.4 %collective-permute-start.5 = (bf16[16,1920]{1,0:T(8,128)(2,1)S(1)}, bf16[16,1920]{1,0:T(8,128)(2,1)S(1)}, u32[]{:S(2)}, u32[]{:S(2)}) collective-permute-start(bf16[16,1920]{1,0:T(8,128)(2,1)S(1)} %get-tuple-element.12.refs_4_), channel_id=1, source_target_pairs={{0,4},{4,0},{8,12},{12,8},{1,5},{5,1},{9,13},{13,9},{2,6},{6,2},{1... | collective-permute-start | bytes 184328 | tf_op jit(solution)/shard_map/ppermute | solution.py:31
  16.4 1.2 %collective-permute-start.6 = (bf16[16,1920]{1,0:T(8,128)(2,1)S(1)}, bf16[16,1920]{1,0:T(8,128)(2,1)S(1)}, u32[]{:S(2)}, u32[]{:S(2)}) collective-permute-start(bf16[16,1920]{1,0:T(8,128)(2,1)S(1)} %collective-permute-done.4.refs_5_), channel_id=1, source_target_pairs={{0,4},{4,0},{8,12},{12,8},{1,5},{5,1},{9,13},{13,9},{2,6},{6,2},{1... | collective-permute-start | bytes 184328 | tf_op jit(solution)/shard_map/ppermute | solution.py:31
  17.6 1.5 %copy-start = (bf16[1,1,1792,512]{3,2,1,0:T(8,128)(2,1)S(1)}, bf16[1,1,1792,512]{3,2,1,0:T(8,128)(2,1)}, u32[]{:S(2)}) copy-start(bf16[1,1,1792,512]{3,2,1,0:T(8,128)(2,1)} %param.17) | copy-start | bytes 5505028
  19.2 1.5 %copy-start.2 = (bf16[1,1,1792,512]{3,2,1,0:T(8,128)(2,1)S(1)}, bf16[1,1,1792,512]{3,2,1,0:T(8,128)(2,1)}, u32[]{:S(2)}) copy-start(bf16[1,1,1792,512]{3,2,1,0:T(8,128)(2,1)} %param.18) | copy-start | bytes 5505028
  20.7 1.5 %copy-start.4 = (bf16[1,1,512,1792]{3,2,1,0:T(8,128)(2,1)S(1)}, bf16[1,1,512,1792]{3,2,1,0:T(8,128)(2,1)}, u32[]{:S(2)}) copy-start(bf16[1,1,512,1792]{3,2,1,0:T(8,128)(2,1)} %param.19) | copy-start | bytes 5505028
  22.2 20.4 %copy-start.1 = (bf16[1,1,1792,512]{3,2,1,0:T(8,128)(2,1)S(1)}, bf16[1,1,1792,512]{3,2,1,0:T(8,128)(2,1)}, u32[]{:S(2)}) copy-start(bf16[1,1,1792,512]{3,2,1,0:T(8,128)(2,1)} %param.17) | copy-start | bytes 5505028
  22.2 20.4 %copy-start.3 = (bf16[1,1,1792,512]{3,2,1,0:T(8,128)(2,1)S(1)}, bf16[1,1,1792,512]{3,2,1,0:T(8,128)(2,1)}, u32[]{:S(2)}) copy-start(bf16[1,1,1792,512]{3,2,1,0:T(8,128)(2,1)} %param.18) | copy-start | bytes 5505028
  22.2 20.4 %copy-start.5 = (bf16[1,1,512,1792]{3,2,1,0:T(8,128)(2,1)S(1)}, bf16[1,1,512,1792]{3,2,1,0:T(8,128)(2,1)}, u32[]{:S(2)}) copy-start(bf16[1,1,512,1792]{3,2,1,0:T(8,128)(2,1)} %param.19) | copy-start | bytes 5505028
  23.6 12.5 %collective-permute-start.7 = (bf16[200,512]{1,0:T(8,128)(2,1)S(1)}, bf16[200,512]{1,0:T(8,128)(2,1)S(1)}, u32[]{:S(2)}, u32[]{:S(2)}) collective-permute-start(bf16[200,512]{1,0:T(8,128)(2,1)S(1)} %get-tuple-element.13), channel_id=1, source_target_pairs={{0,2},{1,3},{2,0},{3,1},{4,6},{5,7},{6,4},{7,5},{8,10},{9,11},{10,... | collective-permute-start | bytes 614408 | tf_op jit(solution)/shard_map/ppermute | solution.py:31
  36.2 6.4 %collective-permute-start.8 = (bf16[200,512]{1,0:T(8,128)(2,1)S(1)}, bf16[200,512]{1,0:T(8,128)(2,1)S(1)}, u32[]{:S(2)}, u32[]{:S(2)}) collective-permute-start(bf16[200,512]{1,0:T(8,128)(2,1)S(1)} %add_convert_fusion.a_ref), channel_id=1, source_target_pairs={{0,1},{1,0},{2,3},{3,2},{4,5},{5,4},{6,7},{7,6},{8,9},{9,8},{10,11... | collective-permute-start | bytes 614408 | tf_op jit(solution)/shard_map/ppermute | solution.py:31
  44.3 1.6 %collective-permute-start.9 = (bf16[2,32,1792]{2,1,0:T(8,128)(2,1)S(1)}, bf16[2,32,1792]{2,1,0:T(8,128)(2,1)S(1)}, u32[]{:S(2)}, u32[]{:S(2)}) collective-permute-start(bf16[2,32,1792]{2,1,0:T(8,128)(2,1)S(1)} %get-tuple-element.17), channel_id=1, source_target_pairs={{0,4},{4,0},{8,12},{12,8},{1,5},{5,1},{9,13},{13,9},{2,6},{6,2},{1... | collective-permute-start | bytes 688136 | tf_op jit(solution)/shard_map/ppermute | solution.py:31
  45.9 5.3 %collective-permute-start.10 = (bf16[32,1792]{1,0:T(8,128)(2,1)S(1)}, bf16[32,1792]{1,0:T(8,128)(2,1)S(1)}, u32[]{:S(2)}, u32[]{:S(2)}) collective-permute-start(bf16[32,1792]{1,0:T(8,128)(2,1)S(1)} %fusion), channel_id=1, source_target_pairs={{0,8},{4,12},{8,0},{12,4},{1,9},{5,13},{9,1},{13,5},{2,10},{6,14},... | collective-permute-start | bytes 344072 | tf_op jit(solution)/shard_map/ppermute | solution.py:31

commit v2 on v1

v2 whole, which is shorter than its diff:
```python
import functools

import jax
import jax.numpy as jnp
from jax import lax
from jax.experimental import pallas as pl
from jax.experimental.pallas import tpu as pltpu
from jax.sharding import PartitionSpec as P

BF16 = jnp.bfloat16
F32 = jnp.float32
LANES = 128
VMEM_LIMIT = 24 * 1024 * 1024


def in_vmem(x):
    return pltpu.with_memory_space_constraint(x, pltpu.VMEM)


def in_hbm(x):
    return pltpu.with_memory_space_constraint(x, pltpu.HBM)


def kernel_call(body, out_shape, flops, bytes_accessed):
    return pl.pallas_call(
        body,
        out_shape=out_shape,
        compiler_params=pltpu.CompilerParams(vmem_limit_bytes=VMEM_LIMIT),
        cost_estimate=pl.CostEstimate(flops=flops, bytes_accessed=bytes_accessed, transcendentals=0),
    )


def swap(x, axis, bit):
    peers = lax.axis_size(axis)
    return lax.ppermute(x, axis, [(i, i ^ bit) for i in range(peers)])


def onward(x, bit):
    sections = lax.axis_size("pipe")
    peers = lax.axis_size("expert")
    pairs = [
        (s * peers + i, (s + 1) % sections * peers + (i ^ bit))
        for s in range(sections)
        for i in range(peers)
    ]
    return lax.ppermute(x, ("pipe", "expert"), pairs)


def pack_kernel(topk, b_hbm, *refs):
    rows, width = b_hbm.shape
    noted, (saved_ref, *held, sem, sems) = refs[:4], refs[4:]
    copies = [pltpu.make_async_copy(b_hbm, saved_ref.at[:, pl.ds(0, width)], sem)]
    for i, (source, target) in enumerate(zip(noted, held)):
        copies.append(pltpu.make_async_copy(source, target, sems.at[i]))
    for copy in copies:
        copy.start()
    for copy in copies[1:]:
        copy.wait()
    notes = jnp.concatenate([r[...].astype(F32) for r in held], axis=0)
    for first in range(0, saved_ref.shape[1] - width, LANES):
        block = first // LANES * rows
        part = notes[block : block + rows]
        part = jnp.pad(part, ((0, rows - part.shape[0]), (0, LANES - part.shape[1])))
        saved_ref[:, width + first : width + first + LANES] = part.astype(BF16)
    copies[0].wait()


def fetch_kernel(*refs):
    count = len(refs) // 2
    sems = refs[-1]
    copies = [
        pltpu.make_async_copy(refs[i], refs[count + i], sems.at[i]) for i in range(count)
    ]
    for copy in copies:
        copy.start()
    for copy in copies:
        copy.wait()


def unpack(saved, width, held, topk):
    per_tile = LANES // held
    tiles = []
    for first in range(0, len(saved), per_tile):
        tile = None
        for place, ref in enumerate(saved[first : first + per_tile]):
            spare = ref.shape[1] - width
            part = jnp.concatenate(
                [
                    ref[:, width + j * LANES : width + (j + 1) * LANES].astype(F32)
                    for j in range(spare // LANES)
                ],
                axis=0,
            )
            if place:
                part = pltpu.roll(part, place * held, 1)
            tile = part if tile is None else tile + part
        tiles.append(tile)
    notes = jnp.concatenate(tiles, axis=1) if len(tiles) > 1 else tiles[0]
    return notes[:, : len(saved) * held]


def places(notes, first, topk, expert, rows):
    tokens = notes.shape[1]
    hit = (notes[first : first + topk] == expert).astype(F32)
    named = jnp.sum(hit, axis=0, keepdims=True)
    weight = jnp.sum(hit * notes[first + topk : first + 2 * topk], axis=0, keepdims=True)
    earlier = lax.broadcasted_iota(jnp.int32, (tokens, tokens), 0) < lax.broadcasted_iota(
        jnp.int32, (tokens, tokens), 1
    )
    rank = jnp.dot(
        jnp.broadcast_to(named, (8, tokens)).astype(BF16),
        earlier.astype(BF16),
        preferred_element_type=F32,
    )[:1]
    row = lax.broadcasted_iota(jnp.int32, (rows, tokens), 0).astype(F32)
    place = jnp.where((row == rank) & (named > 0.0), 1.0, 0.0)
    return place, place * weight


def up_kernel(groups, topk, rows, *refs):
    moved = refs[: 2 * groups]
    saved = refs[2 * groups : 4 * groups]
    (
        w_g_ref,
        w_u_ref,
        w_d_ref,
        part_f_ref,
        part_b_ref,
        place_f_ref,
        place_b_ref,
    ) = refs[4 * groups :]
    held = moved[0].shape[0] // 2
    width = moved[0].shape[1]
    expert = (lax.axis_index("expert") // 2).astype(F32)
    notes = unpack(saved, width, held, topk)
    place_f, _ = places(notes, 0, topk, expert, rows)
    place_b, weigh_b = places(notes, 2 * topk, topk, expert, rows)
    place_f_ref[...] = place_f.astype(BF16)
    place_b_ref[...] = place_b.astype(BF16)
    x_f = jnp.concatenate([r[:held, :] for r in moved], axis=0)
    c_b = jnp.concatenate([r[held:, :] for r in moved], axis=0)
    x_b = jnp.concatenate([r[:, :width] for r in saved], axis=0)
    rows_f = jnp.dot(place_f.astype(BF16), x_f, preferred_element_type=F32)
    rows_b = jnp.dot(place_b.astype(BF16), x_b, preferred_element_type=F32)
    grads_b = jnp.dot(weigh_b.astype(BF16), c_b, preferred_element_type=F32).astype(BF16)
    both = jnp.concatenate([rows_f, rows_b], axis=0).astype(BF16)
    gate = jnp.dot(both, w_g_ref[...], preferred_element_type=F32)
    upper = jnp.dot(both, w_u_ref[...], preferred_element_type=F32)
    dhid = lax.dot_general(grads_b, w_d_ref[...], (((1,), (1,)), ((), ())), preferred_element_type=F32)
    part_f_ref[...] = jnp.concatenate([gate[:rows], upper[:rows]], axis=0).astype(BF16)
    part_b_ref[...] = jnp.concatenate([gate[rows:], upper[rows:], dhid], axis=0).astype(BF16)


def return_rows(groups, place_ref, out, own_ref, other_ref):
    back = (((0,), (0,)), ((), ()))
    full = lax.dot_general(place_ref[...], out, back, preferred_element_type=F32).astype(BF16)
    held = own_ref.shape[1]
    for d in range(groups):
        own_ref[d] = full[d * held : (d + 1) * held]
        other_ref[d] = full[(groups + d) * held : (groups + d + 1) * held]


def down_kernel(groups, rows, a_ref, b_ref, place_ref, w_d_ref, own_ref, other_ref):
    total = a_ref[...].astype(F32) + b_ref[...].astype(F32)
    gate, upper = total[:rows], total[rows:]
    hidden = (gate * jax.nn.sigmoid(gate) * upper).astype(BF16)
    out = jnp.dot(hidden, w_d_ref[...], preferred_element_type=F32).astype(BF16)
    return_rows(groups, place_ref, out, own_ref, other_ref)


def grad_kernel(groups, rows, a_ref, b_ref, place_ref, w_g_ref, w_u_ref, own_ref, other_ref):
    total = a_ref[...].astype(F32) + b_ref[...].astype(F32)
    gate, upper, dhid = total[:rows], total[rows : 2 * rows], total[2 * rows :]
    sigma = jax.nn.sigmoid(gate)
    slope = sigma * (1.0 + gate * (1.0 - sigma))
    dgate = (dhid * upper * slope).astype(BF16)
    dupper = (dhid * (gate * sigma)).astype(BF16)
    turned = (((1,), (1,)), ((), ()))
    grad = lax.dot_general(dgate, w_g_ref[...], turned, preferred_element_type=F32)
    grad = grad + lax.dot_general(dupper, w_u_ref[...], turned, preferred_element_type=F32)
    return_rows(groups, place_ref, grad.astype(BF16), own_ref, other_ref)


def final_kernel(groups, moved_ref, rf_ref, gf_ref, *refs):
    parts_f = refs[: groups + 1]
    parts_b = refs[groups + 1 : 2 * groups + 2]
    out_f_ref, out_b_ref = refs[2 * groups + 2 :]
    held = out_f_ref.shape[0]
    mine = lax.axis_index("expert") // 2
    routes_f = rf_ref[...]
    gates_f = gf_ref[...].astype(F32)
    same = lax.broadcasted_iota(jnp.int32, (held, held), 0) == lax.broadcasted_iota(
        jnp.int32, (held, held), 1
    )
    result_f = moved_ref[:held, :].astype(F32)
    result_b = moved_ref[held:, :].astype(F32)
    for i, (part_f, part_b) in enumerate(zip(parts_f, parts_b)):
        d = max(0, i - 1)
        weight = jnp.sum(jnp.where(routes_f == (mine ^ d), gates_f, 0.0), axis=0, keepdims=True)
        weigh = jnp.where(same, weight, 0.0).astype(BF16)
        rows_f = part_f[0] if i < 2 else part_f[...]
        rows_b = part_b[0] if i < 2 else part_b[...]
        result_f = result_f + jnp.dot(weigh, rows_f, preferred_element_type=F32)
        result_b = result_b + rows_b.astype(F32)
    out_f_ref[...] = result_f.astype(BF16)
    out_b_ref[...] = result_b.astype(BF16)


def local(
    carry_forward,
    carry_cotangent,
    saved_input,
    routes_forward,
    gates_forward,
    routes_backward,
    gates_backward,
    w_gate,
    w_up,
    w_down,
):
    peers = lax.axis_size("expert")
    experts = peers // 2
    groups = peers // 2
    held, width = carry_forward.shape[1:]
    hidden = w_gate.shape[3]
    topk = routes_forward.shape[2]
    capacity = min(held, max(6, held * topk // experts + 2))
    rows = -(-peers * capacity // 8) * 8
    tokens = peers * held
    weight_bytes = 6 * width * hidden
    w_g, w_u, w_d = pl.pallas_call(
        fetch_kernel,
        out_shape=[pltpu.VMEM(w.shape[2:], BF16) for w in (w_gate, w_up, w_down)],
        in_specs=[pl.BlockSpec(memory_space=pltpu.HBM)] * 3,
        out_specs=[pl.BlockSpec(memory_space=pltpu.VMEM)] * 3,
        scratch_shapes=[pltpu.SemaphoreType.DMA((3,))],
        compiler_params=pltpu.CompilerParams(vmem_limit_bytes=VMEM_LIMIT),
        cost_estimate=pl.CostEstimate(flops=0, bytes_accessed=2 * weight_bytes, transcendentals=0),
    )(*[in_hbm(w[0, 0]) for w in (w_gate, w_up, w_down)])
    routes_f, gates_f, routes_b, gates_b = [
        jnp.swapaxes(a[0], 0, 1)
        for a in (routes_forward, gates_forward, routes_backward, gates_backward)
    ]
    spare = -(-4 * topk // held) * LANES
    saved = pl.pallas_call(
        functools.partial(pack_kernel, topk),
        out_shape=jax.ShapeDtypeStruct((held, width + spare), BF16),
        in_specs=[pl.BlockSpec(memory_space=pltpu.HBM)] * 5,
        out_specs=pl.BlockSpec(memory_space=pltpu.VMEM),
        scratch_shapes=[pltpu.VMEM(a.shape, a.dtype) for a in (routes_f, gates_f, routes_b, gates_b)]
        + [pltpu.SemaphoreType.DMA, pltpu.SemaphoreType.DMA((4,))],
        compiler_params=pltpu.CompilerParams(vmem_limit_bytes=VMEM_LIMIT),
        cost_estimate=pl.CostEstimate(flops=0, bytes_accessed=4 * held * width, transcendentals=0),
    )(*[in_hbm(a) for a in (saved_input[0], routes_f, gates_f, routes_b, gates_b)])
    saved_all = [saved] + [swap(saved, "expert", 2 * d) for d in range(1, groups)]
    moved = jnp.concatenate((carry_forward[0], carry_cotangent[0]), axis=0)
    moved_all = [onward(moved, 2 * d) for d in range(groups)]
    moved_all[0], w_g, w_u, w_d = lax.optimization_barrier((moved_all[0], w_g, w_u, w_d))
    moved_all[1], w_g = lax.optimization_barrier((moved_all[1], w_g))
    w_g, w_u, w_d = in_vmem(w_g), in_vmem(w_u), in_vmem(w_d)
    saved_all = saved_all + [swap(x, "expert", 1) for x in saved_all]
    moved_all = moved_all + [swap(x, "expert", 1) for x in moved_all]
    part_f, part_b, place_f, place_b = kernel_call(
        functools.partial(up_kernel, groups, topk, rows),
        (
            jax.ShapeDtypeStruct((2 * rows, hidden), BF16),
            jax.ShapeDtypeStruct((3 * rows, hidden), BF16),
            jax.ShapeDtypeStruct((rows, tokens), BF16),
            jax.ShapeDtypeStruct((rows, tokens), BF16),
        ),
        10 * rows * width * hidden,
        weight_bytes,
    )(*moved_all, *saved_all, w_g, w_u, w_d)
    returned = [jax.ShapeDtypeStruct((groups, held, width), BF16)] * 2

    def summed(part):
        bit = lax.axis_size("dp") // 2
        while bit > 1:
            part = (part.astype(F32) + swap(part, "dp", bit).astype(F32)).astype(BF16)
            bit //= 2
        return part, swap(part, "dp", 1)

    def brought(own, other):
        other = swap(other, "expert", 1)
        came = []
        for d in range(1, groups):
            halves = (own[d].astype(F32) + other[d].astype(F32)).astype(BF16)
            came.append(swap(halves, "expert", 2 * d))
        return [own, other] + came

    back_b = kernel_call(
        functools.partial(grad_kernel, groups, rows),
        returned,
        4 * rows * width * hidden,
        4 * width * hidden,
    )(*summed(part_b), place_b, w_g, w_u)
    back_f = kernel_call(
        functools.partial(down_kernel, groups, rows),
        returned,
        2 * rows * width * hidden,
        2 * width * hidden,
    )(*summed(part_f), place_f, w_d)
    result_f, result_b = kernel_call(
        functools.partial(final_kernel, groups),
        (
            jax.ShapeDtypeStruct((held, width), BF16),
            jax.ShapeDtypeStruct((held, width), BF16),
        ),
        0,
        20 * held * width,
    )(moved_all[0], routes_f, gates_f, *brought(*back_f), *brought(*back_b))
    return (result_f[None], result_b[None])


def solution(mesh):
    placed = (
        P("pipe", "expert", "dp"),
        P("pipe", "expert", "dp"),
        P("pipe", "expert", "dp"),
        P("pipe", "expert", None),
        P("pipe", "expert", None),
        P("pipe", "expert", None),
        P("pipe", "expert", None),
        P("pipe", "expert", "dp", None),
        P("pipe", "expert", "dp", None),
        P("pipe", "expert", None, "dp"),
    )
    return jax.shard_map(
        local,
        mesh=mesh,
        in_specs=placed,
        out_specs=(P("pipe", "expert", "dp"), P("pipe", "expert", "dp")),
        check_vma=False,
    )
```

time: 52.3 us -> 40.7 us (0.78)
  local copies, waits for them, and re-layouts: 9.92 us -> 0.01 us
  waiting for transfers between devices: 27.9 us -> 19.9 us
  Pallas kernels: 3.97 us -> 7.75 us
  starting transfers between devices: 9.3 us -> 11.2 us
  other arithmetic: 0.08 us -> 0.95 us
    unnamed x18 -> x4, local copies, waits for them, and re-layouts: 6.96 us -> 0.01 us
    ppermute x9 -> x13, waiting for transfers between devices: 22.7 us -> 18.2 us  [swap(): return lax.ppermute(x, axis, [(i, i ^ bit) for i in range(peers)])]
    pallas_call x2 -> x4, Pallas kernels: 1.8 us -> 5.48 us  [the longest x1 2.63 us: local(): pl.pallas_call(fetch_kernel, out_shape=[pltpu.VMEM(w.shape[2:], BF16) for...]
    ppermute x2, waiting for transfers between devices: 5.21 us -> 1.74 us  [onward(): return lax.ppermute(x, ('pipe', 'expert'), pairs)]
    squeeze x4 -> x0, local copies, waits for them, and re-layouts: 2.95 us -> none  [the longest x1 0.74 us: local(): gates_backward[0]]
    ppermute x9 -> x13, starting transfers between devices: 4.87 us -> 6.67 us  [swap(): return lax.ppermute(x, axis, [(i, i ^ bit) for i in range(peers)])]
    concatenate x0 -> x1, other arithmetic: none -> 0.86 us  [local(): moved = jnp.concatenate((carry_forward[0], carry_cotangent[0]), axis=0)]
  transfers between devices with their start and end apart: 11 -> 15, of which waited for: 8 -> 11; matrix products, arithmetic and copies ran while one was open for 0% -> 0% of each run, Pallas kernels for 0% -> 14%
where the time goes in v2:
time: 40.7 us; the launch traced here: 40.5 us
  waiting for transfers between devices  19.9 us (49%)
  starting transfers between devices  11.2 us (28%)
  Pallas kernels  7.75 us (19%)
  other arithmetic  0.95 us (2%)
  between operations  0.74 us (2%)
    ppermute x13, waiting for transfers between devices, swap(): return lax.ppermute(x, axis, [(i, i ^ bit) for i in range(peers)])  18.2 us
    ppermute x13, starting transfers between devices, swap(): return lax.ppermute(x, axis, [(i, i ^ bit) for i in range(peers)])  6.67 us
    ppermute x2, starting transfers between devices, onward(): return lax.ppermute(x, ('pipe', 'expert'), pairs)  4.49 us
    pallas_call x1, Pallas kernels, local(): pl.pallas_call(fetch_kernel, out_shape=[pltpu.VMEM(w.shape[2:], BF16) for...  2.63 us
    ppermute x2, waiting for transfers between devices, onward(): return lax.ppermute(x, ('pipe', 'expert'), pairs)  1.74 us
    pallas_call x1, Pallas kernels, local(): kernel_call(functools.partial(up_kernel, groups, topk, rows), (jax.ShapeD...  1.45 us
    pallas_call x1, Pallas kernels, local(): kernel_call(functools.partial(grad_kernel, groups, rows), returned, 4 * r...  1.37 us
    pallas_call x1, Pallas kernels, local(): pl.pallas_call(functools.partial(pack_kernel, topk), out_shape=jax.ShapeD...  0.91 us
  transfers between devices with their start and end apart: 15, of which 11 were waited for; matrix products, arithmetic and copies ran while one was open for 0% of the time, Pallas kernels for 14%

profile of v2, /device:TPU:0, one launch (start us, length us, event | category | flops | bytes accessed | tf_op | source)
XLA Modules:
  0.0 40.5 jit_solution(4479146941492583836)
XLA Ops:
  0.6 0.9 %pad_maximum_fusion = bf16[32,1792]{1,0:T(8,128)(2,1)S(1)} fusion(bf16[16,1792]{1,0:T(8,128)(2,1)} %bitcast.23, bf16[16,1792]{1,0:T(8,128)(2,1)} %bitcast.24), kind=kLoop, calls=%fused_computation.2 | loop fusion | flops 229376 | bytes 229376 | tf_op jit(solution)/shard_map/concatenate | solution.py:256
  1.5 3.0 %collective-permute-start = (bf16[32,1792]{1,0:T(8,128)(2,1)S(1)}, bf16[32,1792]{1,0:T(8,128)(2,1)S(1)}, u32[]{:S(2)}, u32[]{:S(2)}) collective-permute-start(bf16[32,1792]{1,0:T(8,128)(2,1)S(1)} %pad_maximum_fusion), channel_id=1, source_target_pairs={{0,16},{4,20},{8,24},{12,28},{16,0},{20,4},{24,8},{28,12},{1,17},{... | collective-permute-start | bytes 344072 | tf_op jit(solution)/shard_map/ppermute | solution.py:46
  4.5 1.5 %collective-permute-start.1 = (bf16[32,1792]{1,0:T(8,128)(2,1)S(1)}, bf16[32,1792]{1,0:T(8,128)(2,1)S(1)}, u32[]{:S(2)}, u32[]{:S(2)}) collective-permute-start(bf16[32,1792]{1,0:T(8,128)(2,1)S(1)} %pad_maximum_fusion), channel_id=1, source_target_pairs={{0,24},{4,28},{8,16},{12,20},{16,8},{20,12},{24,0},{28,4},{1,25},{... | collective-permute-start | bytes 344072 | tf_op jit(solution)/shard_map/ppermute | solution.py:46
  6.0 0.9 %shard_map.114.refs_4_ = bf16[16,1920]{1,0:T(8,128)(2,1)S(1)} custom-call(bf16[16,1792]{1,0:T(8,128)(2,1)} %bitcast.25, s32[1,16]{1,0:T(1,128)} %bitcast.16, bf16[1,16]{1,0:T(2,128)(2,1)} %bitcast.18, s32[1,16]{1,0:T(1,128)} %bitcast.26, bf16[1,16]{1,0:T(2,128)(2,1)} %bitcast.27), custom_call_target="tpu_custom_call" | custom-call | bytes 114688 | tf_op jit(solution)/shard_map/pallas_call | solution.py:245
  6.9 0.1 collective-permute-start.4
  7.0 2.6 %shard_map.113 = (bf16[1792,512]{1,0:T(8,128)(2,1)S(1)}, bf16[1792,512]{1,0:T(8,128)(2,1)S(1)}, bf16[512,1792]{1,0:T(8,128)(2,1)S(1)}) custom-call(bf16[1792,512]{1,0:T(8,128)(2,1)} %bitcast.20, bf16[1792,512]{1,0:T(8,128)(2,1)} %bitcast.21, bf16[512,1792]{1,0:T(8,128)(2,1)} %bitcast.22), custom_call_target="tpu_custom_call" | custom-call | bytes 11010048 | tf_op jit(solution)/shard_map/pallas_call | solution.py:231
  9.7 1.7 %collective-permute-done.1.refs_1_ = bf16[32,1792]{1,0:T(8,128)(2,1)S(1)} collective-permute-done((bf16[32,1792]{1,0:T(8,128)(2,1)S(1)}, bf16[32,1792]{1,0:T(8,128)(2,1)S(1)}, u32[]{:S(2)}, u32[]{:S(2)}) %collective-permute-start.1) | collective-permute-done | bytes 114720 | tf_op jit(solution)/shard_map/ppermute | solution.py:46
  11.4 0.5 %collective-permute-start.2 = (bf16[32,1792]{1,0:T(8,128)(2,1)S(1)}, bf16[32,1792]{1,0:T(8,128)(2,1)S(1)}, u32[]{:S(2)}, u32[]{:S(2)}) collective-permute-start(bf16[32,1792]{1,0:T(8,128)(2,1)S(1)} %collective-permute-done.refs_0_.moved_ref), channel_id=1, source_target_pairs={{0,4},{4,0},{8,12},{12,8},{1,5},{5,1},{9,13},{13,9},{2,6},{6,2},{1... | collective-permute-start | bytes 344072 | tf_op jit(solution)/shard_map/ppermute | solution.py:35
  11.9 0.0 collective-permute-start.5
  11.9 0.1 collective-permute-done.4.refs_5_
  12.0 0.4 collective-permute-start.6
  12.4 0.7 %collective-permute-done.5.refs_6_ = bf16[16,1920]{1,0:T(8,128)(2,1)S(1)} collective-permute-done((bf16[16,1920]{1,0:T(8,128)(2,1)S(1)}, bf16[16,1920]{1,0:T(8,128)(2,1)S(1)}, u32[]{:S(2)}, u32[]{:S(2)}) %collective-permute-start.5) | collective-permute-done | bytes 61472 | tf_op jit(solution)/shard_map/ppermute | solution.py:35
  13.2 0.2 collective-permute-done.6.refs_7_
  13.3 1.5 %shard_map.115 = (bf16[80,512]{1,0:T(8,128)(2,1)S(1)}, bf16[120,512]{1,0:T(8,128)(2,1)S(1)}, bf16[40,64]{1,0:T(8,128)(2,1)S(1)}, bf16[40,64]{1,0:T(8,128)(2,1)S(1)}) custom-call(bf16[32,1792]{1,0:T(8,128)(2,1)S(1)} %collective-permute-done.refs_0_.moved_ref, bf16[32,1792]{1,0:T(8,128)(2,1)S(1)} %collective-permute-done.1.refs_1_, ...), custom_call_target="tpu_custom_call" | custom-call | flops 367001600 | bytes 5505024 | tf_op jit(solution)/shard_map/pallas_call | solution.py:263
  14.8 2.7 %collective-permute-start.7 = (bf16[80,512]{1,0:T(8,128)(2,1)S(1)}, bf16[80,512]{1,0:T(8,128)(2,1)S(1)}, u32[]{:S(2)}, u32[]{:S(2)}) collective-permute-start(bf16[80,512]{1,0:T(8,128)(2,1)S(1)} %get-tuple-element.30), channel_id=1, source_target_pairs={{0,2},{1,3},{2,0},{3,1},{4,6},{5,7},{6,4},{7,5},{8,10},{9,11},{10,... | collective-permute-start | bytes 245768 | tf_op jit(solution)/shard_map/ppermute | solution.py:35
  17.5 0.3 collective-permute-start.11
  17.8 7.6 %collective-permute-done.7 = bf16[80,512]{1,0:T(8,128)(2,1)S(1)} collective-permute-done((bf16[80,512]{1,0:T(8,128)(2,1)S(1)}, bf16[80,512]{1,0:T(8,128)(2,1)S(1)}, u32[]{:S(2)}, u32[]{:S(2)}) %collective-permute-start.7) | collective-permute-done | bytes 81952 | tf_op jit(solution)/shard_map/ppermute | solution.py:35
  25.4 0.2 collective-permute-start.8
  25.7 1.9 %collective-permute-done.11 = bf16[120,512]{1,0:T(8,128)(2,1)S(1)} collective-permute-done((bf16[120,512]{1,0:T(8,128)(2,1)S(1)}, bf16[120,512]{1,0:T(8,128)(2,1)S(1)}, u32[]{:S(2)}, u32[]{:S(2)}) %collective-permute-start.11) | collective-permute-done | bytes 122912 | tf_op jit(solution)/shard_map/ppermute | solution.py:35
  27.6 0.7 %collective-permute-start.12 = (bf16[120,512]{1,0:T(8,128)(2,1)S(1)}, bf16[120,512]{1,0:T(8,128)(2,1)S(1)}, u32[]{:S(2)}, u32[]{:S(2)}) collective-permute-start(bf16[120,512]{1,0:T(8,128)(2,1)S(1)} %add_convert_fusion.a_ref), channel_id=1, source_target_pairs={{0,1},{1,0},{2,3},{3,2},{4,5},{5,4},{6,7},{7,6},{8,9},{9,8},{10,11... | collective-permute-start | bytes 368648 | tf_op jit(solution)/shard_map/ppermute | solution.py:35
  28.3 1.9 %collective-permute-done.8.b_ref = bf16[80,512]{1,0:T(8,128)(2,1)S(1)} collective-permute-done((bf16[80,512]{1,0:T(8,128)(2,1)S(1)}, bf16[80,512]{1,0:T(8,128)(2,1)S(1)}, u32[]{:S(2)}, u32[]{:S(2)}) %collective-permute-start.8) | collective-permute-done | bytes 81952 | tf_op jit(solution)/shard_map/ppermute | solution.py:35
  30.2 0.6 %shard_map.116 = (bf16[2,16,1792]{2,1,0:T(8,128)(2,1)S(1)}, bf16[2,16,1792]{2,1,0:T(8,128)(2,1)S(1)}) custom-call(bf16[80,512]{1,0:T(8,128)(2,1)S(1)} %add_convert_fusion.1.a_ref, bf16[80,512]{1,0:T(8,128)(2,1)S(1)} %collective-permute-done.8.b_ref, bf16[40,64]{1,0:T(8,128)(2,1)S(1)} %get-tuple-element.31.place_ref, ...), custom_call_target="tpu_custom_call" | custom-call | flops 73400320 | bytes 1835008 | tf_op jit(solution)/shard_map/pallas_call | solution.py:297
  30.8 0.1 collective-permute-start.9
  30.9 1.7 %collective-permute-done.12.b_ref = bf16[120,512]{1,0:T(8,128)(2,1)S(1)} collective-permute-done((bf16[120,512]{1,0:T(8,128)(2,1)S(1)}, bf16[120,512]{1,0:T(8,128)(2,1)S(1)}, u32[]{:S(2)}, u32[]{:S(2)}) %collective-permute-start.12) | collective-permute-done | bytes 122912 | tf_op jit(solution)/shard_map/ppermute | solution.py:35
  32.6 1.4 %shard_map.117 = (bf16[2,16,1792]{2,1,0:T(8,128)(2,1)S(1)}, bf16[2,16,1792]{2,1,0:T(8,128)(2,1)S(1)}) custom-call(bf16[120,512]{1,0:T(8,128)(2,1)S(1)} %add_convert_fusion.a_ref, bf16[120,512]{1,0:T(8,128)(2,1)S(1)} %collective-permute-done.12.b_ref, bf16[40,64]{1,0:T(8,128)(2,1)S(1)} %get-tuple-element.35.place_ref, ...), custom_call_target="tpu_custom_call" | custom-call | flops 146800640 | bytes 3670016 | tf_op jit(solution)/shard_map/pallas_call | solution.py:291
  34.0 0.1 collective-permute-start.13
  34.1 0.7 %collective-permute-start.10 = (bf16[16,1792]{1,0:T(8,128)(2,1)S(1)}, bf16[16,1792]{1,0:T(8,128)(2,1)S(1)}, u32[]{:S(2)}, u32[]{:S(2)}) collective-permute-start(bf16[16,1792]{1,0:T(8,128)(2,1)S(1)} %fusion), channel_id=1, source_target_pairs={{0,8},{4,12},{8,0},{12,4},{1,9},{5,13},{9,1},{13,5},{2,10},{6,14},... | collective-permute-start | bytes 172040 | tf_op jit(solution)/shard_map/ppermute | solution.py:35
  34.8 0.5 %collective-permute-done.13.refs_4_ = bf16[2,16,1792]{2,1,0:T(8,128)(2,1)S(1)} collective-permute-done((bf16[2,16,1792]{2,1,0:T(8,128)(2,1)S(1)}, bf16[2,16,1792]{2,1,0:T(8,128)(2,1)S(1)}, u32[]{:S(2)}, u32[]{:S(2)}) %collective-permute-start.13) | collective-permute-done | bytes 114720 | tf_op jit(solution)/shard_map/ppermute | solution.py:35
  35.4 0.9 %collective-permute-start.14 = (bf16[16,1792]{1,0:T(8,128)(2,1)S(1)}, bf16[16,1792]{1,0:T(8,128)(2,1)S(1)}, u32[]{:S(2)}, u32[]{:S(2)}) collective-permute-start(bf16[16,1792]{1,0:T(8,128)(2,1)S(1)} %fusion.1), channel_id=1, source_target_pairs={{0,8},{4,12},{8,0},{12,4},{1,9},{5,13},{9,1},{13,5},{2,10},{6,14},... | collective-permute-start | bytes 172040 | tf_op jit(solution)/shard_map/ppermute | solution.py:35
  36.2 2.5 %collective-permute-done.10.refs_2_ = bf16[16,1792]{1,0:T(8,128)(2,1)S(1)} collective-permute-done((bf16[16,1792]{1,0:T(8,128)(2,1)S(1)}, bf16[16,1792]{1,0:T(8,128)(2,1)S(1)}, u32[]{:S(2)}, u32[]{:S(2)}) %collective-permute-start.10) | collective-permute-done | bytes 57376 | tf_op jit(solution)/shard_map/ppermute | solution.py:35
  38.8 0.9 %collective-permute-done.14.refs_5_ = bf16[16,1792]{1,0:T(8,128)(2,1)S(1)} collective-permute-done((bf16[16,1792]{1,0:T(8,128)(2,1)S(1)}, bf16[16,1792]{1,0:T(8,128)(2,1)S(1)}, u32[]{:S(2)}, u32[]{:S(2)}) %collective-permute-start.14) | collective-permute-done | bytes 57376 | tf_op jit(solution)/shard_map/ppermute | solution.py:35
  39.7 0.8 %shard_map.118 = (bf16[16,1792]{1,0:T(8,128)(2,1)}, bf16[16,1792]{1,0:T(8,128)(2,1)}) custom-call(bf16[32,1792]{1,0:T(8,128)(2,1)S(1)} %collective-permute-done.refs_0_.moved_ref, s32[1,16]{1,0:T(1,128)S(1)} %bitcast.17, bf16[1,16]{1,0:T(2,128)(2,1)S(1)} %bitcast.19, bf16[2,16,1792]{2,1,0:T(8,128)(2,1)S(1)} %get-tuple-element.32.refs_0_, ...), custom_call_target="tpu_custom_call" | custom-call | bytes 573440 | tf_op jit(solution)/shard_map/pallas_call | solution.py:303
  (13 shorter events, 0.1 us)
Async XLA Ops:
  1.5 8.2 %collective-permute-start = (bf16[32,1792]{1,0:T(8,128)(2,1)S(1)}, bf16[32,1792]{1,0:T(8,128)(2,1)S(1)}, u32[]{:S(2)}, u32[]{:S(2)}) collective-permute-start(bf16[32,1792]{1,0:T(8,128)(2,1)S(1)} %pad_maximum_fusion), channel_id=1, source_target_pairs={{0,16},{4,20},{8,24},{12,28},{16,0},{20,4},{24,8},{28,12},{1,17},{... | collective-permute-start | bytes 344072 | tf_op jit(solution)/shard_map/ppermute | solution.py:46
  4.5 6.9 %collective-permute-start.1 = (bf16[32,1792]{1,0:T(8,128)(2,1)S(1)}, bf16[32,1792]{1,0:T(8,128)(2,1)S(1)}, u32[]{:S(2)}, u32[]{:S(2)}) collective-permute-start(bf16[32,1792]{1,0:T(8,128)(2,1)S(1)} %pad_maximum_fusion), channel_id=1, source_target_pairs={{0,24},{4,28},{8,16},{12,20},{16,8},{20,12},{24,0},{28,4},{1,25},{... | collective-permute-start | bytes 344072 | tf_op jit(solution)/shard_map/ppermute | solution.py:46
  6.9 5.1 %collective-permute-start.4 = (bf16[16,1920]{1,0:T(8,128)(2,1)S(1)}, bf16[16,1920]{1,0:T(8,128)(2,1)S(1)}, u32[]{:S(2)}, u32[]{:S(2)}) collective-permute-start(bf16[16,1920]{1,0:T(8,128)(2,1)S(1)} %shard_map.114.refs_4_), channel_id=1, source_target_pairs={{0,8},{4,12},{8,0},{12,4},{1,9},{5,13},{9,1},{13,5},{2,10},{6,14},... | collective-permute-start | bytes 184328 | tf_op jit(solution)/shard_map/ppermute | solution.py:35
  11.4 1.9 %collective-permute-start.3 = (bf16[32,1792]{1,0:T(8,128)(2,1)S(1)}, bf16[32,1792]{1,0:T(8,128)(2,1)S(1)}, u32[]{:S(2)}, u32[]{:S(2)}) collective-permute-start(bf16[32,1792]{1,0:T(8,128)(2,1)S(1)} %collective-permute-done.1.refs_1_), channel_id=1, source_target_pairs={{0,4},{4,0},{8,12},{12,8},{1,5},{5,1},{9,13},{13,9},{2,6},{6,2},{1... | collective-permute-start | bytes 344072 | tf_op jit(solution)/shard_map/ppermute | solution.py:35
  11.4 1.9 %collective-permute-start.2 = (bf16[32,1792]{1,0:T(8,128)(2,1)S(1)}, bf16[32,1792]{1,0:T(8,128)(2,1)S(1)}, u32[]{:S(2)}, u32[]{:S(2)}) collective-permute-start(bf16[32,1792]{1,0:T(8,128)(2,1)S(1)} %collective-permute-done.refs_0_.moved_ref), channel_id=1, source_target_pairs={{0,4},{4,0},{8,12},{12,8},{1,5},{5,1},{9,13},{13,9},{2,6},{6,2},{1... | collective-permute-start | bytes 344072 | tf_op jit(solution)/shard_map/ppermute | solution.py:35
  11.9 1.2 %collective-permute-start.5 = (bf16[16,1920]{1,0:T(8,128)(2,1)S(1)}, bf16[16,1920]{1,0:T(8,128)(2,1)S(1)}, u32[]{:S(2)}, u32[]{:S(2)}) collective-permute-start(bf16[16,1920]{1,0:T(8,128)(2,1)S(1)} %shard_map.114.refs_4_), channel_id=1, source_target_pairs={{0,4},{4,0},{8,12},{12,8},{1,5},{5,1},{9,13},{13,9},{2,6},{6,2},{1... | collective-permute-start | bytes 184328 | tf_op jit(solution)/shard_map/ppermute | solution.py:35
  12.0 1.3 %collective-permute-start.6 = (bf16[16,1920]{1,0:T(8,128)(2,1)S(1)}, bf16[16,1920]{1,0:T(8,128)(2,1)S(1)}, u32[]{:S(2)}, u32[]{:S(2)}) collective-permute-start(bf16[16,1920]{1,0:T(8,128)(2,1)S(1)} %collective-permute-done.4.refs_5_), channel_id=1, source_target_pairs={{0,4},{4,0},{8,12},{12,8},{1,5},{5,1},{9,13},{13,9},{2,6},{6,2},{1... | collective-permute-start | bytes 184328 | tf_op jit(solution)/shard_map/ppermute | solution.py:35
  14.8 10.6 %collective-permute-start.7 = (bf16[80,512]{1,0:T(8,128)(2,1)S(1)}, bf16[80,512]{1,0:T(8,128)(2,1)S(1)}, u32[]{:S(2)}, u32[]{:S(2)}) collective-permute-start(bf16[80,512]{1,0:T(8,128)(2,1)S(1)} %get-tuple-element.30), channel_id=1, source_target_pairs={{0,2},{1,3},{2,0},{3,1},{4,6},{5,7},{6,4},{7,5},{8,10},{9,11},{10,... | collective-permute-start | bytes 245768 | tf_op jit(solution)/shard_map/ppermute | solution.py:35
  17.5 10.1 %collective-permute-start.11 = (bf16[120,512]{1,0:T(8,128)(2,1)S(1)}, bf16[120,512]{1,0:T(8,128)(2,1)S(1)}, u32[]{:S(2)}, u32[]{:S(2)}) collective-permute-start(bf16[120,512]{1,0:T(8,128)(2,1)S(1)} %get-tuple-element.34), channel_id=1, source_target_pairs={{0,2},{1,3},{2,0},{3,1},{4,6},{5,7},{6,4},{7,5},{8,10},{9,11},{10,... | collective-permute-start | bytes 368648 | tf_op jit(solution)/shard_map/ppermute | solution.py:35
  25.4 4.8 %collective-permute-start.8 = (bf16[80,512]{1,0:T(8,128)(2,1)S(1)}, bf16[80,512]{1,0:T(8,128)(2,1)S(1)}, u32[]{:S(2)}, u32[]{:S(2)}) collective-permute-start(bf16[80,512]{1,0:T(8,128)(2,1)S(1)} %add_convert_fusion.1.a_ref), channel_id=1, source_target_pairs={{0,1},{1,0},{2,3},{3,2},{4,5},{5,4},{6,7},{7,6},{8,9},{9,8},{10,11... | collective-permute-start | bytes 245768 | tf_op jit(solution)/shard_map/ppermute | solution.py:35
  27.6 5.0 %collective-permute-start.12 = (bf16[120,512]{1,0:T(8,128)(2,1)S(1)}, bf16[120,512]{1,0:T(8,128)(2,1)S(1)}, u32[]{:S(2)}, u32[]{:S(2)}) collective-permute-start(bf16[120,512]{1,0:T(8,128)(2,1)S(1)} %add_convert_fusion.a_ref), channel_id=1, source_target_pairs={{0,1},{1,0},{2,3},{3,2},{4,5},{5,4},{6,7},{7,6},{8,9},{9,8},{10,11... | collective-permute-start | bytes 368648 | tf_op jit(solution)/shard_map/ppermute | solution.py:35
  30.8 3.2 %collective-permute-start.9 = (bf16[2,16,1792]{2,1,0:T(8,128)(2,1)S(1)}, bf16[2,16,1792]{2,1,0:T(8,128)(2,1)S(1)}, u32[]{:S(2)}, u32[]{:S(2)}) collective-permute-start(bf16[2,16,1792]{2,1,0:T(8,128)(2,1)S(1)} %get-tuple-element.33), channel_id=1, source_target_pairs={{0,4},{4,0},{8,12},{12,8},{1,5},{5,1},{9,13},{13,9},{2,6},{6,2},{1... | collective-permute-start | bytes 344072 | tf_op jit(solution)/shard_map/ppermute | solution.py:35
  32.6 7.1 %copy-start = (s32[1,16,1]{1,2,0:T(1,128)S(1)}, s32[1,16,1]{1,2,0:T(1,128)}, u32[]{:S(2)}) copy-start(s32[1,16,1]{1,2,0:T(1,128)} %param.13) | copy-start | bytes 196
  32.6 7.1 %copy-start.1 = (bf16[1,16,1]{1,2,0:T(2,128)(2,1)S(1)}, bf16[1,16,1]{1,2,0:T(2,128)(2,1)}, u32[]{:S(2)}) copy-start(bf16[1,16,1]{1,2,0:T(2,128)(2,1)} %param.14) | copy-start | bytes 100
  34.0 1.4 %collective-permute-start.13 = (bf16[2,16,1792]{2,1,0:T(8,128)(2,1)S(1)}, bf16[2,16,1792]{2,1,0:T(8,128)(2,1)S(1)}, u32[]{:S(2)}, u32[]{:S(2)}) collective-permute-start(bf16[2,16,1792]{2,1,0:T(8,128)(2,1)S(1)} %get-tuple-element.37), channel_id=1, source_target_pairs={{0,4},{4,0},{8,12},{12,8},{1,5},{5,1},{9,13},{13,9},{2,6},{6,2},{1... | collective-permute-start | bytes 344072 | tf_op jit(solution)/shard_map/ppermute | solution.py:35
  34.1 4.7 %collective-permute-start.10 = (bf16[16,1792]{1,0:T(8,128)(2,1)S(1)}, bf16[16,1792]{1,0:T(8,128)(2,1)S(1)}, u32[]{:S(2)}, u32[]{:S(2)}) collective-permute-start(bf16[16,1792]{1,0:T(8,128)(2,1)S(1)} %fusion), channel_id=1, source_target_pairs={{0,8},{4,12},{8,0},{12,4},{1,9},{5,13},{9,1},{13,5},{2,10},{6,14},... | collective-permute-start | bytes 172040 | tf_op jit(solution)/shard_map/ppermute | solution.py:35
  35.4 4.3 %collective-permute-start.14 = (bf16[16,1792]{1,0:T(8,128)(2,1)S(1)}, bf16[16,1792]{1,0:T(8,128)(2,1)S(1)}, u32[]{:S(2)}, u32[]{:S(2)}) collective-permute-start(bf16[16,1792]{1,0:T(8,128)(2,1)S(1)} %fusion.1), channel_id=1, source_target_pairs={{0,8},{4,12},{8,0},{12,4},{1,9},{5,13},{9,1},{13,5},{2,10},{6,14},... | collective-permute-start | bytes 172040 | tf_op jit(solution)/shard_map/ppermute | solution.py:35

commit v3 on v2

--- a/solution.py
+++ b/solution.py
@@ -46,15 +46,20 @@
     return lax.ppermute(x, ("pipe", "expert"), pairs)
 
 
-def pack_kernel(topk, b_hbm, *refs):
+def pack_kernel(x_hbm, c_hbm, b_hbm, *refs):
     rows, width = b_hbm.shape
-    noted, (saved_ref, *held, sem, sems) = refs[:4], refs[4:]
-    copies = [pltpu.make_async_copy(b_hbm, saved_ref.at[:, pl.ds(0, width)], sem)]
-    for i, (source, target) in enumerate(zip(noted, held)):
-        copies.append(pltpu.make_async_copy(source, target, sems.at[i]))
+    noted, (moved_ref, saved_ref, *held, sems) = refs[:4], refs[4:]
+    pairs = list(zip(noted, held)) + [
+        (x_hbm, moved_ref.at[pl.ds(0, rows)]),
+        (c_hbm, moved_ref.at[pl.ds(rows, rows)]),
+        (b_hbm, saved_ref.at[:, pl.ds(0, width)]),
+    ]
+    copies = [
+        pltpu.make_async_copy(source, target, sems.at[i]) for i, (source, target) in enumerate(pairs)
+    ]
     for copy in copies:
         copy.start()
-    for copy in copies[1:]:
+    for copy in copies[:4]:
         copy.wait()
     notes = jnp.concatenate([r[...].astype(F32) for r in held], axis=0)
     for first in range(0, saved_ref.shape[1] - width, LANES):
@@ -62,7 +67,8 @@
         part = notes[block : block + rows]
         part = jnp.pad(part, ((0, rows - part.shape[0]), (0, LANES - part.shape[1])))
         saved_ref[:, width + first : width + first + LANES] = part.astype(BF16)
-    copies[0].wait()
+    for copy in copies[4:]:
+        copy.wait()
 
 
 def fetch_kernel(*refs):
@@ -147,44 +153,52 @@
     gate = jnp.dot(both, w_g_ref[...], preferred_element_type=F32)
     upper = jnp.dot(both, w_u_ref[...], preferred_element_type=F32)
     dhid = lax.dot_general(grads_b, w_d_ref[...], (((1,), (1,)), ((), ())), preferred_element_type=F32)
-    part_f_ref[...] = jnp.concatenate([gate[:rows], upper[:rows]], axis=0).astype(BF16)
-    part_b_ref[...] = jnp.concatenate([gate[rows:], upper[rows:], dhid], axis=0).astype(BF16)
-
-
-def return_rows(groups, place_ref, out, own_ref, other_ref):
-    back = (((0,), (0,)), ((), ()))
-    full = lax.dot_general(place_ref[...], out, back, preferred_element_type=F32).astype(BF16)
-    held = own_ref.shape[1]
-    for d in range(groups):
-        own_ref[d] = full[d * held : (d + 1) * held]
-        other_ref[d] = full[(groups + d) * held : (groups + d + 1) * held]
-
-
-def down_kernel(groups, rows, a_ref, b_ref, place_ref, w_d_ref, own_ref, other_ref):
-    total = a_ref[...].astype(F32) + b_ref[...].astype(F32)
-    gate, upper = total[:rows], total[rows:]
-    hidden = (gate * jax.nn.sigmoid(gate) * upper).astype(BF16)
-    out = jnp.dot(hidden, w_d_ref[...], preferred_element_type=F32).astype(BF16)
-    return_rows(groups, place_ref, out, own_ref, other_ref)
-
-
-def grad_kernel(groups, rows, a_ref, b_ref, place_ref, w_g_ref, w_u_ref, own_ref, other_ref):
-    total = a_ref[...].astype(F32) + b_ref[...].astype(F32)
-    gate, upper, dhid = total[:rows], total[rows : 2 * rows], total[2 * rows :]
-    sigma = jax.nn.sigmoid(gate)
-    slope = sigma * (1.0 + gate * (1.0 - sigma))
-    dgate = (dhid * upper * slope).astype(BF16)
-    dupper = (dhid * (gate * sigma)).astype(BF16)
+    part_f_ref[...] = jnp.concatenate([gate[:rows], upper[:rows], dhid], axis=0).astype(BF16)
+    part_b_ref[...] = jnp.concatenate([gate[rows:], upper[rows:]], axis=0).astype(BF16)
+
+
+def down_kernel(
+    groups,
+    rows,
+    fa_ref,
+    fb_ref,
+    ba_ref,
+    bb_ref,
+    place_f_ref,
+    place_b_ref,
+    w_g_ref,
+    w_u_ref,
+    w_d_ref,
+    own_ref,
+    other_ref,
+):
+    total_f = fa_ref[...].astype(F32) + fb_ref[...].astype(F32)
+    total_b = ba_ref[...].astype(F32) + bb_ref[...].astype(F32)
+    gate_f, upper_f, dhid = [total_f[i * rows : (i + 1) * rows] for i in range(3)]
+    gate_b, upper_b = total_b[:rows], total_b[rows:]
+    hidden = (gate_f * jax.nn.sigmoid(gate_f) * upper_f).astype(BF16)
+    sigma = jax.nn.sigmoid(gate_b)
+    slope = sigma * (1.0 + gate_b * (1.0 - sigma))
+    dgate = (dhid * upper_b * slope).astype(BF16)
+    dupper = (dhid * (gate_b * sigma)).astype(BF16)
     turned = (((1,), (1,)), ((), ()))
+    out_f = jnp.dot(hidden, w_d_ref[...], preferred_element_type=F32).astype(BF16)
     grad = lax.dot_general(dgate, w_g_ref[...], turned, preferred_element_type=F32)
     grad = grad + lax.dot_general(dupper, w_u_ref[...], turned, preferred_element_type=F32)
-    return_rows(groups, place_ref, grad.astype(BF16), own_ref, other_ref)
-
-
-def final_kernel(groups, moved_ref, rf_ref, gf_ref, *refs):
-    parts_f = refs[: groups + 1]
-    parts_b = refs[groups + 1 : 2 * groups + 2]
-    out_f_ref, out_b_ref = refs[2 * groups + 2 :]
+    grad = grad.astype(BF16)
+    back = (((0,), (0,)), ((), ()))
+    full_f = lax.dot_general(place_f_ref[...], out_f, back, preferred_element_type=F32).astype(BF16)
+    full_b = lax.dot_general(place_b_ref[...], grad, back, preferred_element_type=F32).astype(BF16)
+    held = own_ref.shape[1] // 2
+    for d in range(groups):
+        for ref, at in ((own_ref, d * held), (other_ref, (groups + d) * held)):
+            ref[d, :held, :] = full_f[at : at + held]
+            ref[d, held:, :] = full_b[at : at + held]
+
+
+def final_kernel(groups, moved_ref, rf_ref, gf_ref, own_ref, other_ref, *refs):
+    came = refs[: groups - 1]
+    out_f_ref, out_b_ref = refs[groups - 1 :]
     held = out_f_ref.shape[0]
     mine = lax.axis_index("expert") // 2
     routes_f = rf_ref[...]
@@ -194,14 +208,12 @@
     )
     result_f = moved_ref[:held, :].astype(F32)
     result_b = moved_ref[held:, :].astype(F32)
-    for i, (part_f, part_b) in enumerate(zip(parts_f, parts_b)):
-        d = max(0, i - 1)
+    for d in range(groups):
         weight = jnp.sum(jnp.where(routes_f == (mine ^ d), gates_f, 0.0), axis=0, keepdims=True)
         weigh = jnp.where(same, weight, 0.0).astype(BF16)
-        rows_f = part_f[0] if i < 2 else part_f[...]
-        rows_b = part_b[0] if i < 2 else part_b[...]
-        result_f = result_f + jnp.dot(weigh, rows_f, preferred_element_type=F32)
-        result_b = result_b + rows_b.astype(F32)
+        for ref in (own_ref.at[0], other_ref.at[0]) if d == 0 else (came[d - 1],):
+            result_f = result_f + jnp.dot(weigh, ref[:held, :], preferred_element_type=F32)
+            result_b = result_b + ref[held:, :].astype(F32)
     out_f_ref[...] = result_f.astype(BF16)
     out_b_ref[...] = result_b.astype(BF16)
 
@@ -242,64 +254,62 @@
         for a in (routes_forward, gates_forward, routes_backward, gates_backward)
     ]
     spare = -(-4 * topk // held) * LANES
-    saved = pl.pallas_call(
-        functools.partial(pack_kernel, topk),
-        out_shape=jax.ShapeDtypeStruct((held, width + spare), BF16),
-        in_specs=[pl.BlockSpec(memory_space=pltpu.HBM)] * 5,
-        out_specs=pl.BlockSpec(memory_space=pltpu.VMEM),
+    moved, saved = pl.pallas_call(
+        pack_kernel,
+        out_shape=[
+            jax.ShapeDtypeStruct((2 * held, width), BF16),
+            jax.ShapeDtypeStruct((held, width + spare), BF16),
+        ],
+        in_specs=[pl.BlockSpec(memory_space=pltpu.HBM)] * 7,
+        out_specs=[pl.BlockSpec(memory_space=pltpu.VMEM)] * 2,
         scratch_shapes=[pltpu.VMEM(a.shape, a.dtype) for a in (routes_f, gates_f, routes_b, gates_b)]
-        + [pltpu.SemaphoreType.DMA, pltpu.SemaphoreType.DMA((4,))],
+        + [pltpu.SemaphoreType.DMA((7,))],
         compiler_params=pltpu.CompilerParams(vmem_limit_bytes=VMEM_LIMIT),
-        cost_estimate=pl.CostEstimate(flops=0, bytes_accessed=4 * held * width, transcendentals=0),
-    )(*[in_hbm(a) for a in (saved_input[0], routes_f, gates_f, routes_b, gates_b)])
+        cost_estimate=pl.CostEstimate(flops=0, bytes_accessed=12 * held * width, transcendentals=0),
+    )(
+        *[in_hbm(a[0]) for a in (carry_forward, carry_cotangent, saved_input)],
+        *[in_hbm(a) for a in (routes_f, gates_f, routes_b, gates_b)],
+    )
+    moved_all = [onward(moved, 2 * d) for d in range(groups)]
+    moved_all = [onward(moved, 2 * d) for d in range(groups)]
     saved_all = [saved] + [swap(saved, "expert", 2 * d) for d in range(1, groups)]
-    moved = jnp.concatenate((carry_forward[0], carry_cotangent[0]), axis=0)
-    moved_all = [onward(moved, 2 * d) for d in range(groups)]
+    saved_all = saved_all + [swap(x, "expert", 1) for x in saved_all]
     moved_all[0], w_g, w_u, w_d = lax.optimization_barrier((moved_all[0], w_g, w_u, w_d))
     moved_all[1], w_g = lax.optimization_barrier((moved_all[1], w_g))
     w_g, w_u, w_d = in_vmem(w_g), in_vmem(w_u), in_vmem(w_d)
-    saved_all = saved_all + [swap(x, "expert", 1) for x in saved_all]
+    moved_all[0], *saved_all = lax.optimization_barrier((moved_all[0], *saved_all))
     moved_all = moved_all + [swap(x, "expert", 1) for x in moved_all]
     part_f, part_b, place_f, place_b = kernel_call(
         functools.partial(up_kernel, groups, topk, rows),
         (
+            jax.ShapeDtypeStruct((3 * rows, hidden), BF16),
             jax.ShapeDtypeStruct((2 * rows, hidden), BF16),
-            jax.ShapeDtypeStruct((3 * rows, hidden), BF16),
             jax.ShapeDtypeStruct((rows, tokens), BF16),
             jax.ShapeDtypeStruct((rows, tokens), BF16),
         ),
         10 * rows * width * hidden,
         weight_bytes,
     )(*moved_all, *saved_all, w_g, w_u, w_d)
-    returned = [jax.ShapeDtypeStruct((groups, held, width), BF16)] * 2
-
-    def summed(part):
-        bit = lax.axis_size("dp") // 2
-        while bit > 1:
-            part = (part.astype(F32) + swap(part, "dp", bit).astype(F32)).astype(BF16)
-            bit //= 2
-        return part, swap(part, "dp", 1)
-
-    def brought(own, other):
-        other = swap(other, "expert", 1)
-        came = []
-        for d in range(1, groups):
-            halves = (own[d].astype(F32) + other[d].astype(F32)).astype(BF16)
-            came.append(swap(halves, "expert", 2 * d))
-        return [own, other] + came
-
-    back_b = kernel_call(
-        functools.partial(grad_kernel, groups, rows),
-        returned,
-        4 * rows * width * hidden,
-        4 * width * hidden,
-    )(*summed(part_b), place_b, w_g, w_u)
-    back_f = kernel_call(
+    bits = [1 << i for i in range(lax.axis_size("dp").bit_length() - 1)]
+    last = bits[-1]
+    for up, down in zip(bits, bits[::-1]):
+        came_f = swap(part_f, "dp", up)
+        came_b = swap(part_b, "dp", down)
+        if up == last:
+            break
+        part_f = (part_f.astype(F32) + came_f.astype(F32)).astype(BF16)
+        part_b = (part_b.astype(F32) + came_b.astype(F32)).astype(BF16)
+    own, other = kernel_call(
         functools.partial(down_kernel, groups, rows),
-        returned,
-        2 * rows * width * hidden,
-        2 * width * hidden,
-    )(*summed(part_f), place_f, w_d)
+        [jax.ShapeDtypeStruct((groups, 2 * held, width), BF16)] * 2,
+        6 * rows * width * hidden,
+        weight_bytes,
+    )(part_f, came_f, part_b, came_b, place_f, place_b, w_g, w_u, w_d)
+    other = swap(other, "expert", 1)
+    came = []
+    for d in range(1, groups):
+        halves = (own[d].astype(F32) + other[d].astype(F32)).astype(BF16)
+        came.append(swap(halves, "expert", 2 * d))
     result_f, result_b = kernel_call(
         functools.partial(final_kernel, groups),
         (
@@ -308,7 +318,7 @@
         ),
         0,
         20 * held * width,
-    )(moved_all[0], routes_f, gates_f, *brought(*back_f), *brought(*back_b))
+    )(moved_all[0], routes_f, gates_f, own, other, *came)
     return (result_f[None], result_b[None])
 
 

time: 40.7 us -> 39.5 us (0.971)
  waiting for transfers between devices: 19.9 us -> 16.2 us
  starting transfers between devices: 11.2 us -> 14.7 us
  other arithmetic: 0.95 us -> 0.08 us
    ppermute x13 -> x11, starting transfers between devices: 6.67 us -> 13.2 us  [swap(): return lax.ppermute(x, axis, [(i, i ^ bit) for i in range(peers)])]
    ppermute x13 -> x11, waiting for transfers between devices: 18.2 us -> 13.8 us  [swap(): return lax.ppermute(x, axis, [(i, i ^ bit) for i in range(peers)])]
    ppermute x2, starting transfers between devices: 4.49 us -> 1.54 us  [onward(): return lax.ppermute(x, ('pipe', 'expert'), pairs)]
    concatenate x1 -> x0, other arithmetic: 0.86 us -> none  [local(): moved = jnp.concatenate((carry_forward[0], carry_cotangent[0]), axis=0)]
    ppermute x2, waiting for transfers between devices: 1.74 us -> 2.34 us  [onward(): return lax.ppermute(x, ('pipe', 'expert'), pairs)]
    pallas_call x3 -> x2, Pallas kernels: 2.85 us -> 2.72 us  [the longest x1 1.71 us: local(): kernel_call(functools.partial(down_kernel, groups, rows), [jax.ShapeDtype...]
  transfers between devices with their start and end apart: 15 -> 13, of which waited for: 11 -> 10; matrix products, arithmetic and copies ran while one was open for 0% -> 0% of each run, Pallas kernels for 14% -> 7%
where the time goes in v3:
time: 39.5 us; the launch traced here: 39.3 us
  waiting for transfers between devices  16.2 us (41%)
  starting transfers between devices  14.7 us (37%)
  Pallas kernels  7.61 us (19%)
  between operations  0.7 us (2%)
    ppermute x11, waiting for transfers between devices, swap(): return lax.ppermute(x, axis, [(i, i ^ bit) for i in range(peers)])  13.8 us
    ppermute x11, starting transfers between devices, swap(): return lax.ppermute(x, axis, [(i, i ^ bit) for i in range(peers)])  13.2 us
    pallas_call x1, Pallas kernels, local(): pl.pallas_call(fetch_kernel, out_shape=[pltpu.VMEM(w.shape[2:], BF16) for...  2.63 us
    ppermute x2, waiting for transfers between devices, onward(): return lax.ppermute(x, ('pipe', 'expert'), pairs)  2.34 us
    pallas_call x1, Pallas kernels, local(): kernel_call(functools.partial(down_kernel, groups, rows), [jax.ShapeDtype...  1.71 us
    ppermute x2, starting transfers between devices, onward(): return lax.ppermute(x, ('pipe', 'expert'), pairs)  1.54 us
    pallas_call x1, Pallas kernels, local(): kernel_call(functools.partial(up_kernel, groups, topk, rows), (jax.ShapeD...  1.45 us
    pallas_call x1, Pallas kernels, local(): pl.pallas_call(pack_kernel, out_shape=[jax.ShapeDtypeStruct((2 * held, wi...  1 us
  transfers between devices with their start and end apart: 13, of which 10 were waited for; matrix products, arithmetic and copies ran while one was open for 0% of the time, Pallas kernels for 7%

profile of v3, /device:TPU:0, one launch (start us, length us, event | category | flops | bytes accessed | tf_op | source)
XLA Modules:
  0.0 39.3 jit_solution(2763154404272359385)
XLA Ops:
  0.6 1.0 %shard_map.113 = (bf16[32,1792]{1,0:T(8,128)(2,1)S(1)}, bf16[16,1920]{1,0:T(8,128)(2,1)S(1)}) custom-call(bf16[16,1792]{1,0:T(8,128)(2,1)} %bitcast.21, bf16[16,1792]{1,0:T(8,128)(2,1)} %bitcast.22, bf16[16,1792]{1,0:T(8,128)(2,1)} %bitcast.23, s32[1,16]{1,0:T(1,128)} %bitcast.14, bf16[1,16]{1,0:T(2,128)(2,1)} %bitcast.16, s32[1,16]{1,0:T(1,128)} %bitcast.24, ...), custom_call_target="tpu_custom_call" | custom-call | bytes 344064 | tf_op jit(solution)/shard_map/pallas_call | solution.py:257
  1.6 3.0 %collective-permute-start.1 = (bf16[16,1920]{1,0:T(8,128)(2,1)S(1)}, bf16[16,1920]{1,0:T(8,128)(2,1)S(1)}, u32[]{:S(2)}, u32[]{:S(2)}) collective-permute-start(bf16[16,1920]{1,0:T(8,128)(2,1)S(1)} %get-tuple-element.35.refs_4_), channel_id=1, source_target_pairs={{0,8},{4,12},{8,0},{12,4},{1,9},{5,13},{9,1},{13,5},{2,10},{6,14},... | collective-permute-start | bytes 184328 | tf_op jit(solution)/shard_map/ppermute | solution.py:35
  4.7 1.5 %collective-permute-start = (bf16[32,1792]{1,0:T(8,128)(2,1)S(1)}, bf16[32,1792]{1,0:T(8,128)(2,1)S(1)}, u32[]{:S(2)}, u32[]{:S(2)}) collective-permute-start(bf16[32,1792]{1,0:T(8,128)(2,1)S(1)} %get-tuple-element.26), channel_id=1, source_target_pairs={{0,16},{4,20},{8,24},{12,28},{16,0},{20,4},{24,8},{28,12},{1,17},{... | collective-permute-start | bytes 344072 | tf_op jit(solution)/shard_map/ppermute | solution.py:46
  6.2 0.0 collective-permute-start.4
  6.2 0.0 collective-permute-start.2
  6.2 0.7 %collective-permute-done.1.refs_5_ = bf16[16,1920]{1,0:T(8,128)(2,1)S(1)} collective-permute-done((bf16[16,1920]{1,0:T(8,128)(2,1)S(1)}, bf16[16,1920]{1,0:T(8,128)(2,1)S(1)}, u32[]{:S(2)}, u32[]{:S(2)}) %collective-permute-start.1) | collective-permute-done | bytes 61472 | tf_op jit(solution)/shard_map/ppermute | solution.py:35
  6.9 0.0 collective-permute-start.3
  6.9 2.6 %shard_map.114 = (bf16[1792,512]{1,0:T(8,128)(2,1)S(1)}, bf16[1792,512]{1,0:T(8,128)(2,1)S(1)}, bf16[512,1792]{1,0:T(8,128)(2,1)S(1)}) custom-call(bf16[1792,512]{1,0:T(8,128)(2,1)} %bitcast.18, bf16[1792,512]{1,0:T(8,128)(2,1)} %bitcast.19, bf16[512,1792]{1,0:T(8,128)(2,1)} %bitcast.20), custom_call_target="tpu_custom_call" | custom-call | bytes 11010048 | tf_op jit(solution)/shard_map/pallas_call | solution.py:243
  9.5 1.0 %collective-permute-done.refs_0_.moved_ref = bf16[32,1792]{1,0:T(8,128)(2,1)S(1)} collective-permute-done((bf16[32,1792]{1,0:T(8,128)(2,1)S(1)}, bf16[32,1792]{1,0:T(8,128)(2,1)S(1)}, u32[]{:S(2)}, u32[]{:S(2)}) %collective-permute-start) | collective-permute-done | bytes 114720 | tf_op jit(solution)/shard_map/ppermute | solution.py:46
  10.5 1.3 %collective-permute-done.4.refs_1_ = bf16[32,1792]{1,0:T(8,128)(2,1)S(1)} collective-permute-done((bf16[32,1792]{1,0:T(8,128)(2,1)S(1)}, bf16[32,1792]{1,0:T(8,128)(2,1)S(1)}, u32[]{:S(2)}, u32[]{:S(2)}) %collective-permute-start.4) | collective-permute-done | bytes 114720 | tf_op jit(solution)/shard_map/ppermute | solution.py:46
  11.9 0.0 collective-permute-start.6
  11.9 0.0 collective-permute-done.2.refs_6_
  11.9 0.0 collective-permute-done.3.refs_7_
  11.9 0.5 %collective-permute-start.5 = (bf16[32,1792]{1,0:T(8,128)(2,1)S(1)}, bf16[32,1792]{1,0:T(8,128)(2,1)S(1)}, u32[]{:S(2)}, u32[]{:S(2)}) collective-permute-start(bf16[32,1792]{1,0:T(8,128)(2,1)S(1)} %collective-permute-done.refs_0_.moved_ref), channel_id=1, source_target_pairs={{0,4},{4,0},{8,12},{12,8},{1,5},{5,1},{9,13},{13,9},{2,6},{6,2},{1... | collective-permute-start | bytes 344072 | tf_op jit(solution)/shard_map/ppermute | solution.py:35
  12.4 0.8 %collective-permute-done.6.refs_3_ = bf16[32,1792]{1,0:T(8,128)(2,1)S(1)} collective-permute-done((bf16[32,1792]{1,0:T(8,128)(2,1)S(1)}, bf16[32,1792]{1,0:T(8,128)(2,1)S(1)}, u32[]{:S(2)}, u32[]{:S(2)}) %collective-permute-start.6) | collective-permute-done | bytes 114720 | tf_op jit(solution)/shard_map/ppermute | solution.py:35
  13.2 0.2 collective-permute-done.5.refs_2_
  13.3 1.4 %shard_map.115 = (bf16[120,512]{1,0:T(8,128)(2,1)S(1)}, bf16[80,512]{1,0:T(8,128)(2,1)S(1)}, bf16[40,64]{1,0:T(8,128)(2,1)S(1)}, bf16[40,64]{1,0:T(8,128)(2,1)S(1)}) custom-call(bf16[32,1792]{1,0:T(8,128)(2,1)S(1)} %collective-permute-done.refs_0_.moved_ref, bf16[32,1792]{1,0:T(8,128)(2,1)S(1)} %collective-permute-done.4.refs_1_, ...), custom_call_target="tpu_custom_call" | custom-call | flops 367001600 | bytes 5505024 | tf_op jit(solution)/shard_map/pallas_call | solution.py:282
  14.8 1.7 %collective-permute-start.7 = (bf16[120,512]{1,0:T(8,128)(2,1)S(1)}, bf16[120,512]{1,0:T(8,128)(2,1)S(1)}, u32[]{:S(2)}, u32[]{:S(2)}) collective-permute-start(bf16[120,512]{1,0:T(8,128)(2,1)S(1)} %get-tuple-element.42), channel_id=1, source_target_pairs={{0,1},{1,0},{2,3},{3,2},{4,5},{5,4},{6,7},{7,6},{8,9},{9,8},{10,11... | collective-permute-start | bytes 368648 | tf_op jit(solution)/shard_map/ppermute | solution.py:35
  16.5 2.6 %collective-permute-start.9 = (bf16[80,512]{1,0:T(8,128)(2,1)S(1)}, bf16[80,512]{1,0:T(8,128)(2,1)S(1)}, u32[]{:S(2)}, u32[]{:S(2)}) collective-permute-start(bf16[80,512]{1,0:T(8,128)(2,1)S(1)} %get-tuple-element.43), channel_id=1, source_target_pairs={{0,2},{1,3},{2,0},{3,1},{4,6},{5,7},{6,4},{7,5},{8,10},{9,11},{10,... | collective-permute-start | bytes 245768 | tf_op jit(solution)/shard_map/ppermute | solution.py:35
  19.0 3.2 %collective-permute-done.7 = bf16[120,512]{1,0:T(8,128)(2,1)S(1)} collective-permute-done((bf16[120,512]{1,0:T(8,128)(2,1)S(1)}, bf16[120,512]{1,0:T(8,128)(2,1)S(1)}, u32[]{:S(2)}, u32[]{:S(2)}) %collective-permute-start.7) | collective-permute-done | bytes 122912 | tf_op jit(solution)/shard_map/ppermute | solution.py:35
  22.2 1.5 %collective-permute-start.8 = (bf16[120,512]{1,0:T(8,128)(2,1)S(1)}, bf16[120,512]{1,0:T(8,128)(2,1)S(1)}, u32[]{:S(2)}, u32[]{:S(2)}) collective-permute-start(bf16[120,512]{1,0:T(8,128)(2,1)S(1)} %add_convert_fusion.fa_ref), channel_id=1, source_target_pairs={{0,2},{1,3},{2,0},{3,1},{4,6},{5,7},{6,4},{7,5},{8,10},{9,11},{10,... | collective-permute-start | bytes 368648 | tf_op jit(solution)/shard_map/ppermute | solution.py:35
  23.7 0.0 collective-permute-done.9
  23.7 2.5 %collective-permute-start.10 = (bf16[80,512]{1,0:T(8,128)(2,1)S(1)}, bf16[80,512]{1,0:T(8,128)(2,1)S(1)}, u32[]{:S(2)}, u32[]{:S(2)}) collective-permute-start(bf16[80,512]{1,0:T(8,128)(2,1)S(1)} %add_convert_fusion.2.ba_ref), channel_id=1, source_target_pairs={{0,1},{1,0},{2,3},{3,2},{4,5},{5,4},{6,7},{7,6},{8,9},{9,8},{10,11... | collective-permute-start | bytes 245768 | tf_op jit(solution)/shard_map/ppermute | solution.py:35
  26.2 3.1 %collective-permute-done.10.bb_ref = bf16[80,512]{1,0:T(8,128)(2,1)S(1)} collective-permute-done((bf16[80,512]{1,0:T(8,128)(2,1)S(1)}, bf16[80,512]{1,0:T(8,128)(2,1)S(1)}, u32[]{:S(2)}, u32[]{:S(2)}) %collective-permute-start.10) | collective-permute-done | bytes 81952 | tf_op jit(solution)/shard_map/ppermute | solution.py:35
  29.4 0.6 %collective-permute-done.8.fb_ref = bf16[120,512]{1,0:T(8,128)(2,1)S(1)} collective-permute-done((bf16[120,512]{1,0:T(8,128)(2,1)S(1)}, bf16[120,512]{1,0:T(8,128)(2,1)S(1)}, u32[]{:S(2)}, u32[]{:S(2)}) %collective-permute-start.8) | collective-permute-done | bytes 122912 | tf_op jit(solution)/shard_map/ppermute | solution.py:35
  29.9 1.7 %shard_map.116 = (bf16[2,32,1792]{2,1,0:T(8,128)(2,1)S(1)}, bf16[2,32,1792]{2,1,0:T(8,128)(2,1)S(1)}) custom-call(bf16[120,512]{1,0:T(8,128)(2,1)S(1)} %add_convert_fusion.fa_ref, bf16[120,512]{1,0:T(8,128)(2,1)S(1)} %collective-permute-done.8.fb_ref, bf16[80,512]{1,0:T(8,128)(2,1)S(1)} %add_convert_fusion.2.ba_ref, ...), custom_call_target="tpu_custom_call" | custom-call | flops 220200960 | bytes 5505024 | tf_op jit(solution)/shard_map/pallas_call | solution.py:302
  31.6 0.1 collective-permute-start.11
  31.7 1.5 %collective-permute-done.11.other_ref = bf16[2,32,1792]{2,1,0:T(8,128)(2,1)S(1)} collective-permute-done((bf16[2,32,1792]{2,1,0:T(8,128)(2,1)S(1)}, bf16[2,32,1792]{2,1,0:T(8,128)(2,1)S(1)}, u32[]{:S(2)}, u32[]{:S(2)}) %collective-permute-start.11) | collective-permute-done | bytes 229408 | tf_op jit(solution)/shard_map/ppermute | solution.py:35
  33.2 1.4 %collective-permute-start.12 = (bf16[32,1792]{1,0:T(8,128)(2,1)S(1)}, bf16[32,1792]{1,0:T(8,128)(2,1)S(1)}, u32[]{:S(2)}, u32[]{:S(2)}) collective-permute-start(bf16[32,1792]{1,0:T(8,128)(2,1)S(1)} %fusion), channel_id=1, source_target_pairs={{0,8},{4,12},{8,0},{12,4},{1,9},{5,13},{9,1},{13,5},{2,10},{6,14},... | collective-permute-start | bytes 344072 | tf_op jit(solution)/shard_map/ppermute | solution.py:35
  34.6 3.9 %collective-permute-done.12.refs_0_ = bf16[32,1792]{1,0:T(8,128)(2,1)S(1)} collective-permute-done((bf16[32,1792]{1,0:T(8,128)(2,1)S(1)}, bf16[32,1792]{1,0:T(8,128)(2,1)S(1)}, u32[]{:S(2)}, u32[]{:S(2)}) %collective-permute-start.12) | collective-permute-done | bytes 114720 | tf_op jit(solution)/shard_map/ppermute | solution.py:35
  38.5 0.0 copy-done
  38.5 0.8 %shard_map.117 = (bf16[16,1792]{1,0:T(8,128)(2,1)}, bf16[16,1792]{1,0:T(8,128)(2,1)}) custom-call(bf16[32,1792]{1,0:T(8,128)(2,1)S(1)} %collective-permute-done.refs_0_.moved_ref, s32[1,16]{1,0:T(1,128)S(1)} %bitcast.15, bf16[1,16]{1,0:T(2,128)(2,1)S(1)} %bitcast.17, bf16[2,32,1792]{2,1,0:T(8,128)(2,1)S(1)} %get-tuple-element.46.own_ref, ...), custom_call_target="tpu_custom_call" | custom-call | bytes 573440 | tf_op jit(solution)/shard_map/pallas_call | solution.py:313
  (6 shorter events, 0.1 us)
Async XLA Ops:
  1.6 5.2 %collective-permute-start.1 = (bf16[16,1920]{1,0:T(8,128)(2,1)S(1)}, bf16[16,1920]{1,0:T(8,128)(2,1)S(1)}, u32[]{:S(2)}, u32[]{:S(2)}) collective-permute-start(bf16[16,1920]{1,0:T(8,128)(2,1)S(1)} %get-tuple-element.35.refs_4_), channel_id=1, source_target_pairs={{0,8},{4,12},{8,0},{12,4},{1,9},{5,13},{9,1},{13,5},{2,10},{6,14},... | collective-permute-start | bytes 184328 | tf_op jit(solution)/shard_map/ppermute | solution.py:35
  4.7 5.8 %collective-permute-start = (bf16[32,1792]{1,0:T(8,128)(2,1)S(1)}, bf16[32,1792]{1,0:T(8,128)(2,1)S(1)}, u32[]{:S(2)}, u32[]{:S(2)}) collective-permute-start(bf16[32,1792]{1,0:T(8,128)(2,1)S(1)} %get-tuple-element.26), channel_id=1, source_target_pairs={{0,16},{4,20},{8,24},{12,28},{16,0},{20,4},{24,8},{28,12},{1,17},{... | collective-permute-start | bytes 344072 | tf_op jit(solution)/shard_map/ppermute | solution.py:46
  6.2 5.7 %collective-permute-start.4 = (bf16[32,1792]{1,0:T(8,128)(2,1)S(1)}, bf16[32,1792]{1,0:T(8,128)(2,1)S(1)}, u32[]{:S(2)}, u32[]{:S(2)}) collective-permute-start(bf16[32,1792]{1,0:T(8,128)(2,1)S(1)} %get-tuple-element.26), channel_id=1, source_target_pairs={{0,24},{4,28},{8,16},{12,20},{16,8},{20,12},{24,0},{28,4},{1,25},{... | collective-permute-start | bytes 344072 | tf_op jit(solution)/shard_map/ppermute | solution.py:46
  6.2 5.6 %collective-permute-start.2 = (bf16[16,1920]{1,0:T(8,128)(2,1)S(1)}, bf16[16,1920]{1,0:T(8,128)(2,1)S(1)}, u32[]{:S(2)}, u32[]{:S(2)}) collective-permute-start(bf16[16,1920]{1,0:T(8,128)(2,1)S(1)} %get-tuple-element.35.refs_4_), channel_id=1, source_target_pairs={{0,4},{4,0},{8,12},{12,8},{1,5},{5,1},{9,13},{13,9},{2,6},{6,2},{1... | collective-permute-start | bytes 184328 | tf_op jit(solution)/shard_map/ppermute | solution.py:35
  6.9 5.0 %collective-permute-start.3 = (bf16[16,1920]{1,0:T(8,128)(2,1)S(1)}, bf16[16,1920]{1,0:T(8,128)(2,1)S(1)}, u32[]{:S(2)}, u32[]{:S(2)}) collective-permute-start(bf16[16,1920]{1,0:T(8,128)(2,1)S(1)} %collective-permute-done.1.refs_5_), channel_id=1, source_target_pairs={{0,4},{4,0},{8,12},{12,8},{1,5},{5,1},{9,13},{13,9},{2,6},{6,2},{1... | collective-permute-start | bytes 184328 | tf_op jit(solution)/shard_map/ppermute | solution.py:35
  11.9 1.3 %collective-permute-start.6 = (bf16[32,1792]{1,0:T(8,128)(2,1)S(1)}, bf16[32,1792]{1,0:T(8,128)(2,1)S(1)}, u32[]{:S(2)}, u32[]{:S(2)}) collective-permute-start(bf16[32,1792]{1,0:T(8,128)(2,1)S(1)} %collective-permute-done.4.refs_1_), channel_id=1, source_target_pairs={{0,4},{4,0},{8,12},{12,8},{1,5},{5,1},{9,13},{13,9},{2,6},{6,2},{1... | collective-permute-start | bytes 344072 | tf_op jit(solution)/shard_map/ppermute | solution.py:35
  11.9 1.5 %collective-permute-start.5 = (bf16[32,1792]{1,0:T(8,128)(2,1)S(1)}, bf16[32,1792]{1,0:T(8,128)(2,1)S(1)}, u32[]{:S(2)}, u32[]{:S(2)}) collective-permute-start(bf16[32,1792]{1,0:T(8,128)(2,1)S(1)} %collective-permute-done.refs_0_.moved_ref), channel_id=1, source_target_pairs={{0,4},{4,0},{8,12},{12,8},{1,5},{5,1},{9,13},{13,9},{2,6},{6,2},{1... | collective-permute-start | bytes 344072 | tf_op jit(solution)/shard_map/ppermute | solution.py:35
  14.8 7.4 %collective-permute-start.7 = (bf16[120,512]{1,0:T(8,128)(2,1)S(1)}, bf16[120,512]{1,0:T(8,128)(2,1)S(1)}, u32[]{:S(2)}, u32[]{:S(2)}) collective-permute-start(bf16[120,512]{1,0:T(8,128)(2,1)S(1)} %get-tuple-element.42), channel_id=1, source_target_pairs={{0,1},{1,0},{2,3},{3,2},{4,5},{5,4},{6,7},{7,6},{8,9},{9,8},{10,11... | collective-permute-start | bytes 368648 | tf_op jit(solution)/shard_map/ppermute | solution.py:35
  16.5 7.3 %collective-permute-start.9 = (bf16[80,512]{1,0:T(8,128)(2,1)S(1)}, bf16[80,512]{1,0:T(8,128)(2,1)S(1)}, u32[]{:S(2)}, u32[]{:S(2)}) collective-permute-start(bf16[80,512]{1,0:T(8,128)(2,1)S(1)} %get-tuple-element.43), channel_id=1, source_target_pairs={{0,2},{1,3},{2,0},{3,1},{4,6},{5,7},{6,4},{7,5},{8,10},{9,11},{10,... | collective-permute-start | bytes 245768 | tf_op jit(solution)/shard_map/ppermute | solution.py:35
  22.2 7.7 %collective-permute-start.8 = (bf16[120,512]{1,0:T(8,128)(2,1)S(1)}, bf16[120,512]{1,0:T(8,128)(2,1)S(1)}, u32[]{:S(2)}, u32[]{:S(2)}) collective-permute-start(bf16[120,512]{1,0:T(8,128)(2,1)S(1)} %add_convert_fusion.fa_ref), channel_id=1, source_target_pairs={{0,2},{1,3},{2,0},{3,1},{4,6},{5,7},{6,4},{7,5},{8,10},{9,11},{10,... | collective-permute-start | bytes 368648 | tf_op jit(solution)/shard_map/ppermute | solution.py:35
  23.7 5.6 %collective-permute-start.10 = (bf16[80,512]{1,0:T(8,128)(2,1)S(1)}, bf16[80,512]{1,0:T(8,128)(2,1)S(1)}, u32[]{:S(2)}, u32[]{:S(2)}) collective-permute-start(bf16[80,512]{1,0:T(8,128)(2,1)S(1)} %add_convert_fusion.2.ba_ref), channel_id=1, source_target_pairs={{0,1},{1,0},{2,3},{3,2},{4,5},{5,4},{6,7},{7,6},{8,9},{9,8},{10,11... | collective-permute-start | bytes 245768 | tf_op jit(solution)/shard_map/ppermute | solution.py:35
  29.9 8.6 %copy-start = (s32[1,16,1]{1,2,0:T(1,128)S(1)}, s32[1,16,1]{1,2,0:T(1,128)}, u32[]{:S(2)}) copy-start(s32[1,16,1]{1,2,0:T(1,128)} %param.13) | copy-start | bytes 196
  29.9 8.6 %copy-start.1 = (bf16[1,16,1]{1,2,0:T(2,128)(2,1)S(1)}, bf16[1,16,1]{1,2,0:T(2,128)(2,1)}, u32[]{:S(2)}) copy-start(bf16[1,16,1]{1,2,0:T(2,128)(2,1)} %param.14) | copy-start | bytes 100
  31.6 1.6 %collective-permute-start.11 = (bf16[2,32,1792]{2,1,0:T(8,128)(2,1)S(1)}, bf16[2,32,1792]{2,1,0:T(8,128)(2,1)S(1)}, u32[]{:S(2)}, u32[]{:S(2)}) collective-permute-start(bf16[2,32,1792]{2,1,0:T(8,128)(2,1)S(1)} %get-tuple-element.47), channel_id=1, source_target_pairs={{0,4},{4,0},{8,12},{12,8},{1,5},{5,1},{9,13},{13,9},{2,6},{6,2},{1... | collective-permute-start | bytes 688136 | tf_op jit(solution)/shard_map/ppermute | solution.py:35
  33.2 5.3 %collective-permute-start.12 = (bf16[32,1792]{1,0:T(8,128)(2,1)S(1)}, bf16[32,1792]{1,0:T(8,128)(2,1)S(1)}, u32[]{:S(2)}, u32[]{:S(2)}) collective-permute-start(bf16[32,1792]{1,0:T(8,128)(2,1)S(1)} %fusion), channel_id=1, source_target_pairs={{0,8},{4,12},{8,0},{12,4},{1,9},{5,13},{9,1},{13,5},{2,10},{6,14},... | collective-permute-start | bytes 344072 | tf_op jit(solution)/shard_map/ppermute | solution.py:35

commit v4 on v3

--- a/solution.py
+++ b/solution.py
@@ -105,7 +105,7 @@
     return notes[:, : len(saved) * held]
 
 
-def places(notes, first, topk, expert, rows):
+def places(notes, first, topk, expert, rows, base=0):
     tokens = notes.shape[1]
     hit = (notes[first : first + topk] == expert).astype(F32)
     named = jnp.sum(hit, axis=0, keepdims=True)
@@ -119,11 +119,43 @@
         preferred_element_type=F32,
     )[:1]
     row = lax.broadcasted_iota(jnp.int32, (rows, tokens), 0).astype(F32)
-    place = jnp.where((row == rank) & (named > 0.0), 1.0, 0.0)
-    return place, place * weight
-
-
-def up_kernel(groups, topk, rows, *refs):
+    place = jnp.where((row == rank + base) & (named > 0.0), 1.0, 0.0)
+    return place, place * weight, named
+
+
+def slots(named_f, named_b, held, capacity, slot_rows, rows):
+    tokens = named_f.shape[1]
+    total = tokens // held * slot_rows
+    block = lax.broadcasted_iota(jnp.int32, (total, tokens), 0) // slot_rows
+    before = lax.broadcasted_iota(jnp.int32, (total, tokens), 1) < block * held
+    offset_f = jnp.sum(jnp.where(before, named_f, 0.0), axis=1, keepdims=True)
+    offset_b = jnp.sum(jnp.where(before, named_b, 0.0), axis=1, keepdims=True)
+    slot = lax.broadcasted_iota(jnp.int32, (total, 2 * rows), 0) % slot_rows
+    row = lax.broadcasted_iota(jnp.int32, (total, 2 * rows), 1)
+    slot_value, row_value = slot.astype(F32), row.astype(F32)
+    taken_f = (slot < capacity) & (row < rows) & (row_value == offset_f + slot_value)
+    taken_b = (
+        (slot >= capacity)
+        & (slot < 2 * capacity)
+        & (row_value == offset_b + slot_value + float(rows - capacity))
+    )
+    return jnp.where(taken_f | taken_b, 1.0, 0.0)
+
+
+def home_kernel(topk, capacity, rf_ref, gf_ref, rb_ref, gb_ref, home_ref):
+    notes = jnp.concatenate(
+        [r[...].astype(F32) for r in (rf_ref, gf_ref, rb_ref, gb_ref)], axis=0
+    )
+    groups, _, slot_rows = home_ref.shape
+    mine = lax.axis_index("expert") // 2
+    for d in range(groups):
+        expert = (mine ^ d).astype(F32)
+        _, weighed, _ = places(notes, 0, topk, expert, slot_rows)
+        placed, _, _ = places(notes, 2 * topk, topk, expert, slot_rows, capacity)
+        home_ref[d] = jnp.concatenate([weighed, placed], axis=1).T.astype(BF16)
+
+
+def up_kernel(groups, topk, rows, capacity, slot_rows, *refs):
     moved = refs[: 2 * groups]
     saved = refs[2 * groups : 4 * groups]
     (
@@ -132,17 +164,15 @@
         w_d_ref,
         part_f_ref,
         part_b_ref,
-        place_f_ref,
-        place_b_ref,
+        slot_ref,
     ) = refs[4 * groups :]
     held = moved[0].shape[0] // 2
     width = moved[0].shape[1]
     expert = (lax.axis_index("expert") // 2).astype(F32)
     notes = unpack(saved, width, held, topk)
-    place_f, _ = places(notes, 0, topk, expert, rows)
-    place_b, weigh_b = places(notes, 2 * topk, topk, expert, rows)
-    place_f_ref[...] = place_f.astype(BF16)
-    place_b_ref[...] = place_b.astype(BF16)
+    place_f, _, named_f = places(notes, 0, topk, expert, rows)
+    place_b, weigh_b, named_b = places(notes, 2 * topk, topk, expert, rows)
+    slot_ref[...] = slots(named_f, named_b, held, capacity, slot_rows, rows).astype(BF16)
     x_f = jnp.concatenate([r[:held, :] for r in moved], axis=0)
     c_b = jnp.concatenate([r[held:, :] for r in moved], axis=0)
     x_b = jnp.concatenate([r[:, :width] for r in saved], axis=0)
@@ -164,8 +194,7 @@
     fb_ref,
     ba_ref,
     bb_ref,
-    place_f_ref,
-    place_b_ref,
+    slot_ref,
     w_g_ref,
     w_u_ref,
     w_d_ref,
@@ -182,40 +211,27 @@
     dgate = (dhid * upper_b * slope).astype(BF16)
     dupper = (dhid * (gate_b * sigma)).astype(BF16)
     turned = (((1,), (1,)), ((), ()))
-    out_f = jnp.dot(hidden, w_d_ref[...], preferred_element_type=F32).astype(BF16)
+    out_f = jnp.dot(hidden, w_d_ref[...], preferred_element_type=F32)
     grad = lax.dot_general(dgate, w_g_ref[...], turned, preferred_element_type=F32)
     grad = grad + lax.dot_general(dupper, w_u_ref[...], turned, preferred_element_type=F32)
-    grad = grad.astype(BF16)
-    back = (((0,), (0,)), ((), ()))
-    full_f = lax.dot_general(place_f_ref[...], out_f, back, preferred_element_type=F32).astype(BF16)
-    full_b = lax.dot_general(place_b_ref[...], grad, back, preferred_element_type=F32).astype(BF16)
-    held = own_ref.shape[1] // 2
+    both = jnp.concatenate([out_f, grad], axis=0).astype(BF16)
+    full = jnp.dot(slot_ref[...], both, preferred_element_type=F32)
+    slot_rows = own_ref.shape[1]
     for d in range(groups):
-        for ref, at in ((own_ref, d * held), (other_ref, (groups + d) * held)):
-            ref[d, :held, :] = full_f[at : at + held]
-            ref[d, held:, :] = full_b[at : at + held]
-
-
-def final_kernel(groups, moved_ref, rf_ref, gf_ref, own_ref, other_ref, *refs):
+        for ref, block in ((own_ref, d), (other_ref, groups + d)):
+            ref[d] = full[block * slot_rows : (block + 1) * slot_rows].astype(BF16)
+
+
+def final_kernel(groups, moved_ref, home_ref, own_ref, other_ref, *refs):
     came = refs[: groups - 1]
     out_f_ref, out_b_ref = refs[groups - 1 :]
     held = out_f_ref.shape[0]
-    mine = lax.axis_index("expert") // 2
-    routes_f = rf_ref[...]
-    gates_f = gf_ref[...].astype(F32)
-    same = lax.broadcasted_iota(jnp.int32, (held, held), 0) == lax.broadcasted_iota(
-        jnp.int32, (held, held), 1
-    )
-    result_f = moved_ref[:held, :].astype(F32)
-    result_b = moved_ref[held:, :].astype(F32)
+    result = moved_ref[...].astype(F32)
     for d in range(groups):
-        weight = jnp.sum(jnp.where(routes_f == (mine ^ d), gates_f, 0.0), axis=0, keepdims=True)
-        weigh = jnp.where(same, weight, 0.0).astype(BF16)
-        for ref in (own_ref.at[0], other_ref.at[0]) if d == 0 else (came[d - 1],):
-            result_f = result_f + jnp.dot(weigh, ref[:held, :], preferred_element_type=F32)
-            result_b = result_b + ref[held:, :].astype(F32)
-    out_f_ref[...] = result_f.astype(BF16)
-    out_b_ref[...] = result_b.astype(BF16)
+        for part in (own_ref[0], other_ref[0]) if d == 0 else (came[d - 1][...],):
+            result = result + jnp.dot(home_ref[d], part, preferred_element_type=F32)
+    out_f_ref[...] = result[:held].astype(BF16)
+    out_b_ref[...] = result[held:].astype(BF16)
 
 
 def local(
@@ -238,7 +254,7 @@
     topk = routes_forward.shape[2]
     capacity = min(held, max(6, held * topk // experts + 2))
     rows = -(-peers * capacity // 8) * 8
-    tokens = peers * held
+    slot_rows = -(-2 * capacity // 8) * 8
     weight_bytes = 6 * width * hidden
     w_g, w_u, w_d = pl.pallas_call(
         fetch_kernel,
@@ -279,13 +295,12 @@
     w_g, w_u, w_d = in_vmem(w_g), in_vmem(w_u), in_vmem(w_d)
     moved_all[0], *saved_all = lax.optimization_barrier((moved_all[0], *saved_all))
     moved_all = moved_all + [swap(x, "expert", 1) for x in moved_all]
-    part_f, part_b, place_f, place_b = kernel_call(
-        functools.partial(up_kernel, groups, topk, rows),
+    part_f, part_b, slot = kernel_call(
+        functools.partial(up_kernel, groups, topk, rows, capacity, slot_rows),
         (
             jax.ShapeDtypeStruct((3 * rows, hidden), BF16),
             jax.ShapeDtypeStruct((2 * rows, hidden), BF16),
-            jax.ShapeDtypeStruct((rows, tokens), BF16),
-            jax.ShapeDtypeStruct((rows, tokens), BF16),
+            jax.ShapeDtypeStruct((peers * slot_rows, 2 * rows), BF16),
         ),
         10 * rows * width * hidden,
         weight_bytes,
@@ -301,15 +316,23 @@
         part_b = (part_b.astype(F32) + came_b.astype(F32)).astype(BF16)
     own, other = kernel_call(
         functools.partial(down_kernel, groups, rows),
-        [jax.ShapeDtypeStruct((groups, 2 * held, width), BF16)] * 2,
+        [jax.ShapeDtypeStruct((groups, slot_rows, width), BF16)] * 2,
         6 * rows * width * hidden,
         weight_bytes,
-    )(part_f, came_f, part_b, came_b, place_f, place_b, w_g, w_u, w_d)
+    )(part_f, came_f, part_b, came_b, slot, w_g, w_u, w_d)
     other = swap(other, "expert", 1)
     came = []
     for d in range(1, groups):
         halves = (own[d].astype(F32) + other[d].astype(F32)).astype(BF16)
         came.append(swap(halves, "expert", 2 * d))
+    noted = (routes_f, gates_f, routes_b, gates_b)
+    *noted, _ = lax.optimization_barrier((*noted, slot))
+    home = kernel_call(
+        functools.partial(home_kernel, topk, capacity),
+        jax.ShapeDtypeStruct((groups, 2 * held, slot_rows), BF16),
+        0,
+        8 * groups * slot_rows * held,
+    )(*noted)
     result_f, result_b = kernel_call(
         functools.partial(final_kernel, groups),
         (
@@ -318,7 +341,7 @@
         ),
         0,
         20 * held * width,
-    )(moved_all[0], routes_f, gates_f, own, other, *came)
+    )(moved_all[0], home, own, other, *came)
     return (result_f[None], result_b[None])
 
 

time: 39.5 us -> 38.8 us (0.982)
  waiting for transfers between devices: 16.2 us -> 15.2 us
    ppermute x11, waiting for transfers between devices: 13.8 us -> 12.8 us  [swap(): return lax.ppermute(x, axis, [(i, i ^ bit) for i in range(peers)])]
    pallas_call x1 -> x2, Pallas kernels: 1.45 us -> 1.72 us  [the longest x1 1.44 us: local(): kernel_call(functools.partial(up_kernel, groups, topk, rows, capacity, sl...]
  transfers between devices with their start and end apart: 13 -> 13, of which waited for: 10 -> 10; matrix products, arithmetic and copies ran while one was open for 0% -> 0% of each run, Pallas kernels for 7% -> 8%
where the time goes in v4:
time: 38.8 us; the launch traced here: 38.7 us
  waiting for transfers between devices  15.2 us (39%)
  starting transfers between devices  14.7 us (38%)
  Pallas kernels  7.97 us (21%)
  between operations  0.7 us (2%)
    ppermute x11, starting transfers between devices, swap(): return lax.ppermute(x, axis, [(i, i ^ bit) for i in range(peers)])  13.2 us
    ppermute x11, waiting for transfers between devices, swap(): return lax.ppermute(x, axis, [(i, i ^ bit) for i in range(peers)])  12.8 us
    pallas_call x1, Pallas kernels, local(): pl.pallas_call(fetch_kernel, out_shape=[pltpu.VMEM(w.shape[2:], BF16) for...  2.63 us
    ppermute x2, waiting for transfers between devices, onward(): return lax.ppermute(x, ('pipe', 'expert'), pairs)  2.34 us
    pallas_call x1, Pallas kernels, local(): kernel_call(functools.partial(down_kernel, groups, rows), [jax.ShapeDtype...  1.74 us
    ppermute x2, starting transfers between devices, onward(): return lax.ppermute(x, ('pipe', 'expert'), pairs)  1.54 us
    pallas_call x1, Pallas kernels, local(): kernel_call(functools.partial(up_kernel, groups, topk, rows, capacity, sl...  1.44 us
    pallas_call x1, Pallas kernels, local(): pl.pallas_call(pack_kernel, out_shape=[jax.ShapeDtypeStruct((2 * held, wi...  1 us
  transfers between devices with their start and end apart: 13, of which 10 were waited for; matrix products, arithmetic and copies ran while one was open for 0% of the time, Pallas kernels for 8%

profile of v4, /device:TPU:0, one launch (start us, length us, event | category | flops | bytes accessed | tf_op | source)
XLA Modules:
  0.0 38.7 jit_solution(1106724106208470678)
XLA Ops:
  0.6 1.0 %shard_map.113 = (bf16[32,1792]{1,0:T(8,128)(2,1)S(1)}, bf16[16,1920]{1,0:T(8,128)(2,1)S(1)}) custom-call(bf16[16,1792]{1,0:T(8,128)(2,1)} %bitcast.25, bf16[16,1792]{1,0:T(8,128)(2,1)} %bitcast.26, bf16[16,1792]{1,0:T(8,128)(2,1)} %bitcast.27, s32[1,16]{1,0:T(1,128)} %bitcast.14, bf16[1,16]{1,0:T(2,128)(2,1)} %bitcast.16, s32[1,16]{1,0:T(1,128)} %bitcast.18, ...), custom_call_target="tpu_custom_call" | custom-call | bytes 344064 | tf_op jit(solution)/shard_map/pallas_call | solution.py:273
  1.6 3.0 %collective-permute-start.1 = (bf16[16,1920]{1,0:T(8,128)(2,1)S(1)}, bf16[16,1920]{1,0:T(8,128)(2,1)S(1)}, u32[]{:S(2)}, u32[]{:S(2)}) collective-permute-start(bf16[16,1920]{1,0:T(8,128)(2,1)S(1)} %get-tuple-element.38.refs_4_), channel_id=1, source_target_pairs={{0,8},{4,12},{8,0},{12,4},{1,9},{5,13},{9,1},{13,5},{2,10},{6,14},... | collective-permute-start | bytes 184328 | tf_op jit(solution)/shard_map/ppermute | solution.py:35
  4.7 1.5 %collective-permute-start = (bf16[32,1792]{1,0:T(8,128)(2,1)S(1)}, bf16[32,1792]{1,0:T(8,128)(2,1)S(1)}, u32[]{:S(2)}, u32[]{:S(2)}) collective-permute-start(bf16[32,1792]{1,0:T(8,128)(2,1)S(1)} %get-tuple-element.29), channel_id=1, source_target_pairs={{0,16},{4,20},{8,24},{12,28},{16,0},{20,4},{24,8},{28,12},{1,17},{... | collective-permute-start | bytes 344072 | tf_op jit(solution)/shard_map/ppermute | solution.py:46
  6.2 0.0 collective-permute-start.4
  6.2 0.0 collective-permute-start.2
  6.2 0.7 %collective-permute-done.1.refs_5_ = bf16[16,1920]{1,0:T(8,128)(2,1)S(1)} collective-permute-done((bf16[16,1920]{1,0:T(8,128)(2,1)S(1)}, bf16[16,1920]{1,0:T(8,128)(2,1)S(1)}, u32[]{:S(2)}, u32[]{:S(2)}) %collective-permute-start.1) | collective-permute-done | bytes 61472 | tf_op jit(solution)/shard_map/ppermute | solution.py:35
  6.9 0.0 collective-permute-start.3
  6.9 2.6 %shard_map.114 = (bf16[1792,512]{1,0:T(8,128)(2,1)S(1)}, bf16[1792,512]{1,0:T(8,128)(2,1)S(1)}, bf16[512,1792]{1,0:T(8,128)(2,1)S(1)}) custom-call(bf16[1792,512]{1,0:T(8,128)(2,1)} %bitcast.22, bf16[1792,512]{1,0:T(8,128)(2,1)} %bitcast.23, bf16[512,1792]{1,0:T(8,128)(2,1)} %bitcast.24), custom_call_target="tpu_custom_call" | custom-call | bytes 11010048 | tf_op jit(solution)/shard_map/pallas_call | solution.py:259
  9.5 1.0 %collective-permute-done.refs_0_.moved_ref = bf16[32,1792]{1,0:T(8,128)(2,1)S(1)} collective-permute-done((bf16[32,1792]{1,0:T(8,128)(2,1)S(1)}, bf16[32,1792]{1,0:T(8,128)(2,1)S(1)}, u32[]{:S(2)}, u32[]{:S(2)}) %collective-permute-start) | collective-permute-done | bytes 114720 | tf_op jit(solution)/shard_map/ppermute | solution.py:46
  10.5 1.3 %collective-permute-done.4.refs_1_ = bf16[32,1792]{1,0:T(8,128)(2,1)S(1)} collective-permute-done((bf16[32,1792]{1,0:T(8,128)(2,1)S(1)}, bf16[32,1792]{1,0:T(8,128)(2,1)S(1)}, u32[]{:S(2)}, u32[]{:S(2)}) %collective-permute-start.4) | collective-permute-done | bytes 114720 | tf_op jit(solution)/shard_map/ppermute | solution.py:46
  11.9 0.0 collective-permute-start.6
  11.9 0.0 collective-permute-done.2.refs_6_
  11.9 0.0 collective-permute-done.3.refs_7_
  11.9 0.5 %collective-permute-start.5 = (bf16[32,1792]{1,0:T(8,128)(2,1)S(1)}, bf16[32,1792]{1,0:T(8,128)(2,1)S(1)}, u32[]{:S(2)}, u32[]{:S(2)}) collective-permute-start(bf16[32,1792]{1,0:T(8,128)(2,1)S(1)} %collective-permute-done.refs_0_.moved_ref), channel_id=1, source_target_pairs={{0,4},{4,0},{8,12},{12,8},{1,5},{5,1},{9,13},{13,9},{2,6},{6,2},{1... | collective-permute-start | bytes 344072 | tf_op jit(solution)/shard_map/ppermute | solution.py:35
  12.4 0.8 %collective-permute-done.6.refs_3_ = bf16[32,1792]{1,0:T(8,128)(2,1)S(1)} collective-permute-done((bf16[32,1792]{1,0:T(8,128)(2,1)S(1)}, bf16[32,1792]{1,0:T(8,128)(2,1)S(1)}, u32[]{:S(2)}, u32[]{:S(2)}) %collective-permute-start.6) | collective-permute-done | bytes 114720 | tf_op jit(solution)/shard_map/ppermute | solution.py:35
  13.2 0.2 collective-permute-done.5.refs_2_
  13.3 1.4 %shard_map.115 = (bf16[120,512]{1,0:T(8,128)(2,1)S(1)}, bf16[80,512]{1,0:T(8,128)(2,1)S(1)}, bf16[96,80]{1,0:T(8,128)(2,1)S(1)}) custom-call(bf16[32,1792]{1,0:T(8,128)(2,1)S(1)} %collective-permute-done.refs_0_.moved_ref, bf16[32,1792]{1,0:T(8,128)(2,1)S(1)} %collective-permute-done.4.refs_1_, bf16[32,1792]{1,0:T(8,128)(2,1)S(1)} %collective-permute-done.5.refs_2_, ...), custom_call_target="tpu_custom_call" | custom-call | flops 367001600 | bytes 5505024 | tf_op jit(solution)/shard_map/pallas_call | solution.py:298
  14.8 1.7 %collective-permute-start.7 = (bf16[120,512]{1,0:T(8,128)(2,1)S(1)}, bf16[120,512]{1,0:T(8,128)(2,1)S(1)}, u32[]{:S(2)}, u32[]{:S(2)}) collective-permute-start(bf16[120,512]{1,0:T(8,128)(2,1)S(1)} %get-tuple-element.50), channel_id=1, source_target_pairs={{0,1},{1,0},{2,3},{3,2},{4,5},{5,4},{6,7},{7,6},{8,9},{9,8},{10,11... | collective-permute-start | bytes 368648 | tf_op jit(solution)/shard_map/ppermute | solution.py:35
  16.4 2.6 %collective-permute-start.9 = (bf16[80,512]{1,0:T(8,128)(2,1)S(1)}, bf16[80,512]{1,0:T(8,128)(2,1)S(1)}, u32[]{:S(2)}, u32[]{:S(2)}) collective-permute-start(bf16[80,512]{1,0:T(8,128)(2,1)S(1)} %get-tuple-element.51), channel_id=1, source_target_pairs={{0,2},{1,3},{2,0},{3,1},{4,6},{5,7},{6,4},{7,5},{8,10},{9,11},{10,... | collective-permute-start | bytes 245768 | tf_op jit(solution)/shard_map/ppermute | solution.py:35
  19.0 3.2 %collective-permute-done.7 = bf16[120,512]{1,0:T(8,128)(2,1)S(1)} collective-permute-done((bf16[120,512]{1,0:T(8,128)(2,1)S(1)}, bf16[120,512]{1,0:T(8,128)(2,1)S(1)}, u32[]{:S(2)}, u32[]{:S(2)}) %collective-permute-start.7) | collective-permute-done | bytes 122912 | tf_op jit(solution)/shard_map/ppermute | solution.py:35
  22.2 1.5 %collective-permute-start.8 = (bf16[120,512]{1,0:T(8,128)(2,1)S(1)}, bf16[120,512]{1,0:T(8,128)(2,1)S(1)}, u32[]{:S(2)}, u32[]{:S(2)}) collective-permute-start(bf16[120,512]{1,0:T(8,128)(2,1)S(1)} %add_convert_fusion.fa_ref), channel_id=1, source_target_pairs={{0,2},{1,3},{2,0},{3,1},{4,6},{5,7},{6,4},{7,5},{8,10},{9,11},{10,... | collective-permute-start | bytes 368648 | tf_op jit(solution)/shard_map/ppermute | solution.py:35
  23.7 0.0 collective-permute-done.9
  23.7 2.5 %collective-permute-start.10 = (bf16[80,512]{1,0:T(8,128)(2,1)S(1)}, bf16[80,512]{1,0:T(8,128)(2,1)S(1)}, u32[]{:S(2)}, u32[]{:S(2)}) collective-permute-start(bf16[80,512]{1,0:T(8,128)(2,1)S(1)} %add_convert_fusion.2.ba_ref), channel_id=1, source_target_pairs={{0,1},{1,0},{2,3},{3,2},{4,5},{5,4},{6,7},{7,6},{8,9},{9,8},{10,11... | collective-permute-start | bytes 245768 | tf_op jit(solution)/shard_map/ppermute | solution.py:35
  26.2 3.1 %collective-permute-done.10.bb_ref = bf16[80,512]{1,0:T(8,128)(2,1)S(1)} collective-permute-done((bf16[80,512]{1,0:T(8,128)(2,1)S(1)}, bf16[80,512]{1,0:T(8,128)(2,1)S(1)}, u32[]{:S(2)}, u32[]{:S(2)}) %collective-permute-start.10) | collective-permute-done | bytes 81952 | tf_op jit(solution)/shard_map/ppermute | solution.py:35
  29.3 0.6 %collective-permute-done.8.fb_ref = bf16[120,512]{1,0:T(8,128)(2,1)S(1)} collective-permute-done((bf16[120,512]{1,0:T(8,128)(2,1)S(1)}, bf16[120,512]{1,0:T(8,128)(2,1)S(1)}, u32[]{:S(2)}, u32[]{:S(2)}) %collective-permute-start.8) | collective-permute-done | bytes 122912 | tf_op jit(solution)/shard_map/ppermute | solution.py:35
  29.9 1.7 %shard_map.117 = (bf16[2,24,1792]{2,1,0:T(8,128)(2,1)S(1)}, bf16[2,24,1792]{2,1,0:T(8,128)(2,1)S(1)}) custom-call(bf16[120,512]{1,0:T(8,128)(2,1)S(1)} %add_convert_fusion.fa_ref, bf16[120,512]{1,0:T(8,128)(2,1)S(1)} %collective-permute-done.8.fb_ref, bf16[80,512]{1,0:T(8,128)(2,1)S(1)} %add_convert_fusion.2.ba_ref, ...), custom_call_target="tpu_custom_call" | custom-call | flops 220200960 | bytes 5505024 | tf_op jit(solution)/shard_map/pallas_call | solution.py:317
  31.7 0.1 collective-permute-start.11
  31.7 1.4 %collective-permute-done.11.other_ref = bf16[2,24,1792]{2,1,0:T(8,128)(2,1)S(1)} collective-permute-done((bf16[2,24,1792]{2,1,0:T(8,128)(2,1)S(1)}, bf16[2,24,1792]{2,1,0:T(8,128)(2,1)S(1)}, u32[]{:S(2)}, u32[]{:S(2)}) %collective-permute-start.11) | collective-permute-done | bytes 172064 | tf_op jit(solution)/shard_map/ppermute | solution.py:35
  33.2 1.4 %collective-permute-start.12 = (bf16[24,1792]{1,0:T(8,128)(2,1)S(1)}, bf16[24,1792]{1,0:T(8,128)(2,1)S(1)}, u32[]{:S(2)}, u32[]{:S(2)}) collective-permute-start(bf16[24,1792]{1,0:T(8,128)(2,1)S(1)} %fusion), channel_id=1, source_target_pairs={{0,8},{4,12},{8,0},{12,4},{1,9},{5,13},{9,1},{13,5},{2,10},{6,14},... | collective-permute-start | bytes 258056 | tf_op jit(solution)/shard_map/ppermute | solution.py:35
  34.6 0.3 shard_map.116.home_ref
  34.9 2.9 %collective-permute-done.12.refs_0_ = bf16[24,1792]{1,0:T(8,128)(2,1)S(1)} collective-permute-done((bf16[24,1792]{1,0:T(8,128)(2,1)S(1)}, bf16[24,1792]{1,0:T(8,128)(2,1)S(1)}, u32[]{:S(2)}, u32[]{:S(2)}) %collective-permute-start.12) | collective-permute-done | bytes 86048 | tf_op jit(solution)/shard_map/ppermute | solution.py:35
  37.8 0.9 %shard_map.118 = (bf16[16,1792]{1,0:T(8,128)(2,1)}, bf16[16,1792]{1,0:T(8,128)(2,1)}) custom-call(bf16[32,1792]{1,0:T(8,128)(2,1)S(1)} %collective-permute-done.refs_0_.moved_ref, bf16[2,32,24]{2,1,0:T(8,128)(2,1)S(1)} %shard_map.116.home_ref, bf16[2,24,1792]{2,1,0:T(8,128)(2,1)S(1)} %get-tuple-element.52.own_ref, ...), custom_call_target="tpu_custom_call" | custom-call | bytes 573440 | tf_op jit(solution)/shard_map/pallas_call | solution.py:336
  (11 shorter events, 0.1 us)
Async XLA Ops:
  1.6 5.2 %collective-permute-start.1 = (bf16[16,1920]{1,0:T(8,128)(2,1)S(1)}, bf16[16,1920]{1,0:T(8,128)(2,1)S(1)}, u32[]{:S(2)}, u32[]{:S(2)}) collective-permute-start(bf16[16,1920]{1,0:T(8,128)(2,1)S(1)} %get-tuple-element.38.refs_4_), channel_id=1, source_target_pairs={{0,8},{4,12},{8,0},{12,4},{1,9},{5,13},{9,1},{13,5},{2,10},{6,14},... | collective-permute-start | bytes 184328 | tf_op jit(solution)/shard_map/ppermute | solution.py:35
  4.7 5.8 %collective-permute-start = (bf16[32,1792]{1,0:T(8,128)(2,1)S(1)}, bf16[32,1792]{1,0:T(8,128)(2,1)S(1)}, u32[]{:S(2)}, u32[]{:S(2)}) collective-permute-start(bf16[32,1792]{1,0:T(8,128)(2,1)S(1)} %get-tuple-element.29), channel_id=1, source_target_pairs={{0,16},{4,20},{8,24},{12,28},{16,0},{20,4},{24,8},{28,12},{1,17},{... | collective-permute-start | bytes 344072 | tf_op jit(solution)/shard_map/ppermute | solution.py:46
  6.2 5.7 %collective-permute-start.4 = (bf16[32,1792]{1,0:T(8,128)(2,1)S(1)}, bf16[32,1792]{1,0:T(8,128)(2,1)S(1)}, u32[]{:S(2)}, u32[]{:S(2)}) collective-permute-start(bf16[32,1792]{1,0:T(8,128)(2,1)S(1)} %get-tuple-element.29), channel_id=1, source_target_pairs={{0,24},{4,28},{8,16},{12,20},{16,8},{20,12},{24,0},{28,4},{1,25},{... | collective-permute-start | bytes 344072 | tf_op jit(solution)/shard_map/ppermute | solution.py:46
  6.2 5.6 %collective-permute-start.2 = (bf16[16,1920]{1,0:T(8,128)(2,1)S(1)}, bf16[16,1920]{1,0:T(8,128)(2,1)S(1)}, u32[]{:S(2)}, u32[]{:S(2)}) collective-permute-start(bf16[16,1920]{1,0:T(8,128)(2,1)S(1)} %get-tuple-element.38.refs_4_), channel_id=1, source_target_pairs={{0,4},{4,0},{8,12},{12,8},{1,5},{5,1},{9,13},{13,9},{2,6},{6,2},{1... | collective-permute-start | bytes 184328 | tf_op jit(solution)/shard_map/ppermute | solution.py:35
  6.9 5.0 %collective-permute-start.3 = (bf16[16,1920]{1,0:T(8,128)(2,1)S(1)}, bf16[16,1920]{1,0:T(8,128)(2,1)S(1)}, u32[]{:S(2)}, u32[]{:S(2)}) collective-permute-start(bf16[16,1920]{1,0:T(8,128)(2,1)S(1)} %collective-permute-done.1.refs_5_), channel_id=1, source_target_pairs={{0,4},{4,0},{8,12},{12,8},{1,5},{5,1},{9,13},{13,9},{2,6},{6,2},{1... | collective-permute-start | bytes 184328 | tf_op jit(solution)/shard_map/ppermute | solution.py:35
  11.9 1.3 %collective-permute-start.6 = (bf16[32,1792]{1,0:T(8,128)(2,1)S(1)}, bf16[32,1792]{1,0:T(8,128)(2,1)S(1)}, u32[]{:S(2)}, u32[]{:S(2)}) collective-permute-start(bf16[32,1792]{1,0:T(8,128)(2,1)S(1)} %collective-permute-done.4.refs_1_), channel_id=1, source_target_pairs={{0,4},{4,0},{8,12},{12,8},{1,5},{5,1},{9,13},{13,9},{2,6},{6,2},{1... | collective-permute-start | bytes 344072 | tf_op jit(solution)/shard_map/ppermute | solution.py:35
  11.9 1.5 %collective-permute-start.5 = (bf16[32,1792]{1,0:T(8,128)(2,1)S(1)}, bf16[32,1792]{1,0:T(8,128)(2,1)S(1)}, u32[]{:S(2)}, u32[]{:S(2)}) collective-permute-start(bf16[32,1792]{1,0:T(8,128)(2,1)S(1)} %collective-permute-done.refs_0_.moved_ref), channel_id=1, source_target_pairs={{0,4},{4,0},{8,12},{12,8},{1,5},{5,1},{9,13},{13,9},{2,6},{6,2},{1... | collective-permute-start | bytes 344072 | tf_op jit(solution)/shard_map/ppermute | solution.py:35
  14.8 7.4 %collective-permute-start.7 = (bf16[120,512]{1,0:T(8,128)(2,1)S(1)}, bf16[120,512]{1,0:T(8,128)(2,1)S(1)}, u32[]{:S(2)}, u32[]{:S(2)}) collective-permute-start(bf16[120,512]{1,0:T(8,128)(2,1)S(1)} %get-tuple-element.50), channel_id=1, source_target_pairs={{0,1},{1,0},{2,3},{3,2},{4,5},{5,4},{6,7},{7,6},{8,9},{9,8},{10,11... | collective-permute-start | bytes 368648 | tf_op jit(solution)/shard_map/ppermute | solution.py:35
  16.4 7.3 %collective-permute-start.9 = (bf16[80,512]{1,0:T(8,128)(2,1)S(1)}, bf16[80,512]{1,0:T(8,128)(2,1)S(1)}, u32[]{:S(2)}, u32[]{:S(2)}) collective-permute-start(bf16[80,512]{1,0:T(8,128)(2,1)S(1)} %get-tuple-element.51), channel_id=1, source_target_pairs={{0,2},{1,3},{2,0},{3,1},{4,6},{5,7},{6,4},{7,5},{8,10},{9,11},{10,... | collective-permute-start | bytes 245768 | tf_op jit(solution)/shard_map/ppermute | solution.py:35
  22.2 7.7 %collective-permute-start.8 = (bf16[120,512]{1,0:T(8,128)(2,1)S(1)}, bf16[120,512]{1,0:T(8,128)(2,1)S(1)}, u32[]{:S(2)}, u32[]{:S(2)}) collective-permute-start(bf16[120,512]{1,0:T(8,128)(2,1)S(1)} %add_convert_fusion.fa_ref), channel_id=1, source_target_pairs={{0,2},{1,3},{2,0},{3,1},{4,6},{5,7},{6,4},{7,5},{8,10},{9,11},{10,... | collective-permute-start | bytes 368648 | tf_op jit(solution)/shard_map/ppermute | solution.py:35
  23.7 5.6 %collective-permute-start.10 = (bf16[80,512]{1,0:T(8,128)(2,1)S(1)}, bf16[80,512]{1,0:T(8,128)(2,1)S(1)}, u32[]{:S(2)}, u32[]{:S(2)}) collective-permute-start(bf16[80,512]{1,0:T(8,128)(2,1)S(1)} %add_convert_fusion.2.ba_ref), channel_id=1, source_target_pairs={{0,1},{1,0},{2,3},{3,2},{4,5},{5,4},{6,7},{7,6},{8,9},{9,8},{10,11... | collective-permute-start | bytes 245768 | tf_op jit(solution)/shard_map/ppermute | solution.py:35
  29.9 4.7 %copy-start = (s32[1,16,1]{1,2,0:T(1,128)S(1)}, s32[1,16,1]{1,2,0:T(1,128)}, u32[]{:S(2)}) copy-start(s32[1,16,1]{1,2,0:T(1,128)} %param.13) | copy-start | bytes 196
  29.9 4.7 %copy-start.1 = (bf16[1,16,1]{1,2,0:T(2,128)(2,1)S(1)}, bf16[1,16,1]{1,2,0:T(2,128)(2,1)}, u32[]{:S(2)}) copy-start(bf16[1,16,1]{1,2,0:T(2,128)(2,1)} %param.14) | copy-start | bytes 100
  29.9 4.7 %copy-start.2 = (s32[1,16,1]{1,2,0:T(1,128)S(1)}, s32[1,16,1]{1,2,0:T(1,128)}, u32[]{:S(2)}) copy-start(s32[1,16,1]{1,2,0:T(1,128)} %param.15) | copy-start | bytes 196
  29.9 4.7 %copy-start.3 = (bf16[1,16,1]{1,2,0:T(2,128)(2,1)S(1)}, bf16[1,16,1]{1,2,0:T(2,128)(2,1)}, u32[]{:S(2)}) copy-start(bf16[1,16,1]{1,2,0:T(2,128)(2,1)} %param.16) | copy-start | bytes 100
  31.7 1.5 %collective-permute-start.11 = (bf16[2,24,1792]{2,1,0:T(8,128)(2,1)S(1)}, bf16[2,24,1792]{2,1,0:T(8,128)(2,1)S(1)}, u32[]{:S(2)}, u32[]{:S(2)}) collective-permute-start(bf16[2,24,1792]{2,1,0:T(8,128)(2,1)S(1)} %get-tuple-element.53), channel_id=1, source_target_pairs={{0,4},{4,0},{8,12},{12,8},{1,5},{5,1},{9,13},{13,9},{2,6},{6,2},{1... | collective-permute-start | bytes 516104 | tf_op jit(solution)/shard_map/ppermute | solution.py:35
  33.2 4.6 %collective-permute-start.12 = (bf16[24,1792]{1,0:T(8,128)(2,1)S(1)}, bf16[24,1792]{1,0:T(8,128)(2,1)S(1)}, u32[]{:S(2)}, u32[]{:S(2)}) collective-permute-start(bf16[24,1792]{1,0:T(8,128)(2,1)S(1)} %fusion), channel_id=1, source_target_pairs={{0,8},{4,12},{8,0},{12,4},{1,9},{5,13},{9,1},{13,5},{2,10},{6,14},... | collective-permute-start | bytes 258056 | tf_op jit(solution)/shard_map/ppermute | solution.py:35

commit v5 on v4

--- a/solution.py
+++ b/solution.py
@@ -293,8 +293,12 @@
     moved_all[0], w_g, w_u, w_d = lax.optimization_barrier((moved_all[0], w_g, w_u, w_d))
     moved_all[1], w_g = lax.optimization_barrier((moved_all[1], w_g))
     w_g, w_u, w_d = in_vmem(w_g), in_vmem(w_u), in_vmem(w_d)
-    moved_all[0], *saved_all = lax.optimization_barrier((moved_all[0], *saved_all))
-    moved_all = moved_all + [swap(x, "expert", 1) for x in moved_all]
+    moved_swap = []
+    for x in moved_all:
+        if moved_swap:
+            x, *_ = lax.optimization_barrier((x, moved_swap[-1], *saved_all))
+        moved_swap.append(swap(x, "expert", 1))
+    moved_all = moved_all + moved_swap
     part_f, part_b, slot = kernel_call(
         functools.partial(up_kernel, groups, topk, rows, capacity, slot_rows),
         (

time: 38.8 us -> 38.4 us (0.990)
  waiting for transfers between devices: 15.2 us -> 13.9 us
  starting transfers between devices: 14.7 us -> 15.5 us
    ppermute x2, starting transfers between devices: 1.54 us -> 3.02 us  [onward(): return lax.ppermute(x, ('pipe', 'expert'), pairs)]
    ppermute x11, waiting for transfers between devices: 12.8 us -> 11.6 us  [swap(): return lax.ppermute(x, axis, [(i, i ^ bit) for i in range(peers)])]
    ppermute x11, starting transfers between devices: 13.2 us -> 12.4 us  [swap(): return lax.ppermute(x, axis, [(i, i ^ bit) for i in range(peers)])]
  transfers between devices with their start and end apart: 13 -> 13, of which waited for: 10 -> 7; matrix products, arithmetic and copies ran while one was open for 0% -> 0% of each run, Pallas kernels for 8% -> 8%
where the time goes in v5:
time: 38.4 us; the launch traced here: 38.2 us
  starting transfers between devices  15.5 us (40%)
  waiting for transfers between devices  13.9 us (36%)
  Pallas kernels  7.96 us (21%)
  between operations  0.73 us (2%)
    ppermute x11, starting transfers between devices, swap(): return lax.ppermute(x, axis, [(i, i ^ bit) for i in range(peers)])  12.4 us
    ppermute x11, waiting for transfers between devices, swap(): return lax.ppermute(x, axis, [(i, i ^ bit) for i in range(peers)])  11.6 us
    ppermute x2, starting transfers between devices, onward(): return lax.ppermute(x, ('pipe', 'expert'), pairs)  3.02 us
    pallas_call x1, Pallas kernels, local(): pl.pallas_call(fetch_kernel, out_shape=[pltpu.VMEM(w.shape[2:], BF16) for...  2.63 us
    ppermute x2, waiting for transfers between devices, onward(): return lax.ppermute(x, ('pipe', 'expert'), pairs)  2.36 us
    pallas_call x1, Pallas kernels, local(): kernel_call(functools.partial(down_kernel, groups, rows), [jax.ShapeDtype...  1.74 us
    pallas_call x1, Pallas kernels, local(): kernel_call(functools.partial(up_kernel, groups, topk, rows, capacity, sl...  1.44 us
    pallas_call x1, Pallas kernels, local(): pl.pallas_call(pack_kernel, out_shape=[jax.ShapeDtypeStruct((2 * held, wi...  1 us
  transfers between devices with their start and end apart: 13, of which 7 were waited for; matrix products, arithmetic and copies ran while one was open for 0% of the time, Pallas kernels for 8%

profile of v5, /device:TPU:0, one launch (start us, length us, event | category | flops | bytes accessed | tf_op | source)
XLA Modules:
  0.0 38.2 jit_solution(13753018582871379877)
XLA Ops:
  0.6 1.0 %shard_map.113 = (bf16[32,1792]{1,0:T(8,128)(2,1)S(1)}, bf16[16,1920]{1,0:T(8,128)(2,1)S(1)}) custom-call(bf16[16,1792]{1,0:T(8,128)(2,1)} %bitcast.25, bf16[16,1792]{1,0:T(8,128)(2,1)} %bitcast.26, bf16[16,1792]{1,0:T(8,128)(2,1)} %bitcast.27, s32[1,16]{1,0:T(1,128)} %bitcast.14, bf16[1,16]{1,0:T(2,128)(2,1)} %bitcast.16, s32[1,16]{1,0:T(1,128)} %bitcast.18, ...), custom_call_target="tpu_custom_call" | custom-call | bytes 344064 | tf_op jit(solution)/shard_map/pallas_call | solution.py:273
  1.6 3.0 %collective-permute-start = (bf16[32,1792]{1,0:T(8,128)(2,1)S(1)}, bf16[32,1792]{1,0:T(8,128)(2,1)S(1)}, u32[]{:S(2)}, u32[]{:S(2)}) collective-permute-start(bf16[32,1792]{1,0:T(8,128)(2,1)S(1)} %get-tuple-element.25), channel_id=1, source_target_pairs={{0,16},{4,20},{8,24},{12,28},{16,0},{20,4},{24,8},{28,12},{1,17},{... | collective-permute-start | bytes 344072 | tf_op jit(solution)/shard_map/ppermute | solution.py:46
  4.6 1.5 %collective-permute-start.3 = (bf16[16,1920]{1,0:T(8,128)(2,1)S(1)}, bf16[16,1920]{1,0:T(8,128)(2,1)S(1)}, u32[]{:S(2)}, u32[]{:S(2)}) collective-permute-start(bf16[16,1920]{1,0:T(8,128)(2,1)S(1)} %get-tuple-element.32.refs_4_), channel_id=1, source_target_pairs={{0,8},{4,12},{8,0},{12,4},{1,9},{5,13},{9,1},{13,5},{2,10},{6,14},... | collective-permute-start | bytes 184328 | tf_op jit(solution)/shard_map/ppermute | solution.py:35
  6.2 0.0 collective-permute-start.1
  6.2 2.6 %shard_map.114 = (bf16[1792,512]{1,0:T(8,128)(2,1)S(1)}, bf16[1792,512]{1,0:T(8,128)(2,1)S(1)}, bf16[512,1792]{1,0:T(8,128)(2,1)S(1)}) custom-call(bf16[1792,512]{1,0:T(8,128)(2,1)} %bitcast.22, bf16[1792,512]{1,0:T(8,128)(2,1)} %bitcast.23, bf16[512,1792]{1,0:T(8,128)(2,1)} %bitcast.24), custom_call_target="tpu_custom_call" | custom-call | bytes 11010048 | tf_op jit(solution)/shard_map/pallas_call | solution.py:259
  8.8 0.0 collective-permute-done.refs_0_.moved_ref
  8.8 0.1 collective-permute-start.2
  8.9 0.5 %collective-permute-start.4 = (bf16[16,1920]{1,0:T(8,128)(2,1)S(1)}, bf16[16,1920]{1,0:T(8,128)(2,1)S(1)}, u32[]{:S(2)}, u32[]{:S(2)}) collective-permute-start(bf16[16,1920]{1,0:T(8,128)(2,1)S(1)} %get-tuple-element.32.refs_4_), channel_id=1, source_target_pairs={{0,4},{4,0},{8,12},{12,8},{1,5},{5,1},{9,13},{13,9},{2,6},{6,2},{1... | collective-permute-start | bytes 184328 | tf_op jit(solution)/shard_map/ppermute | solution.py:35
  9.4 0.0 collective-permute-done.3.refs_5_
  9.4 0.1 collective-permute-start.5
  9.5 2.4 %collective-permute-done.1.refs_1_ = bf16[32,1792]{1,0:T(8,128)(2,1)S(1)} collective-permute-done((bf16[32,1792]{1,0:T(8,128)(2,1)S(1)}, bf16[32,1792]{1,0:T(8,128)(2,1)S(1)}, u32[]{:S(2)}, u32[]{:S(2)}) %collective-permute-start.1) | collective-permute-done | bytes 114720 | tf_op jit(solution)/shard_map/ppermute | solution.py:46
  11.9 0.0 collective-permute-done.4.refs_6_
  11.9 0.0 collective-permute-done.5.refs_7_
  11.9 0.0 collective-permute-done.2.refs_2_
  11.9 0.1 collective-permute-start.6
  11.9 1.3 %collective-permute-done.6.refs_3_ = bf16[32,1792]{1,0:T(8,128)(2,1)S(1)} collective-permute-done((bf16[32,1792]{1,0:T(8,128)(2,1)S(1)}, bf16[32,1792]{1,0:T(8,128)(2,1)S(1)}, u32[]{:S(2)}, u32[]{:S(2)}) %collective-permute-start.6) | collective-permute-done | bytes 114720 | tf_op jit(solution)/shard_map/ppermute | solution.py:35
  13.3 1.4 %shard_map.115 = (bf16[120,512]{1,0:T(8,128)(2,1)S(1)}, bf16[80,512]{1,0:T(8,128)(2,1)S(1)}, bf16[96,80]{1,0:T(8,128)(2,1)S(1)}) custom-call(bf16[32,1792]{1,0:T(8,128)(2,1)S(1)} %collective-permute-done.refs_0_.moved_ref, bf16[32,1792]{1,0:T(8,128)(2,1)S(1)} %collective-permute-done.1.refs_1_, bf16[32,1792]{1,0:T(8,128)(2,1)S(1)} %collective-permute-done.2.refs_2_, ...), custom_call_target="tpu_custom_call" | custom-call | flops 367001600 | bytes 5505024 | tf_op jit(solution)/shard_map/pallas_call | solution.py:302
  14.7 1.6 %collective-permute-start.7 = (bf16[120,512]{1,0:T(8,128)(2,1)S(1)}, bf16[120,512]{1,0:T(8,128)(2,1)S(1)}, u32[]{:S(2)}, u32[]{:S(2)}) collective-permute-start(bf16[120,512]{1,0:T(8,128)(2,1)S(1)} %get-tuple-element.42), channel_id=1, source_target_pairs={{0,1},{1,0},{2,3},{3,2},{4,5},{5,4},{6,7},{7,6},{8,9},{9,8},{10,11... | collective-permute-start | bytes 368648 | tf_op jit(solution)/shard_map/ppermute | solution.py:35
  16.3 2.6 %collective-permute-start.9 = (bf16[80,512]{1,0:T(8,128)(2,1)S(1)}, bf16[80,512]{1,0:T(8,128)(2,1)S(1)}, u32[]{:S(2)}, u32[]{:S(2)}) collective-permute-start(bf16[80,512]{1,0:T(8,128)(2,1)S(1)} %get-tuple-element.43), channel_id=1, source_target_pairs={{0,2},{1,3},{2,0},{3,1},{4,6},{5,7},{6,4},{7,5},{8,10},{9,11},{10,... | collective-permute-start | bytes 245768 | tf_op jit(solution)/shard_map/ppermute | solution.py:35
  18.9 2.9 %collective-permute-done.7 = bf16[120,512]{1,0:T(8,128)(2,1)S(1)} collective-permute-done((bf16[120,512]{1,0:T(8,128)(2,1)S(1)}, bf16[120,512]{1,0:T(8,128)(2,1)S(1)}, u32[]{:S(2)}, u32[]{:S(2)}) %collective-permute-start.7) | collective-permute-done | bytes 122912 | tf_op jit(solution)/shard_map/ppermute | solution.py:35
  21.8 1.8 %collective-permute-start.8 = (bf16[120,512]{1,0:T(8,128)(2,1)S(1)}, bf16[120,512]{1,0:T(8,128)(2,1)S(1)}, u32[]{:S(2)}, u32[]{:S(2)}) collective-permute-start(bf16[120,512]{1,0:T(8,128)(2,1)S(1)} %add_convert_fusion.fa_ref), channel_id=1, source_target_pairs={{0,2},{1,3},{2,0},{3,1},{4,6},{5,7},{6,4},{7,5},{8,10},{9,11},{10,... | collective-permute-start | bytes 368648 | tf_op jit(solution)/shard_map/ppermute | solution.py:35
  23.6 0.0 collective-permute-done.9
  23.7 2.1 %collective-permute-start.10 = (bf16[80,512]{1,0:T(8,128)(2,1)S(1)}, bf16[80,512]{1,0:T(8,128)(2,1)S(1)}, u32[]{:S(2)}, u32[]{:S(2)}) collective-permute-start(bf16[80,512]{1,0:T(8,128)(2,1)S(1)} %add_convert_fusion.2.ba_ref), channel_id=1, source_target_pairs={{0,1},{1,0},{2,3},{3,2},{4,5},{5,4},{6,7},{7,6},{8,9},{9,8},{10,11... | collective-permute-start | bytes 245768 | tf_op jit(solution)/shard_map/ppermute | solution.py:35
  25.7 2.9 %collective-permute-done.10.bb_ref = bf16[80,512]{1,0:T(8,128)(2,1)S(1)} collective-permute-done((bf16[80,512]{1,0:T(8,128)(2,1)S(1)}, bf16[80,512]{1,0:T(8,128)(2,1)S(1)}, u32[]{:S(2)}, u32[]{:S(2)}) %collective-permute-start.10) | collective-permute-done | bytes 81952 | tf_op jit(solution)/shard_map/ppermute | solution.py:35
  28.6 0.6 %collective-permute-done.8.fb_ref = bf16[120,512]{1,0:T(8,128)(2,1)S(1)} collective-permute-done((bf16[120,512]{1,0:T(8,128)(2,1)S(1)}, bf16[120,512]{1,0:T(8,128)(2,1)S(1)}, u32[]{:S(2)}, u32[]{:S(2)}) %collective-permute-start.8) | collective-permute-done | bytes 122912 | tf_op jit(solution)/shard_map/ppermute | solution.py:35
  29.2 1.7 %shard_map.117 = (bf16[2,24,1792]{2,1,0:T(8,128)(2,1)S(1)}, bf16[2,24,1792]{2,1,0:T(8,128)(2,1)S(1)}) custom-call(bf16[120,512]{1,0:T(8,128)(2,1)S(1)} %add_convert_fusion.fa_ref, bf16[120,512]{1,0:T(8,128)(2,1)S(1)} %collective-permute-done.8.fb_ref, bf16[80,512]{1,0:T(8,128)(2,1)S(1)} %add_convert_fusion.2.ba_ref, ...), custom_call_target="tpu_custom_call" | custom-call | flops 220200960 | bytes 5505024 | tf_op jit(solution)/shard_map/pallas_call | solution.py:321
  31.0 0.1 collective-permute-start.11
  31.0 1.4 %collective-permute-done.11.other_ref = bf16[2,24,1792]{2,1,0:T(8,128)(2,1)S(1)} collective-permute-done((bf16[2,24,1792]{2,1,0:T(8,128)(2,1)S(1)}, bf16[2,24,1792]{2,1,0:T(8,128)(2,1)S(1)}, u32[]{:S(2)}, u32[]{:S(2)}) %collective-permute-start.11) | collective-permute-done | bytes 172064 | tf_op jit(solution)/shard_map/ppermute | solution.py:35
  32.5 2.0 %collective-permute-start.12 = (bf16[24,1792]{1,0:T(8,128)(2,1)S(1)}, bf16[24,1792]{1,0:T(8,128)(2,1)S(1)}, u32[]{:S(2)}, u32[]{:S(2)}) collective-permute-start(bf16[24,1792]{1,0:T(8,128)(2,1)S(1)} %fusion), channel_id=1, source_target_pairs={{0,8},{4,12},{8,0},{12,4},{1,9},{5,13},{9,1},{13,5},{2,10},{6,14},... | collective-permute-start | bytes 258056 | tf_op jit(solution)/shard_map/ppermute | solution.py:35
  34.5 0.3 shard_map.116.home_ref
  34.8 2.5 %collective-permute-done.12.refs_0_ = bf16[24,1792]{1,0:T(8,128)(2,1)S(1)} collective-permute-done((bf16[24,1792]{1,0:T(8,128)(2,1)S(1)}, bf16[24,1792]{1,0:T(8,128)(2,1)S(1)}, u32[]{:S(2)}, u32[]{:S(2)}) %collective-permute-start.12) | collective-permute-done | bytes 86048 | tf_op jit(solution)/shard_map/ppermute | solution.py:35
  37.3 0.9 %shard_map.118 = (bf16[16,1792]{1,0:T(8,128)(2,1)}, bf16[16,1792]{1,0:T(8,128)(2,1)}) custom-call(bf16[32,1792]{1,0:T(8,128)(2,1)S(1)} %collective-permute-done.refs_0_.moved_ref, bf16[2,32,24]{2,1,0:T(8,128)(2,1)S(1)} %shard_map.116.home_ref, bf16[2,24,1792]{2,1,0:T(8,128)(2,1)S(1)} %get-tuple-element.44.own_ref, ...), custom_call_target="tpu_custom_call" | custom-call | bytes 573440 | tf_op jit(solution)/shard_map/pallas_call | solution.py:340
  (11 shorter events, 0.1 us)
Async XLA Ops:
  1.6 7.2 %collective-permute-start = (bf16[32,1792]{1,0:T(8,128)(2,1)S(1)}, bf16[32,1792]{1,0:T(8,128)(2,1)S(1)}, u32[]{:S(2)}, u32[]{:S(2)}) collective-permute-start(bf16[32,1792]{1,0:T(8,128)(2,1)S(1)} %get-tuple-element.25), channel_id=1, source_target_pairs={{0,16},{4,20},{8,24},{12,28},{16,0},{20,4},{24,8},{28,12},{1,17},{... | collective-permute-start | bytes 344072 | tf_op jit(solution)/shard_map/ppermute | solution.py:46
  4.6 4.8 %collective-permute-start.3 = (bf16[16,1920]{1,0:T(8,128)(2,1)S(1)}, bf16[16,1920]{1,0:T(8,128)(2,1)S(1)}, u32[]{:S(2)}, u32[]{:S(2)}) collective-permute-start(bf16[16,1920]{1,0:T(8,128)(2,1)S(1)} %get-tuple-element.32.refs_4_), channel_id=1, source_target_pairs={{0,8},{4,12},{8,0},{12,4},{1,9},{5,13},{9,1},{13,5},{2,10},{6,14},... | collective-permute-start | bytes 184328 | tf_op jit(solution)/shard_map/ppermute | solution.py:35
  6.2 5.7 %collective-permute-start.1 = (bf16[32,1792]{1,0:T(8,128)(2,1)S(1)}, bf16[32,1792]{1,0:T(8,128)(2,1)S(1)}, u32[]{:S(2)}, u32[]{:S(2)}) collective-permute-start(bf16[32,1792]{1,0:T(8,128)(2,1)S(1)} %get-tuple-element.25), channel_id=1, source_target_pairs={{0,24},{4,28},{8,16},{12,20},{16,8},{20,12},{24,0},{28,4},{1,25},{... | collective-permute-start | bytes 344072 | tf_op jit(solution)/shard_map/ppermute | solution.py:46
  8.8 3.0 %collective-permute-start.2 = (bf16[32,1792]{1,0:T(8,128)(2,1)S(1)}, bf16[32,1792]{1,0:T(8,128)(2,1)S(1)}, u32[]{:S(2)}, u32[]{:S(2)}) collective-permute-start(bf16[32,1792]{1,0:T(8,128)(2,1)S(1)} %collective-permute-done.refs_0_.moved_ref), channel_id=1, source_target_pairs={{0,4},{4,0},{8,12},{12,8},{1,5},{5,1},{9,13},{13,9},{2,6},{6,2},{1... | collective-permute-start | bytes 344072 | tf_op jit(solution)/shard_map/ppermute | solution.py:35
  8.9 2.9 %collective-permute-start.4 = (bf16[16,1920]{1,0:T(8,128)(2,1)S(1)}, bf16[16,1920]{1,0:T(8,128)(2,1)S(1)}, u32[]{:S(2)}, u32[]{:S(2)}) collective-permute-start(bf16[16,1920]{1,0:T(8,128)(2,1)S(1)} %get-tuple-element.32.refs_4_), channel_id=1, source_target_pairs={{0,4},{4,0},{8,12},{12,8},{1,5},{5,1},{9,13},{13,9},{2,6},{6,2},{1... | collective-permute-start | bytes 184328 | tf_op jit(solution)/shard_map/ppermute | solution.py:35
  9.4 2.4 %collective-permute-start.5 = (bf16[16,1920]{1,0:T(8,128)(2,1)S(1)}, bf16[16,1920]{1,0:T(8,128)(2,1)S(1)}, u32[]{:S(2)}, u32[]{:S(2)}) collective-permute-start(bf16[16,1920]{1,0:T(8,128)(2,1)S(1)} %collective-permute-done.3.refs_5_), channel_id=1, source_target_pairs={{0,4},{4,0},{8,12},{12,8},{1,5},{5,1},{9,13},{13,9},{2,6},{6,2},{1... | collective-permute-start | bytes 184328 | tf_op jit(solution)/shard_map/ppermute | solution.py:35
  11.9 1.4 %collective-permute-start.6 = (bf16[32,1792]{1,0:T(8,128)(2,1)S(1)}, bf16[32,1792]{1,0:T(8,128)(2,1)S(1)}, u32[]{:S(2)}, u32[]{:S(2)}) collective-permute-start(bf16[32,1792]{1,0:T(8,128)(2,1)S(1)} %collective-permute-done.1.refs_1_), channel_id=1, source_target_pairs={{0,4},{4,0},{8,12},{12,8},{1,5},{5,1},{9,13},{13,9},{2,6},{6,2},{1... | collective-permute-start | bytes 344072 | tf_op jit(solution)/shard_map/ppermute | solution.py:35
  14.7 7.1 %collective-permute-start.7 = (bf16[120,512]{1,0:T(8,128)(2,1)S(1)}, bf16[120,512]{1,0:T(8,128)(2,1)S(1)}, u32[]{:S(2)}, u32[]{:S(2)}) collective-permute-start(bf16[120,512]{1,0:T(8,128)(2,1)S(1)} %get-tuple-element.42), channel_id=1, source_target_pairs={{0,1},{1,0},{2,3},{3,2},{4,5},{5,4},{6,7},{7,6},{8,9},{9,8},{10,11... | collective-permute-start | bytes 368648 | tf_op jit(solution)/shard_map/ppermute | solution.py:35
  16.3 7.3 %collective-permute-start.9 = (bf16[80,512]{1,0:T(8,128)(2,1)S(1)}, bf16[80,512]{1,0:T(8,128)(2,1)S(1)}, u32[]{:S(2)}, u32[]{:S(2)}) collective-permute-start(bf16[80,512]{1,0:T(8,128)(2,1)S(1)} %get-tuple-element.43), channel_id=1, source_target_pairs={{0,2},{1,3},{2,0},{3,1},{4,6},{5,7},{6,4},{7,5},{8,10},{9,11},{10,... | collective-permute-start | bytes 245768 | tf_op jit(solution)/shard_map/ppermute | solution.py:35
  21.8 7.4 %collective-permute-start.8 = (bf16[120,512]{1,0:T(8,128)(2,1)S(1)}, bf16[120,512]{1,0:T(8,128)(2,1)S(1)}, u32[]{:S(2)}, u32[]{:S(2)}) collective-permute-start(bf16[120,512]{1,0:T(8,128)(2,1)S(1)} %add_convert_fusion.fa_ref), channel_id=1, source_target_pairs={{0,2},{1,3},{2,0},{3,1},{4,6},{5,7},{6,4},{7,5},{8,10},{9,11},{10,... | collective-permute-start | bytes 368648 | tf_op jit(solution)/shard_map/ppermute | solution.py:35
  23.7 5.0 %collective-permute-start.10 = (bf16[80,512]{1,0:T(8,128)(2,1)S(1)}, bf16[80,512]{1,0:T(8,128)(2,1)S(1)}, u32[]{:S(2)}, u32[]{:S(2)}) collective-permute-start(bf16[80,512]{1,0:T(8,128)(2,1)S(1)} %add_convert_fusion.2.ba_ref), channel_id=1, source_target_pairs={{0,1},{1,0},{2,3},{3,2},{4,5},{5,4},{6,7},{7,6},{8,9},{9,8},{10,11... | collective-permute-start | bytes 245768 | tf_op jit(solution)/shard_map/ppermute | solution.py:35
  29.2 5.3 %copy-start = (s32[1,16,1]{1,2,0:T(1,128)S(1)}, s32[1,16,1]{1,2,0:T(1,128)}, u32[]{:S(2)}) copy-start(s32[1,16,1]{1,2,0:T(1,128)} %param.13) | copy-start | bytes 196
  29.2 5.3 %copy-start.1 = (bf16[1,16,1]{1,2,0:T(2,128)(2,1)S(1)}, bf16[1,16,1]{1,2,0:T(2,128)(2,1)}, u32[]{:S(2)}) copy-start(bf16[1,16,1]{1,2,0:T(2,128)(2,1)} %param.14) | copy-start | bytes 100
  29.2 5.3 %copy-start.2 = (s32[1,16,1]{1,2,0:T(1,128)S(1)}, s32[1,16,1]{1,2,0:T(1,128)}, u32[]{:S(2)}) copy-start(s32[1,16,1]{1,2,0:T(1,128)} %param.15) | copy-start | bytes 196
  29.2 5.3 %copy-start.3 = (bf16[1,16,1]{1,2,0:T(2,128)(2,1)S(1)}, bf16[1,16,1]{1,2,0:T(2,128)(2,1)}, u32[]{:S(2)}) copy-start(bf16[1,16,1]{1,2,0:T(2,128)(2,1)} %param.16) | copy-start | bytes 100
  31.0 1.5 %collective-permute-start.11 = (bf16[2,24,1792]{2,1,0:T(8,128)(2,1)S(1)}, bf16[2,24,1792]{2,1,0:T(8,128)(2,1)S(1)}, u32[]{:S(2)}, u32[]{:S(2)}) collective-permute-start(bf16[2,24,1792]{2,1,0:T(8,128)(2,1)S(1)} %get-tuple-element.45), channel_id=1, source_target_pairs={{0,4},{4,0},{8,12},{12,8},{1,5},{5,1},{9,13},{13,9},{2,6},{6,2},{1... | collective-permute-start | bytes 516104 | tf_op jit(solution)/shard_map/ppermute | solution.py:35
  32.5 4.9 %collective-permute-start.12 = (bf16[24,1792]{1,0:T(8,128)(2,1)S(1)}, bf16[24,1792]{1,0:T(8,128)(2,1)S(1)}, u32[]{:S(2)}, u32[]{:S(2)}) collective-permute-start(bf16[24,1792]{1,0:T(8,128)(2,1)S(1)} %fusion), channel_id=1, source_target_pairs={{0,8},{4,12},{8,0},{12,4},{1,9},{5,13},{9,1},{13,5},{2,10},{6,14},... | collective-permute-start | bytes 258056 | tf_op jit(solution)/shard_map/ppermute | solution.py:35

commit v6 on v5

--- a/solution.py
+++ b/solution.py
@@ -183,8 +183,9 @@
     gate = jnp.dot(both, w_g_ref[...], preferred_element_type=F32)
     upper = jnp.dot(both, w_u_ref[...], preferred_element_type=F32)
     dhid = lax.dot_general(grads_b, w_d_ref[...], (((1,), (1,)), ((), ())), preferred_element_type=F32)
-    part_f_ref[...] = jnp.concatenate([gate[:rows], upper[:rows], dhid], axis=0).astype(BF16)
-    part_b_ref[...] = jnp.concatenate([gate[rows:], upper[rows:]], axis=0).astype(BF16)
+    cut = part_f_ref.shape[1] - 2 * dhid.shape[1]
+    part_f_ref[...] = jnp.concatenate([gate[:rows], upper[:rows], dhid[:, :cut]], axis=1).astype(BF16)
+    part_b_ref[...] = jnp.concatenate([gate[rows:], upper[rows:], dhid[:, cut:]], axis=1).astype(BF16)
 
 
 def down_kernel(
@@ -203,8 +204,10 @@
 ):
     total_f = fa_ref[...].astype(F32) + fb_ref[...].astype(F32)
     total_b = ba_ref[...].astype(F32) + bb_ref[...].astype(F32)
-    gate_f, upper_f, dhid = [total_f[i * rows : (i + 1) * rows] for i in range(3)]
-    gate_b, upper_b = total_b[:rows], total_b[rows:]
+    units = w_d_ref.shape[0]
+    gate_f, upper_f = total_f[:, :units], total_f[:, units : 2 * units]
+    gate_b, upper_b = total_b[:, :units], total_b[:, units : 2 * units]
+    dhid = jnp.concatenate([total_f[:, 2 * units :], total_b[:, 2 * units :]], axis=1)
     hidden = (gate_f * jax.nn.sigmoid(gate_f) * upper_f).astype(BF16)
     sigma = jax.nn.sigmoid(gate_b)
     slope = sigma * (1.0 + gate_b * (1.0 - sigma))
@@ -254,6 +257,7 @@
     topk = routes_forward.shape[2]
     capacity = min(held, max(6, held * topk // experts + 2))
     rows = -(-peers * capacity // 8) * 8
+    cut = hidden * 3 // 4
     slot_rows = -(-2 * capacity // 8) * 8
     weight_bytes = 6 * width * hidden
     w_g, w_u, w_d = pl.pallas_call(
@@ -302,8 +306,8 @@
     part_f, part_b, slot = kernel_call(
         functools.partial(up_kernel, groups, topk, rows, capacity, slot_rows),
         (
-            jax.ShapeDtypeStruct((3 * rows, hidden), BF16),
-            jax.ShapeDtypeStruct((2 * rows, hidden), BF16),
+            jax.ShapeDtypeStruct((rows, 2 * hidden + cut), BF16),
+            jax.ShapeDtypeStruct((rows, 3 * hidden - cut), BF16),
             jax.ShapeDtypeStruct((peers * slot_rows, 2 * rows), BF16),
         ),
         10 * rows * width * hidden,

time: 38.4 us -> 38.1 us (level)
  transfers between devices with their start and end apart: 13 -> 13, of which waited for: 7 -> 6; matrix products, arithmetic and copies ran while one was open for 0% -> 0% of each run, Pallas kernels for 8% -> 8%
where the time goes in v6:
time: 38.1 us; the launch traced here: 37.9 us
  starting transfers between devices  15.5 us (41%)
  waiting for transfers between devices  13.6 us (36%)
  Pallas kernels  7.97 us (21%)
  between operations  0.74 us (2%)
    ppermute x11, starting transfers between devices, swap(): return lax.ppermute(x, axis, [(i, i ^ bit) for i in range(peers)])  12.5 us
    ppermute x11, waiting for transfers between devices, swap(): return lax.ppermute(x, axis, [(i, i ^ bit) for i in range(peers)])  11.2 us
    ppermute x2, starting transfers between devices, onward(): return lax.ppermute(x, ('pipe', 'expert'), pairs)  3.02 us
    pallas_call x1, Pallas kernels, local(): pl.pallas_call(fetch_kernel, out_shape=[pltpu.VMEM(w.shape[2:], BF16) for...  2.63 us
    ppermute x2, waiting for transfers between devices, onward(): return lax.ppermute(x, ('pipe', 'expert'), pairs)  2.36 us
    pallas_call x1, Pallas kernels, local(): kernel_call(functools.partial(down_kernel, groups, rows), [jax.ShapeDtype...  1.74 us
    pallas_call x1, Pallas kernels, local(): kernel_call(functools.partial(up_kernel, groups, topk, rows, capacity, sl...  1.45 us
    pallas_call x1, Pallas kernels, local(): pl.pallas_call(pack_kernel, out_shape=[jax.ShapeDtypeStruct((2 * held, wi...  1 us
  transfers between devices with their start and end apart: 13, of which 6 were waited for; matrix products, arithmetic and copies ran while one was open for 0% of the time, Pallas kernels for 8%

profile of v6, /device:TPU:0, one launch (start us, length us, event | category | flops | bytes accessed | tf_op | source)
XLA Modules:
  0.0 37.9 jit_solution(14331545338280697215)
XLA Ops:
  0.6 1.0 %shard_map.113 = (bf16[32,1792]{1,0:T(8,128)(2,1)S(1)}, bf16[16,1920]{1,0:T(8,128)(2,1)S(1)}) custom-call(bf16[16,1792]{1,0:T(8,128)(2,1)} %bitcast.25, bf16[16,1792]{1,0:T(8,128)(2,1)} %bitcast.26, bf16[16,1792]{1,0:T(8,128)(2,1)} %bitcast.27, s32[1,16]{1,0:T(1,128)} %bitcast.14, bf16[1,16]{1,0:T(2,128)(2,1)} %bitcast.16, s32[1,16]{1,0:T(1,128)} %bitcast.18, ...), custom_call_target="tpu_custom_call" | custom-call | bytes 344064 | tf_op jit(solution)/shard_map/pallas_call | solution.py:277
  1.6 3.0 %collective-permute-start = (bf16[32,1792]{1,0:T(8,128)(2,1)S(1)}, bf16[32,1792]{1,0:T(8,128)(2,1)S(1)}, u32[]{:S(2)}, u32[]{:S(2)}) collective-permute-start(bf16[32,1792]{1,0:T(8,128)(2,1)S(1)} %get-tuple-element.25), channel_id=1, source_target_pairs={{0,16},{4,20},{8,24},{12,28},{16,0},{20,4},{24,8},{28,12},{1,17},{... | collective-permute-start | bytes 344072 | tf_op jit(solution)/shard_map/ppermute | solution.py:46
  4.6 1.5 %collective-permute-start.3 = (bf16[16,1920]{1,0:T(8,128)(2,1)S(1)}, bf16[16,1920]{1,0:T(8,128)(2,1)S(1)}, u32[]{:S(2)}, u32[]{:S(2)}) collective-permute-start(bf16[16,1920]{1,0:T(8,128)(2,1)S(1)} %get-tuple-element.32.refs_4_), channel_id=1, source_target_pairs={{0,8},{4,12},{8,0},{12,4},{1,9},{5,13},{9,1},{13,5},{2,10},{6,14},... | collective-permute-start | bytes 184328 | tf_op jit(solution)/shard_map/ppermute | solution.py:35
  6.2 0.0 collective-permute-start.1
  6.2 2.6 %shard_map.114 = (bf16[1792,512]{1,0:T(8,128)(2,1)S(1)}, bf16[1792,512]{1,0:T(8,128)(2,1)S(1)}, bf16[512,1792]{1,0:T(8,128)(2,1)S(1)}) custom-call(bf16[1792,512]{1,0:T(8,128)(2,1)} %bitcast.22, bf16[1792,512]{1,0:T(8,128)(2,1)} %bitcast.23, bf16[512,1792]{1,0:T(8,128)(2,1)} %bitcast.24), custom_call_target="tpu_custom_call" | custom-call | bytes 11010048 | tf_op jit(solution)/shard_map/pallas_call | solution.py:263
  8.8 0.0 collective-permute-done.refs_0_.moved_ref
  8.8 0.1 collective-permute-start.2
  8.9 0.5 %collective-permute-start.4 = (bf16[16,1920]{1,0:T(8,128)(2,1)S(1)}, bf16[16,1920]{1,0:T(8,128)(2,1)S(1)}, u32[]{:S(2)}, u32[]{:S(2)}) collective-permute-start(bf16[16,1920]{1,0:T(8,128)(2,1)S(1)} %get-tuple-element.32.refs_4_), channel_id=1, source_target_pairs={{0,4},{4,0},{8,12},{12,8},{1,5},{5,1},{9,13},{13,9},{2,6},{6,2},{1... | collective-permute-start | bytes 184328 | tf_op jit(solution)/shard_map/ppermute | solution.py:35
  9.4 0.0 collective-permute-done.3.refs_5_
  9.4 0.1 collective-permute-start.5
  9.5 2.4 %collective-permute-done.1.refs_1_ = bf16[32,1792]{1,0:T(8,128)(2,1)S(1)} collective-permute-done((bf16[32,1792]{1,0:T(8,128)(2,1)S(1)}, bf16[32,1792]{1,0:T(8,128)(2,1)S(1)}, u32[]{:S(2)}, u32[]{:S(2)}) %collective-permute-start.1) | collective-permute-done | bytes 114720 | tf_op jit(solution)/shard_map/ppermute | solution.py:46
  11.9 0.0 collective-permute-done.4.refs_6_
  11.9 0.0 collective-permute-done.5.refs_7_
  11.9 0.0 collective-permute-done.2.refs_2_
  11.9 0.1 collective-permute-start.6
  11.9 1.3 %collective-permute-done.6.refs_3_ = bf16[32,1792]{1,0:T(8,128)(2,1)S(1)} collective-permute-done((bf16[32,1792]{1,0:T(8,128)(2,1)S(1)}, bf16[32,1792]{1,0:T(8,128)(2,1)S(1)}, u32[]{:S(2)}, u32[]{:S(2)}) %collective-permute-start.6) | collective-permute-done | bytes 114720 | tf_op jit(solution)/shard_map/ppermute | solution.py:35
  13.3 1.4 %shard_map.115 = (bf16[40,1408]{1,0:T(8,128)(2,1)S(1)}, bf16[40,1152]{1,0:T(8,128)(2,1)S(1)}, bf16[96,80]{1,0:T(8,128)(2,1)S(1)}) custom-call(bf16[32,1792]{1,0:T(8,128)(2,1)S(1)} %collective-permute-done.refs_0_.moved_ref, bf16[32,1792]{1,0:T(8,128)(2,1)S(1)} %collective-permute-done.1.refs_1_, bf16[32,1792]{1,0:T(8,128)(2,1)S(1)} %collective-permute-done.2.refs_2_, ...), custom_call_target="tpu_custom_call" | custom-call | flops 367001600 | bytes 5505024 | tf_op jit(solution)/shard_map/pallas_call | solution.py:306
  14.7 1.6 %collective-permute-start.7 = (bf16[40,1408]{1,0:T(8,128)(2,1)S(1)}, bf16[40,1408]{1,0:T(8,128)(2,1)S(1)}, u32[]{:S(2)}, u32[]{:S(2)}) collective-permute-start(bf16[40,1408]{1,0:T(8,128)(2,1)S(1)} %get-tuple-element.42), channel_id=1, source_target_pairs={{0,1},{1,0},{2,3},{3,2},{4,5},{5,4},{6,7},{7,6},{8,9},{9,8},{10,11... | collective-permute-start | bytes 337928 | tf_op jit(solution)/shard_map/ppermute | solution.py:35
  16.4 2.6 %collective-permute-start.9 = (bf16[40,1152]{1,0:T(8,128)(2,1)S(1)}, bf16[40,1152]{1,0:T(8,128)(2,1)S(1)}, u32[]{:S(2)}, u32[]{:S(2)}) collective-permute-start(bf16[40,1152]{1,0:T(8,128)(2,1)S(1)} %get-tuple-element.43), channel_id=1, source_target_pairs={{0,2},{1,3},{2,0},{3,1},{4,6},{5,7},{6,4},{7,5},{8,10},{9,11},{10,... | collective-permute-start | bytes 276488 | tf_op jit(solution)/shard_map/ppermute | solution.py:35
  18.9 2.5 %collective-permute-done.7 = bf16[40,1408]{1,0:T(8,128)(2,1)S(1)} collective-permute-done((bf16[40,1408]{1,0:T(8,128)(2,1)S(1)}, bf16[40,1408]{1,0:T(8,128)(2,1)S(1)}, u32[]{:S(2)}, u32[]{:S(2)}) %collective-permute-start.7) | collective-permute-done | bytes 112672 | tf_op jit(solution)/shard_map/ppermute | solution.py:35
  21.4 2.0 %collective-permute-start.8 = (bf16[40,1408]{1,0:T(8,128)(2,1)S(1)}, bf16[40,1408]{1,0:T(8,128)(2,1)S(1)}, u32[]{:S(2)}, u32[]{:S(2)}) collective-permute-start(bf16[40,1408]{1,0:T(8,128)(2,1)S(1)} %add_convert_fusion.fa_ref), channel_id=1, source_target_pairs={{0,2},{1,3},{2,0},{3,1},{4,6},{5,7},{6,4},{7,5},{8,10},{9,11},{10,... | collective-permute-start | bytes 337928 | tf_op jit(solution)/shard_map/ppermute | solution.py:35
  23.4 2.0 %collective-permute-start.10 = (bf16[40,1152]{1,0:T(8,128)(2,1)S(1)}, bf16[40,1152]{1,0:T(8,128)(2,1)S(1)}, u32[]{:S(2)}, u32[]{:S(2)}) collective-permute-start(bf16[40,1152]{1,0:T(8,128)(2,1)S(1)} %add_convert_fusion.1.ba_ref), channel_id=1, source_target_pairs={{0,1},{1,0},{2,3},{3,2},{4,5},{5,4},{6,7},{7,6},{8,9},{9,8},{10,11... | collective-permute-start | bytes 276488 | tf_op jit(solution)/shard_map/ppermute | solution.py:35
  25.4 3.5 %collective-permute-done.10.bb_ref = bf16[40,1152]{1,0:T(8,128)(2,1)S(1)} collective-permute-done((bf16[40,1152]{1,0:T(8,128)(2,1)S(1)}, bf16[40,1152]{1,0:T(8,128)(2,1)S(1)}, u32[]{:S(2)}, u32[]{:S(2)}) %collective-permute-start.10) | collective-permute-done | bytes 92192 | tf_op jit(solution)/shard_map/ppermute | solution.py:35
  28.9 0.0 collective-permute-done.8.fb_ref
  28.9 0.0 copy-start.3
  28.9 1.7 %shard_map.117 = (bf16[2,24,1792]{2,1,0:T(8,128)(2,1)S(1)}, bf16[2,24,1792]{2,1,0:T(8,128)(2,1)S(1)}) custom-call(bf16[40,1408]{1,0:T(8,128)(2,1)S(1)} %add_convert_fusion.fa_ref, bf16[40,1408]{1,0:T(8,128)(2,1)S(1)} %collective-permute-done.8.fb_ref, bf16[40,1152]{1,0:T(8,128)(2,1)S(1)} %add_convert_fusion.1.ba_ref, ...), custom_call_target="tpu_custom_call" | custom-call | flops 220200960 | bytes 5505024 | tf_op jit(solution)/shard_map/pallas_call | solution.py:325
  30.7 0.1 collective-permute-start.11
  30.8 1.4 %collective-permute-done.11.other_ref = bf16[2,24,1792]{2,1,0:T(8,128)(2,1)S(1)} collective-permute-done((bf16[2,24,1792]{2,1,0:T(8,128)(2,1)S(1)}, bf16[2,24,1792]{2,1,0:T(8,128)(2,1)S(1)}, u32[]{:S(2)}, u32[]{:S(2)}) %collective-permute-start.11) | collective-permute-done | bytes 172064 | tf_op jit(solution)/shard_map/ppermute | solution.py:35
  32.2 2.0 %collective-permute-start.12 = (bf16[24,1792]{1,0:T(8,128)(2,1)S(1)}, bf16[24,1792]{1,0:T(8,128)(2,1)S(1)}, u32[]{:S(2)}, u32[]{:S(2)}) collective-permute-start(bf16[24,1792]{1,0:T(8,128)(2,1)S(1)} %fusion), channel_id=1, source_target_pairs={{0,8},{4,12},{8,0},{12,4},{1,9},{5,13},{9,1},{13,5},{2,10},{6,14},... | collective-permute-start | bytes 258056 | tf_op jit(solution)/shard_map/ppermute | solution.py:35
  34.2 0.3 shard_map.116.home_ref
  34.5 2.5 %collective-permute-done.12.refs_0_ = bf16[24,1792]{1,0:T(8,128)(2,1)S(1)} collective-permute-done((bf16[24,1792]{1,0:T(8,128)(2,1)S(1)}, bf16[24,1792]{1,0:T(8,128)(2,1)S(1)}, u32[]{:S(2)}, u32[]{:S(2)}) %collective-permute-start.12) | collective-permute-done | bytes 86048 | tf_op jit(solution)/shard_map/ppermute | solution.py:35
  37.0 0.9 %shard_map.118 = (bf16[16,1792]{1,0:T(8,128)(2,1)}, bf16[16,1792]{1,0:T(8,128)(2,1)}) custom-call(bf16[32,1792]{1,0:T(8,128)(2,1)S(1)} %collective-permute-done.refs_0_.moved_ref, bf16[2,32,24]{2,1,0:T(8,128)(2,1)S(1)} %shard_map.116.home_ref, bf16[2,24,1792]{2,1,0:T(8,128)(2,1)S(1)} %get-tuple-element.44.own_ref, ...), custom_call_target="tpu_custom_call" | custom-call | bytes 573440 | tf_op jit(solution)/shard_map/pallas_call | solution.py:344
  (11 shorter events, 0.1 us)
Async XLA Ops:
  1.6 7.2 %collective-permute-start = (bf16[32,1792]{1,0:T(8,128)(2,1)S(1)}, bf16[32,1792]{1,0:T(8,128)(2,1)S(1)}, u32[]{:S(2)}, u32[]{:S(2)}) collective-permute-start(bf16[32,1792]{1,0:T(8,128)(2,1)S(1)} %get-tuple-element.25), channel_id=1, source_target_pairs={{0,16},{4,20},{8,24},{12,28},{16,0},{20,4},{24,8},{28,12},{1,17},{... | collective-permute-start | bytes 344072 | tf_op jit(solution)/shard_map/ppermute | solution.py:46
  4.6 4.8 %collective-permute-start.3 = (bf16[16,1920]{1,0:T(8,128)(2,1)S(1)}, bf16[16,1920]{1,0:T(8,128)(2,1)S(1)}, u32[]{:S(2)}, u32[]{:S(2)}) collective-permute-start(bf16[16,1920]{1,0:T(8,128)(2,1)S(1)} %get-tuple-element.32.refs_4_), channel_id=1, source_target_pairs={{0,8},{4,12},{8,0},{12,4},{1,9},{5,13},{9,1},{13,5},{2,10},{6,14},... | collective-permute-start | bytes 184328 | tf_op jit(solution)/shard_map/ppermute | solution.py:35
  6.2 5.7 %collective-permute-start.1 = (bf16[32,1792]{1,0:T(8,128)(2,1)S(1)}, bf16[32,1792]{1,0:T(8,128)(2,1)S(1)}, u32[]{:S(2)}, u32[]{:S(2)}) collective-permute-start(bf16[32,1792]{1,0:T(8,128)(2,1)S(1)} %get-tuple-element.25), channel_id=1, source_target_pairs={{0,24},{4,28},{8,16},{12,20},{16,8},{20,12},{24,0},{28,4},{1,25},{... | collective-permute-start | bytes 344072 | tf_op jit(solution)/shard_map/ppermute | solution.py:46
  8.8 3.0 %collective-permute-start.2 = (bf16[32,1792]{1,0:T(8,128)(2,1)S(1)}, bf16[32,1792]{1,0:T(8,128)(2,1)S(1)}, u32[]{:S(2)}, u32[]{:S(2)}) collective-permute-start(bf16[32,1792]{1,0:T(8,128)(2,1)S(1)} %collective-permute-done.refs_0_.moved_ref), channel_id=1, source_target_pairs={{0,4},{4,0},{8,12},{12,8},{1,5},{5,1},{9,13},{13,9},{2,6},{6,2},{1... | collective-permute-start | bytes 344072 | tf_op jit(solution)/shard_map/ppermute | solution.py:35
  8.9 2.9 %collective-permute-start.4 = (bf16[16,1920]{1,0:T(8,128)(2,1)S(1)}, bf16[16,1920]{1,0:T(8,128)(2,1)S(1)}, u32[]{:S(2)}, u32[]{:S(2)}) collective-permute-start(bf16[16,1920]{1,0:T(8,128)(2,1)S(1)} %get-tuple-element.32.refs_4_), channel_id=1, source_target_pairs={{0,4},{4,0},{8,12},{12,8},{1,5},{5,1},{9,13},{13,9},{2,6},{6,2},{1... | collective-permute-start | bytes 184328 | tf_op jit(solution)/shard_map/ppermute | solution.py:35
  9.4 2.4 %collective-permute-start.5 = (bf16[16,1920]{1,0:T(8,128)(2,1)S(1)}, bf16[16,1920]{1,0:T(8,128)(2,1)S(1)}, u32[]{:S(2)}, u32[]{:S(2)}) collective-permute-start(bf16[16,1920]{1,0:T(8,128)(2,1)S(1)} %collective-permute-done.3.refs_5_), channel_id=1, source_target_pairs={{0,4},{4,0},{8,12},{12,8},{1,5},{5,1},{9,13},{13,9},{2,6},{6,2},{1... | collective-permute-start | bytes 184328 | tf_op jit(solution)/shard_map/ppermute | solution.py:35
  11.9 1.4 %collective-permute-start.6 = (bf16[32,1792]{1,0:T(8,128)(2,1)S(1)}, bf16[32,1792]{1,0:T(8,128)(2,1)S(1)}, u32[]{:S(2)}, u32[]{:S(2)}) collective-permute-start(bf16[32,1792]{1,0:T(8,128)(2,1)S(1)} %collective-permute-done.1.refs_1_), channel_id=1, source_target_pairs={{0,4},{4,0},{8,12},{12,8},{1,5},{5,1},{9,13},{13,9},{2,6},{6,2},{1... | collective-permute-start | bytes 344072 | tf_op jit(solution)/shard_map/ppermute | solution.py:35
  14.7 6.7 %collective-permute-start.7 = (bf16[40,1408]{1,0:T(8,128)(2,1)S(1)}, bf16[40,1408]{1,0:T(8,128)(2,1)S(1)}, u32[]{:S(2)}, u32[]{:S(2)}) collective-permute-start(bf16[40,1408]{1,0:T(8,128)(2,1)S(1)} %get-tuple-element.42), channel_id=1, source_target_pairs={{0,1},{1,0},{2,3},{3,2},{4,5},{5,4},{6,7},{7,6},{8,9},{9,8},{10,11... | collective-permute-start | bytes 337928 | tf_op jit(solution)/shard_map/ppermute | solution.py:35
  16.4 7.1 %collective-permute-start.9 = (bf16[40,1152]{1,0:T(8,128)(2,1)S(1)}, bf16[40,1152]{1,0:T(8,128)(2,1)S(1)}, u32[]{:S(2)}, u32[]{:S(2)}) collective-permute-start(bf16[40,1152]{1,0:T(8,128)(2,1)S(1)} %get-tuple-element.43), channel_id=1, source_target_pairs={{0,2},{1,3},{2,0},{3,1},{4,6},{5,7},{6,4},{7,5},{8,10},{9,11},{10,... | collective-permute-start | bytes 276488 | tf_op jit(solution)/shard_map/ppermute | solution.py:35
  21.4 7.5 %collective-permute-start.8 = (bf16[40,1408]{1,0:T(8,128)(2,1)S(1)}, bf16[40,1408]{1,0:T(8,128)(2,1)S(1)}, u32[]{:S(2)}, u32[]{:S(2)}) collective-permute-start(bf16[40,1408]{1,0:T(8,128)(2,1)S(1)} %add_convert_fusion.fa_ref), channel_id=1, source_target_pairs={{0,2},{1,3},{2,0},{3,1},{4,6},{5,7},{6,4},{7,5},{8,10},{9,11},{10,... | collective-permute-start | bytes 337928 | tf_op jit(solution)/shard_map/ppermute | solution.py:35
  23.4 5.5 %collective-permute-start.10 = (bf16[40,1152]{1,0:T(8,128)(2,1)S(1)}, bf16[40,1152]{1,0:T(8,128)(2,1)S(1)}, u32[]{:S(2)}, u32[]{:S(2)}) collective-permute-start(bf16[40,1152]{1,0:T(8,128)(2,1)S(1)} %add_convert_fusion.1.ba_ref), channel_id=1, source_target_pairs={{0,1},{1,0},{2,3},{3,2},{4,5},{5,4},{6,7},{7,6},{8,9},{9,8},{10,11... | collective-permute-start | bytes 276488 | tf_op jit(solution)/shard_map/ppermute | solution.py:35
  28.9 5.3 %copy-start = (s32[1,16,1]{1,2,0:T(1,128)S(1)}, s32[1,16,1]{1,2,0:T(1,128)}, u32[]{:S(2)}) copy-start(s32[1,16,1]{1,2,0:T(1,128)} %param.13) | copy-start | bytes 196
  28.9 5.3 %copy-start.1 = (bf16[1,16,1]{1,2,0:T(2,128)(2,1)S(1)}, bf16[1,16,1]{1,2,0:T(2,128)(2,1)}, u32[]{:S(2)}) copy-start(bf16[1,16,1]{1,2,0:T(2,128)(2,1)} %param.14) | copy-start | bytes 100
  28.9 5.3 %copy-start.2 = (s32[1,16,1]{1,2,0:T(1,128)S(1)}, s32[1,16,1]{1,2,0:T(1,128)}, u32[]{:S(2)}) copy-start(s32[1,16,1]{1,2,0:T(1,128)} %param.15) | copy-start | bytes 196
  28.9 5.3 %copy-start.3 = (bf16[1,16,1]{1,2,0:T(2,128)(2,1)S(1)}, bf16[1,16,1]{1,2,0:T(2,128)(2,1)}, u32[]{:S(2)}) copy-start(bf16[1,16,1]{1,2,0:T(2,128)(2,1)} %param.16) | copy-start | bytes 100
  30.7 1.5 %collective-permute-start.11 = (bf16[2,24,1792]{2,1,0:T(8,128)(2,1)S(1)}, bf16[2,24,1792]{2,1,0:T(8,128)(2,1)S(1)}, u32[]{:S(2)}, u32[]{:S(2)}) collective-permute-start(bf16[2,24,1792]{2,1,0:T(8,128)(2,1)S(1)} %get-tuple-element.45), channel_id=1, source_target_pairs={{0,4},{4,0},{8,12},{12,8},{1,5},{5,1},{9,13},{13,9},{2,6},{6,2},{1... | collective-permute-start | bytes 516104 | tf_op jit(solution)/shard_map/ppermute | solution.py:35
  32.2 4.9 %collective-permute-start.12 = (bf16[24,1792]{1,0:T(8,128)(2,1)S(1)}, bf16[24,1792]{1,0:T(8,128)(2,1)S(1)}, u32[]{:S(2)}, u32[]{:S(2)}) collective-permute-start(bf16[24,1792]{1,0:T(8,128)(2,1)S(1)} %fusion), channel_id=1, source_target_pairs={{0,8},{4,12},{8,0},{12,4},{1,9},{5,13},{9,1},{13,5},{2,10},{6,14},... | collective-permute-start | bytes 258056 | tf_op jit(solution)/shard_map/ppermute | solution.py:35

commit v7 on v6

--- a/solution.py
+++ b/solution.py
@@ -33,6 +33,17 @@
 def swap(x, axis, bit):
     peers = lax.axis_size(axis)
     return lax.ppermute(x, axis, [(i, i ^ bit) for i in range(peers)])
+
+
+def mixed(x, even, odd):
+    peers = lax.axis_size("expert")
+    parts = lax.axis_size("dp")
+    pairs = [
+        (i * parts + k, i * parts + (k ^ (odd if i % 2 else even)))
+        for i in range(peers)
+        for k in range(parts)
+    ]
+    return lax.ppermute(x, ("expert", "dp"), pairs)
 
 
 def onward(x, bit):
@@ -257,7 +268,7 @@
     topk = routes_forward.shape[2]
     capacity = min(held, max(6, held * topk // experts + 2))
     rows = -(-peers * capacity // 8) * 8
-    cut = hidden * 3 // 4
+    cut = hidden * 2 // 4
     slot_rows = -(-2 * capacity // 8) * 8
     weight_bytes = 6 * width * hidden
     w_g, w_u, w_d = pl.pallas_call(
@@ -316,8 +327,8 @@
     bits = [1 << i for i in range(lax.axis_size("dp").bit_length() - 1)]
     last = bits[-1]
     for up, down in zip(bits, bits[::-1]):
-        came_f = swap(part_f, "dp", up)
-        came_b = swap(part_b, "dp", down)
+        came_f = mixed(part_f, up, down)
+        came_b = mixed(part_b, up, down)
         if up == last:
             break
         part_f = (part_f.astype(F32) + came_f.astype(F32)).astype(BF16)

time: 38.1 us -> 37.6 us (0.987)
  starting transfers between devices: 15.5 us -> 13 us
  waiting for transfers between devices: 13.6 us -> 15.6 us
    ppermute x11 -> x7, starting transfers between devices: 12.5 us -> 4.32 us  [swap(): return lax.ppermute(x, axis, [(i, i ^ bit) for i in range(peers)])]
    ppermute x0 -> x4, waiting for transfers between devices: none -> 7.98 us  [mixed(): return lax.ppermute(x, ('expert', 'dp'), pairs)]
    ppermute x11 -> x7, waiting for transfers between devices: 11.2 us -> 5.26 us  [swap(): return lax.ppermute(x, axis, [(i, i ^ bit) for i in range(peers)])]
    ppermute x0 -> x4, starting transfers between devices: none -> 5.68 us  [mixed(): return lax.ppermute(x, ('expert', 'dp'), pairs)]
  transfers between devices with their start and end apart: 13 -> 13, of which waited for: 6 -> 8; matrix products, arithmetic and copies ran while one was open for 0% -> 0% of each run, Pallas kernels for 8% -> 8%
where the time goes in v7:
time: 37.6 us; the launch traced here: 37.4 us
  waiting for transfers between devices  15.6 us (41%)
  starting transfers between devices  13 us (35%)
  Pallas kernels  7.96 us (21%)
  between operations  0.73 us (2%)
    ppermute x4, waiting for transfers between devices, mixed(): return lax.ppermute(x, ('expert', 'dp'), pairs)  7.98 us
    ppermute x4, starting transfers between devices, mixed(): return lax.ppermute(x, ('expert', 'dp'), pairs)  5.68 us
    ppermute x7, waiting for transfers between devices, swap(): return lax.ppermute(x, axis, [(i, i ^ bit) for i in range(peers)])  5.26 us
    ppermute x7, starting transfers between devices, swap(): return lax.ppermute(x, axis, [(i, i ^ bit) for i in range(peers)])  4.32 us
    ppermute x2, starting transfers between devices, onward(): return lax.ppermute(x, ('pipe', 'expert'), pairs)  3.02 us
    pallas_call x1, Pallas kernels, local(): pl.pallas_call(fetch_kernel, out_shape=[pltpu.VMEM(w.shape[2:], BF16) for...  2.63 us
    ppermute x2, waiting for transfers between devices, onward(): return lax.ppermute(x, ('pipe', 'expert'), pairs)  2.36 us
    pallas_call x1, Pallas kernels, local(): kernel_call(functools.partial(down_kernel, groups, rows), [jax.ShapeDtype...  1.73 us
  transfers between devices with their start and end apart: 13, of which 8 were waited for; matrix products, arithmetic and copies ran while one was open for 0% of the time, Pallas kernels for 8%

profile of v7, /device:TPU:0, one launch (start us, length us, event | category | flops | bytes accessed | tf_op | source)
XLA Modules:
  0.0 37.4 jit_solution(3415423883341203646)
XLA Ops:
  0.6 1.0 %shard_map.113 = (bf16[32,1792]{1,0:T(8,128)(2,1)S(1)}, bf16[16,1920]{1,0:T(8,128)(2,1)S(1)}) custom-call(bf16[16,1792]{1,0:T(8,128)(2,1)} %bitcast.25, bf16[16,1792]{1,0:T(8,128)(2,1)} %bitcast.26, bf16[16,1792]{1,0:T(8,128)(2,1)} %bitcast.27, s32[1,16]{1,0:T(1,128)} %bitcast.14, bf16[1,16]{1,0:T(2,128)(2,1)} %bitcast.16, s32[1,16]{1,0:T(1,128)} %bitcast.18, ...), custom_call_target="tpu_custom_call" | custom-call | bytes 344064 | tf_op jit(solution)/shard_map/pallas_call | solution.py:288
  1.6 3.0 %collective-permute-start = (bf16[32,1792]{1,0:T(8,128)(2,1)S(1)}, bf16[32,1792]{1,0:T(8,128)(2,1)S(1)}, u32[]{:S(2)}, u32[]{:S(2)}) collective-permute-start(bf16[32,1792]{1,0:T(8,128)(2,1)S(1)} %get-tuple-element.25), channel_id=1, source_target_pairs={{0,16},{4,20},{8,24},{12,28},{16,0},{20,4},{24,8},{28,12},{1,17},{... | collective-permute-start | bytes 344072 | tf_op jit(solution)/shard_map/ppermute | solution.py:57
  4.6 1.5 %collective-permute-start.3 = (bf16[16,1920]{1,0:T(8,128)(2,1)S(1)}, bf16[16,1920]{1,0:T(8,128)(2,1)S(1)}, u32[]{:S(2)}, u32[]{:S(2)}) collective-permute-start(bf16[16,1920]{1,0:T(8,128)(2,1)S(1)} %get-tuple-element.32.refs_4_), channel_id=1, source_target_pairs={{0,8},{4,12},{8,0},{12,4},{1,9},{5,13},{9,1},{13,5},{2,10},{6,14},... | collective-permute-start | bytes 184328 | tf_op jit(solution)/shard_map/ppermute | solution.py:35
  6.2 0.0 collective-permute-start.1
  6.2 2.6 %shard_map.114 = (bf16[1792,512]{1,0:T(8,128)(2,1)S(1)}, bf16[1792,512]{1,0:T(8,128)(2,1)S(1)}, bf16[512,1792]{1,0:T(8,128)(2,1)S(1)}) custom-call(bf16[1792,512]{1,0:T(8,128)(2,1)} %bitcast.22, bf16[1792,512]{1,0:T(8,128)(2,1)} %bitcast.23, bf16[512,1792]{1,0:T(8,128)(2,1)} %bitcast.24), custom_call_target="tpu_custom_call" | custom-call | bytes 11010048 | tf_op jit(solution)/shard_map/pallas_call | solution.py:274
  8.8 0.0 collective-permute-done.refs_0_.moved_ref
  8.8 0.1 collective-permute-start.2
  8.9 0.5 %collective-permute-start.4 = (bf16[16,1920]{1,0:T(8,128)(2,1)S(1)}, bf16[16,1920]{1,0:T(8,128)(2,1)S(1)}, u32[]{:S(2)}, u32[]{:S(2)}) collective-permute-start(bf16[16,1920]{1,0:T(8,128)(2,1)S(1)} %get-tuple-element.32.refs_4_), channel_id=1, source_target_pairs={{0,4},{4,0},{8,12},{12,8},{1,5},{5,1},{9,13},{13,9},{2,6},{6,2},{1... | collective-permute-start | bytes 184328 | tf_op jit(solution)/shard_map/ppermute | solution.py:35
  9.4 0.0 collective-permute-done.3.refs_5_
  9.4 0.1 collective-permute-start.5
  9.5 2.4 %collective-permute-done.1.refs_1_ = bf16[32,1792]{1,0:T(8,128)(2,1)S(1)} collective-permute-done((bf16[32,1792]{1,0:T(8,128)(2,1)S(1)}, bf16[32,1792]{1,0:T(8,128)(2,1)S(1)}, u32[]{:S(2)}, u32[]{:S(2)}) %collective-permute-start.1) | collective-permute-done | bytes 114720 | tf_op jit(solution)/shard_map/ppermute | solution.py:57
  11.9 0.0 collective-permute-done.4.refs_6_
  11.9 0.0 collective-permute-done.5.refs_7_
  11.9 0.0 collective-permute-done.2.refs_2_
  11.9 0.1 collective-permute-start.6
  11.9 1.3 %collective-permute-done.6.refs_3_ = bf16[32,1792]{1,0:T(8,128)(2,1)S(1)} collective-permute-done((bf16[32,1792]{1,0:T(8,128)(2,1)S(1)}, bf16[32,1792]{1,0:T(8,128)(2,1)S(1)}, u32[]{:S(2)}, u32[]{:S(2)}) %collective-permute-start.6) | collective-permute-done | bytes 114720 | tf_op jit(solution)/shard_map/ppermute | solution.py:35
  13.3 1.4 %shard_map.115 = (bf16[40,1280]{1,0:T(8,128)(2,1)S(1)}, bf16[40,1280]{1,0:T(8,128)(2,1)S(1)}, bf16[96,80]{1,0:T(8,128)(2,1)S(1)}) custom-call(bf16[32,1792]{1,0:T(8,128)(2,1)S(1)} %collective-permute-done.refs_0_.moved_ref, bf16[32,1792]{1,0:T(8,128)(2,1)S(1)} %collective-permute-done.1.refs_1_, bf16[32,1792]{1,0:T(8,128)(2,1)S(1)} %collective-permute-done.2.refs_2_, ...), custom_call_target="tpu_custom_call" | custom-call | flops 367001600 | bytes 5505024 | tf_op jit(solution)/shard_map/pallas_call | solution.py:317
  14.7 1.6 %collective-permute-start.7 = (bf16[40,1280]{1,0:T(8,128)(2,1)S(1)}, bf16[40,1280]{1,0:T(8,128)(2,1)S(1)}, u32[]{:S(2)}, u32[]{:S(2)}) collective-permute-start(bf16[40,1280]{1,0:T(8,128)(2,1)S(1)} %get-tuple-element.42), channel_id=1, source_target_pairs={{0,1},{1,0},{2,3},{3,2},{4,6},{5,7},{6,4},{7,5},{8,9},{9,8},{10,11... | collective-permute-start | bytes 307208 | tf_op jit(solution)/shard_map/ppermute | solution.py:46
  16.3 0.5 %collective-permute-start.9 = (bf16[40,1280]{1,0:T(8,128)(2,1)S(1)}, bf16[40,1280]{1,0:T(8,128)(2,1)S(1)}, u32[]{:S(2)}, u32[]{:S(2)}) collective-permute-start(bf16[40,1280]{1,0:T(8,128)(2,1)S(1)} %get-tuple-element.43), channel_id=1, source_target_pairs={{0,1},{1,0},{2,3},{3,2},{4,6},{5,7},{6,4},{7,5},{8,9},{9,8},{10,11... | collective-permute-start | bytes 307208 | tf_op jit(solution)/shard_map/ppermute | solution.py:46
  16.8 3.7 %collective-permute-done.7 = bf16[40,1280]{1,0:T(8,128)(2,1)S(1)} collective-permute-done((bf16[40,1280]{1,0:T(8,128)(2,1)S(1)}, bf16[40,1280]{1,0:T(8,128)(2,1)S(1)}, u32[]{:S(2)}, u32[]{:S(2)}) %collective-permute-start.7) | collective-permute-done | bytes 102432 | tf_op jit(solution)/shard_map/ppermute | solution.py:46
  20.5 1.8 %collective-permute-start.8 = (bf16[40,1280]{1,0:T(8,128)(2,1)S(1)}, bf16[40,1280]{1,0:T(8,128)(2,1)S(1)}, u32[]{:S(2)}, u32[]{:S(2)}) collective-permute-start(bf16[40,1280]{1,0:T(8,128)(2,1)S(1)} %add_convert_fusion.1.fa_ref), channel_id=1, source_target_pairs={{0,2},{1,3},{2,0},{3,1},{4,5},{5,4},{6,7},{7,6},{8,10},{9,11},{10,... | collective-permute-start | bytes 307208 | tf_op jit(solution)/shard_map/ppermute | solution.py:46
  22.3 0.4 %collective-permute-done.9 = bf16[40,1280]{1,0:T(8,128)(2,1)S(1)} collective-permute-done((bf16[40,1280]{1,0:T(8,128)(2,1)S(1)}, bf16[40,1280]{1,0:T(8,128)(2,1)S(1)}, u32[]{:S(2)}, u32[]{:S(2)}) %collective-permute-start.9) | collective-permute-done | bytes 102432 | tf_op jit(solution)/shard_map/ppermute | solution.py:46
  22.8 1.8 %collective-permute-start.10 = (bf16[40,1280]{1,0:T(8,128)(2,1)S(1)}, bf16[40,1280]{1,0:T(8,128)(2,1)S(1)}, u32[]{:S(2)}, u32[]{:S(2)}) collective-permute-start(bf16[40,1280]{1,0:T(8,128)(2,1)S(1)} %add_convert_fusion.ba_ref), channel_id=1, source_target_pairs={{0,2},{1,3},{2,0},{3,1},{4,5},{5,4},{6,7},{7,6},{8,10},{9,11},{10,... | collective-permute-start | bytes 307208 | tf_op jit(solution)/shard_map/ppermute | solution.py:46
  24.6 1.8 %collective-permute-done.8.fb_ref = bf16[40,1280]{1,0:T(8,128)(2,1)S(1)} collective-permute-done((bf16[40,1280]{1,0:T(8,128)(2,1)S(1)}, bf16[40,1280]{1,0:T(8,128)(2,1)S(1)}, u32[]{:S(2)}, u32[]{:S(2)}) %collective-permute-start.8) | collective-permute-done | bytes 102432 | tf_op jit(solution)/shard_map/ppermute | solution.py:46
  26.4 2.0 %collective-permute-done.10.bb_ref = bf16[40,1280]{1,0:T(8,128)(2,1)S(1)} collective-permute-done((bf16[40,1280]{1,0:T(8,128)(2,1)S(1)}, bf16[40,1280]{1,0:T(8,128)(2,1)S(1)}, u32[]{:S(2)}, u32[]{:S(2)}) %collective-permute-start.10) | collective-permute-done | bytes 102432 | tf_op jit(solution)/shard_map/ppermute | solution.py:46
  28.4 1.7 %shard_map.117 = (bf16[2,24,1792]{2,1,0:T(8,128)(2,1)S(1)}, bf16[2,24,1792]{2,1,0:T(8,128)(2,1)S(1)}) custom-call(bf16[40,1280]{1,0:T(8,128)(2,1)S(1)} %add_convert_fusion.1.fa_ref, bf16[40,1280]{1,0:T(8,128)(2,1)S(1)} %collective-permute-done.8.fb_ref, bf16[40,1280]{1,0:T(8,128)(2,1)S(1)} %add_convert_fusion.ba_ref, ...), custom_call_target="tpu_custom_call" | custom-call | flops 220200960 | bytes 5505024 | tf_op jit(solution)/shard_map/pallas_call | solution.py:336
  30.2 0.1 collective-permute-start.11
  30.3 1.4 %collective-permute-done.11.other_ref = bf16[2,24,1792]{2,1,0:T(8,128)(2,1)S(1)} collective-permute-done((bf16[2,24,1792]{2,1,0:T(8,128)(2,1)S(1)}, bf16[2,24,1792]{2,1,0:T(8,128)(2,1)S(1)}, u32[]{:S(2)}, u32[]{:S(2)}) %collective-permute-start.11) | collective-permute-done | bytes 172064 | tf_op jit(solution)/shard_map/ppermute | solution.py:35
  31.7 2.0 %collective-permute-start.12 = (bf16[24,1792]{1,0:T(8,128)(2,1)S(1)}, bf16[24,1792]{1,0:T(8,128)(2,1)S(1)}, u32[]{:S(2)}, u32[]{:S(2)}) collective-permute-start(bf16[24,1792]{1,0:T(8,128)(2,1)S(1)} %fusion), channel_id=1, source_target_pairs={{0,8},{4,12},{8,0},{12,4},{1,9},{5,13},{9,1},{13,5},{2,10},{6,14},... | collective-permute-start | bytes 258056 | tf_op jit(solution)/shard_map/ppermute | solution.py:35
  33.7 0.3 shard_map.116.home_ref
  34.0 2.5 %collective-permute-done.12.refs_0_ = bf16[24,1792]{1,0:T(8,128)(2,1)S(1)} collective-permute-done((bf16[24,1792]{1,0:T(8,128)(2,1)S(1)}, bf16[24,1792]{1,0:T(8,128)(2,1)S(1)}, u32[]{:S(2)}, u32[]{:S(2)}) %collective-permute-start.12) | collective-permute-done | bytes 86048 | tf_op jit(solution)/shard_map/ppermute | solution.py:35
  36.5 0.9 %shard_map.118 = (bf16[16,1792]{1,0:T(8,128)(2,1)}, bf16[16,1792]{1,0:T(8,128)(2,1)}) custom-call(bf16[32,1792]{1,0:T(8,128)(2,1)S(1)} %collective-permute-done.refs_0_.moved_ref, bf16[2,32,24]{2,1,0:T(8,128)(2,1)S(1)} %shard_map.116.home_ref, bf16[2,24,1792]{2,1,0:T(8,128)(2,1)S(1)} %get-tuple-element.44.own_ref, ...), custom_call_target="tpu_custom_call" | custom-call | bytes 573440 | tf_op jit(solution)/shard_map/pallas_call | solution.py:355
  (11 shorter events, 0.1 us)
Async XLA Ops:
  1.6 7.2 %collective-permute-start = (bf16[32,1792]{1,0:T(8,128)(2,1)S(1)}, bf16[32,1792]{1,0:T(8,128)(2,1)S(1)}, u32[]{:S(2)}, u32[]{:S(2)}) collective-permute-start(bf16[32,1792]{1,0:T(8,128)(2,1)S(1)} %get-tuple-element.25), channel_id=1, source_target_pairs={{0,16},{4,20},{8,24},{12,28},{16,0},{20,4},{24,8},{28,12},{1,17},{... | collective-permute-start | bytes 344072 | tf_op jit(solution)/shard_map/ppermute | solution.py:57
  4.6 4.8 %collective-permute-start.3 = (bf16[16,1920]{1,0:T(8,128)(2,1)S(1)}, bf16[16,1920]{1,0:T(8,128)(2,1)S(1)}, u32[]{:S(2)}, u32[]{:S(2)}) collective-permute-start(bf16[16,1920]{1,0:T(8,128)(2,1)S(1)} %get-tuple-element.32.refs_4_), channel_id=1, source_target_pairs={{0,8},{4,12},{8,0},{12,4},{1,9},{5,13},{9,1},{13,5},{2,10},{6,14},... | collective-permute-start | bytes 184328 | tf_op jit(solution)/shard_map/ppermute | solution.py:35
  6.2 5.7 %collective-permute-start.1 = (bf16[32,1792]{1,0:T(8,128)(2,1)S(1)}, bf16[32,1792]{1,0:T(8,128)(2,1)S(1)}, u32[]{:S(2)}, u32[]{:S(2)}) collective-permute-start(bf16[32,1792]{1,0:T(8,128)(2,1)S(1)} %get-tuple-element.25), channel_id=1, source_target_pairs={{0,24},{4,28},{8,16},{12,20},{16,8},{20,12},{24,0},{28,4},{1,25},{... | collective-permute-start | bytes 344072 | tf_op jit(solution)/shard_map/ppermute | solution.py:57
  8.8 3.0 %collective-permute-start.2 = (bf16[32,1792]{1,0:T(8,128)(2,1)S(1)}, bf16[32,1792]{1,0:T(8,128)(2,1)S(1)}, u32[]{:S(2)}, u32[]{:S(2)}) collective-permute-start(bf16[32,1792]{1,0:T(8,128)(2,1)S(1)} %collective-permute-done.refs_0_.moved_ref), channel_id=1, source_target_pairs={{0,4},{4,0},{8,12},{12,8},{1,5},{5,1},{9,13},{13,9},{2,6},{6,2},{1... | collective-permute-start | bytes 344072 | tf_op jit(solution)/shard_map/ppermute | solution.py:35
  8.9 2.9 %collective-permute-start.4 = (bf16[16,1920]{1,0:T(8,128)(2,1)S(1)}, bf16[16,1920]{1,0:T(8,128)(2,1)S(1)}, u32[]{:S(2)}, u32[]{:S(2)}) collective-permute-start(bf16[16,1920]{1,0:T(8,128)(2,1)S(1)} %get-tuple-element.32.refs_4_), channel_id=1, source_target_pairs={{0,4},{4,0},{8,12},{12,8},{1,5},{5,1},{9,13},{13,9},{2,6},{6,2},{1... | collective-permute-start | bytes 184328 | tf_op jit(solution)/shard_map/ppermute | solution.py:35
  9.4 2.4 %collective-permute-start.5 = (bf16[16,1920]{1,0:T(8,128)(2,1)S(1)}, bf16[16,1920]{1,0:T(8,128)(2,1)S(1)}, u32[]{:S(2)}, u32[]{:S(2)}) collective-permute-start(bf16[16,1920]{1,0:T(8,128)(2,1)S(1)} %collective-permute-done.3.refs_5_), channel_id=1, source_target_pairs={{0,4},{4,0},{8,12},{12,8},{1,5},{5,1},{9,13},{13,9},{2,6},{6,2},{1... | collective-permute-start | bytes 184328 | tf_op jit(solution)/shard_map/ppermute | solution.py:35
  11.9 1.4 %collective-permute-start.6 = (bf16[32,1792]{1,0:T(8,128)(2,1)S(1)}, bf16[32,1792]{1,0:T(8,128)(2,1)S(1)}, u32[]{:S(2)}, u32[]{:S(2)}) collective-permute-start(bf16[32,1792]{1,0:T(8,128)(2,1)S(1)} %collective-permute-done.1.refs_1_), channel_id=1, source_target_pairs={{0,4},{4,0},{8,12},{12,8},{1,5},{5,1},{9,13},{13,9},{2,6},{6,2},{1... | collective-permute-start | bytes 344072 | tf_op jit(solution)/shard_map/ppermute | solution.py:35
  14.7 5.8 %collective-permute-start.7 = (bf16[40,1280]{1,0:T(8,128)(2,1)S(1)}, bf16[40,1280]{1,0:T(8,128)(2,1)S(1)}, u32[]{:S(2)}, u32[]{:S(2)}) collective-permute-start(bf16[40,1280]{1,0:T(8,128)(2,1)S(1)} %get-tuple-element.42), channel_id=1, source_target_pairs={{0,1},{1,0},{2,3},{3,2},{4,6},{5,7},{6,4},{7,5},{8,9},{9,8},{10,11... | collective-permute-start | bytes 307208 | tf_op jit(solution)/shard_map/ppermute | solution.py:46
  16.3 6.4 %collective-permute-start.9 = (bf16[40,1280]{1,0:T(8,128)(2,1)S(1)}, bf16[40,1280]{1,0:T(8,128)(2,1)S(1)}, u32[]{:S(2)}, u32[]{:S(2)}) collective-permute-start(bf16[40,1280]{1,0:T(8,128)(2,1)S(1)} %get-tuple-element.43), channel_id=1, source_target_pairs={{0,1},{1,0},{2,3},{3,2},{4,6},{5,7},{6,4},{7,5},{8,9},{9,8},{10,11... | collective-permute-start | bytes 307208 | tf_op jit(solution)/shard_map/ppermute | solution.py:46
  20.5 5.9 %collective-permute-start.8 = (bf16[40,1280]{1,0:T(8,128)(2,1)S(1)}, bf16[40,1280]{1,0:T(8,128)(2,1)S(1)}, u32[]{:S(2)}, u32[]{:S(2)}) collective-permute-start(bf16[40,1280]{1,0:T(8,128)(2,1)S(1)} %add_convert_fusion.1.fa_ref), channel_id=1, source_target_pairs={{0,2},{1,3},{2,0},{3,1},{4,5},{5,4},{6,7},{7,6},{8,10},{9,11},{10,... | collective-permute-start | bytes 307208 | tf_op jit(solution)/shard_map/ppermute | solution.py:46
  22.8 5.7 %collective-permute-start.10 = (bf16[40,1280]{1,0:T(8,128)(2,1)S(1)}, bf16[40,1280]{1,0:T(8,128)(2,1)S(1)}, u32[]{:S(2)}, u32[]{:S(2)}) collective-permute-start(bf16[40,1280]{1,0:T(8,128)(2,1)S(1)} %add_convert_fusion.ba_ref), channel_id=1, source_target_pairs={{0,2},{1,3},{2,0},{3,1},{4,5},{5,4},{6,7},{7,6},{8,10},{9,11},{10,... | collective-permute-start | bytes 307208 | tf_op jit(solution)/shard_map/ppermute | solution.py:46
  28.4 5.3 %copy-start = (s32[1,16,1]{1,2,0:T(1,128)S(1)}, s32[1,16,1]{1,2,0:T(1,128)}, u32[]{:S(2)}) copy-start(s32[1,16,1]{1,2,0:T(1,128)} %param.13) | copy-start | bytes 196
  28.4 5.3 %copy-start.1 = (bf16[1,16,1]{1,2,0:T(2,128)(2,1)S(1)}, bf16[1,16,1]{1,2,0:T(2,128)(2,1)}, u32[]{:S(2)}) copy-start(bf16[1,16,1]{1,2,0:T(2,128)(2,1)} %param.14) | copy-start | bytes 100
  28.4 5.3 %copy-start.2 = (s32[1,16,1]{1,2,0:T(1,128)S(1)}, s32[1,16,1]{1,2,0:T(1,128)}, u32[]{:S(2)}) copy-start(s32[1,16,1]{1,2,0:T(1,128)} %param.15) | copy-start | bytes 196
  28.4 5.3 %copy-start.3 = (bf16[1,16,1]{1,2,0:T(2,128)(2,1)S(1)}, bf16[1,16,1]{1,2,0:T(2,128)(2,1)}, u32[]{:S(2)}) copy-start(bf16[1,16,1]{1,2,0:T(2,128)(2,1)} %param.16) | copy-start | bytes 100
  30.2 1.5 %collective-permute-start.11 = (bf16[2,24,1792]{2,1,0:T(8,128)(2,1)S(1)}, bf16[2,24,1792]{2,1,0:T(8,128)(2,1)S(1)}, u32[]{:S(2)}, u32[]{:S(2)}) collective-permute-start(bf16[2,24,1792]{2,1,0:T(8,128)(2,1)S(1)} %get-tuple-element.45), channel_id=1, source_target_pairs={{0,4},{4,0},{8,12},{12,8},{1,5},{5,1},{9,13},{13,9},{2,6},{6,2},{1... | collective-permute-start | bytes 516104 | tf_op jit(solution)/shard_map/ppermute | solution.py:35
  31.7 4.9 %collective-permute-start.12 = (bf16[24,1792]{1,0:T(8,128)(2,1)S(1)}, bf16[24,1792]{1,0:T(8,128)(2,1)S(1)}, u32[]{:S(2)}, u32[]{:S(2)}) collective-permute-start(bf16[24,1792]{1,0:T(8,128)(2,1)S(1)} %fusion), channel_id=1, source_target_pairs={{0,8},{4,12},{8,0},{12,4},{1,9},{5,13},{9,1},{13,5},{2,10},{6,14},... | collective-permute-start | bytes 258056 | tf_op jit(solution)/shard_map/ppermute | solution.py:35

commit v8 on v7

--- a/solution.py
+++ b/solution.py
@@ -199,6 +199,14 @@
     part_b_ref[...] = jnp.concatenate([gate[rows:], upper[rows:], dhid[:, cut:]], axis=1).astype(BF16)
 
 
+def out_kernel(a_ref, b_ref, w_d_ref, out_ref):
+    units = w_d_ref.shape[0]
+    gate = a_ref[:, :units].astype(F32) + b_ref[:, :units].astype(F32)
+    upper = a_ref[:, units : 2 * units].astype(F32) + b_ref[:, units : 2 * units].astype(F32)
+    hidden = (gate * jax.nn.sigmoid(gate) * upper).astype(BF16)
+    out_ref[...] = jnp.dot(hidden, w_d_ref[...], preferred_element_type=F32)
+
+
 def down_kernel(
     groups,
     rows,
@@ -206,29 +214,26 @@
     fb_ref,
     ba_ref,
     bb_ref,
+    out_ref,
     slot_ref,
     w_g_ref,
     w_u_ref,
-    w_d_ref,
     own_ref,
     other_ref,
 ):
-    total_f = fa_ref[...].astype(F32) + fb_ref[...].astype(F32)
+    units = w_g_ref.shape[1]
     total_b = ba_ref[...].astype(F32) + bb_ref[...].astype(F32)
-    units = w_d_ref.shape[0]
-    gate_f, upper_f = total_f[:, :units], total_f[:, units : 2 * units]
+    part_f = fa_ref[:, 2 * units :].astype(F32) + fb_ref[:, 2 * units :].astype(F32)
     gate_b, upper_b = total_b[:, :units], total_b[:, units : 2 * units]
-    dhid = jnp.concatenate([total_f[:, 2 * units :], total_b[:, 2 * units :]], axis=1)
-    hidden = (gate_f * jax.nn.sigmoid(gate_f) * upper_f).astype(BF16)
+    dhid = jnp.concatenate([part_f, total_b[:, 2 * units :]], axis=1)
     sigma = jax.nn.sigmoid(gate_b)
     slope = sigma * (1.0 + gate_b * (1.0 - sigma))
     dgate = (dhid * upper_b * slope).astype(BF16)
     dupper = (dhid * (gate_b * sigma)).astype(BF16)
     turned = (((1,), (1,)), ((), ()))
-    out_f = jnp.dot(hidden, w_d_ref[...], preferred_element_type=F32)
     grad = lax.dot_general(dgate, w_g_ref[...], turned, preferred_element_type=F32)
     grad = grad + lax.dot_general(dupper, w_u_ref[...], turned, preferred_element_type=F32)
-    both = jnp.concatenate([out_f, grad], axis=0).astype(BF16)
+    both = jnp.concatenate([out_ref[...], grad], axis=0).astype(BF16)
     full = jnp.dot(slot_ref[...], both, preferred_element_type=F32)
     slot_rows = own_ref.shape[1]
     for d in range(groups):
@@ -333,12 +338,18 @@
             break
         part_f = (part_f.astype(F32) + came_f.astype(F32)).astype(BF16)
         part_b = (part_b.astype(F32) + came_b.astype(F32)).astype(BF16)
+    out_f = kernel_call(
+        out_kernel,
+        jax.ShapeDtypeStruct((rows, width), F32),
+        2 * rows * width * hidden,
+        2 * width * hidden,
+    )(part_f, came_f, w_d)
     own, other = kernel_call(
         functools.partial(down_kernel, groups, rows),
         [jax.ShapeDtypeStruct((groups, slot_rows, width), BF16)] * 2,
-        6 * rows * width * hidden,
-        weight_bytes,
-    )(part_f, came_f, part_b, came_b, slot, w_g, w_u, w_d)
+        4 * rows * width * hidden,
+        4 * width * hidden,
+    )(part_f, came_f, part_b, came_b, out_f, slot, w_g, w_u)
     other = swap(other, "expert", 1)
     came = []
     for d in range(1, groups):

time: 37.6 us -> 37.2 us (0.989)
  waiting for transfers between devices: 15.6 us -> 15.2 us
    pallas_call x0 -> x1, Pallas kernels: none -> 0.4 us  [local(): kernel_call(out_kernel, jax.ShapeDtypeStruct((rows, width), F32), 2 * row...]
    ppermute x4, waiting for transfers between devices: 7.98 us -> 7.57 us  [mixed(): return lax.ppermute(x, ('expert', 'dp'), pairs)]
  transfers between devices with their start and end apart: 13 -> 13, of which waited for: 8 -> 8; matrix products, arithmetic and copies ran while one was open for 0% -> 0% of each run, Pallas kernels for 8% -> 9%
where the time goes in v8:
time: 37.2 us; the launch traced here: 37 us
  waiting for transfers between devices  15.2 us (41%)
  starting transfers between devices  13 us (35%)
  Pallas kernels  8 us (22%)
  between operations  0.73 us (2%)
    ppermute x4, waiting for transfers between devices, mixed(): return lax.ppermute(x, ('expert', 'dp'), pairs)  7.57 us
    ppermute x4, starting transfers between devices, mixed(): return lax.ppermute(x, ('expert', 'dp'), pairs)  5.68 us
    ppermute x7, waiting for transfers between devices, swap(): return lax.ppermute(x, axis, [(i, i ^ bit) for i in range(peers)])  5.26 us
    ppermute x7, starting transfers between devices, swap(): return lax.ppermute(x, axis, [(i, i ^ bit) for i in range(peers)])  4.32 us
    ppermute x2, starting transfers between devices, onward(): return lax.ppermute(x, ('pipe', 'expert'), pairs)  3.02 us
    pallas_call x1, Pallas kernels, local(): pl.pallas_call(fetch_kernel, out_shape=[pltpu.VMEM(w.shape[2:], BF16) for...  2.63 us
    ppermute x2, waiting for transfers between devices, onward(): return lax.ppermute(x, ('pipe', 'expert'), pairs)  2.36 us
    pallas_call x1, Pallas kernels, local(): kernel_call(functools.partial(up_kernel, groups, topk, rows, capacity, sl...  1.44 us
  transfers between devices with their start and end apart: 13, of which 8 were waited for; matrix products, arithmetic and copies ran while one was open for 0% of the time, Pallas kernels for 9%

profile of v8, /device:TPU:0, one launch (start us, length us, event | category | flops | bytes accessed | tf_op | source)
XLA Modules:
  0.0 37.0 jit_solution(15055168838672264635)
XLA Ops:
  0.6 1.0 %shard_map.113 = (bf16[32,1792]{1,0:T(8,128)(2,1)S(1)}, bf16[16,1920]{1,0:T(8,128)(2,1)S(1)}) custom-call(bf16[16,1792]{1,0:T(8,128)(2,1)} %bitcast.25, bf16[16,1792]{1,0:T(8,128)(2,1)} %bitcast.26, bf16[16,1792]{1,0:T(8,128)(2,1)} %bitcast.27, s32[1,16]{1,0:T(1,128)} %bitcast.14, bf16[1,16]{1,0:T(2,128)(2,1)} %bitcast.16, s32[1,16]{1,0:T(1,128)} %bitcast.18, ...), custom_call_target="tpu_custom_call" | custom-call | bytes 344064 | tf_op jit(solution)/shard_map/pallas_call | solution.py:293
  1.6 3.0 %collective-permute-start = (bf16[32,1792]{1,0:T(8,128)(2,1)S(1)}, bf16[32,1792]{1,0:T(8,128)(2,1)S(1)}, u32[]{:S(2)}, u32[]{:S(2)}) collective-permute-start(bf16[32,1792]{1,0:T(8,128)(2,1)S(1)} %get-tuple-element.25), channel_id=1, source_target_pairs={{0,16},{4,20},{8,24},{12,28},{16,0},{20,4},{24,8},{28,12},{1,17},{... | collective-permute-start | bytes 344072 | tf_op jit(solution)/shard_map/ppermute | solution.py:57
  4.6 1.5 %collective-permute-start.3 = (bf16[16,1920]{1,0:T(8,128)(2,1)S(1)}, bf16[16,1920]{1,0:T(8,128)(2,1)S(1)}, u32[]{:S(2)}, u32[]{:S(2)}) collective-permute-start(bf16[16,1920]{1,0:T(8,128)(2,1)S(1)} %get-tuple-element.32.refs_4_), channel_id=1, source_target_pairs={{0,8},{4,12},{8,0},{12,4},{1,9},{5,13},{9,1},{13,5},{2,10},{6,14},... | collective-permute-start | bytes 184328 | tf_op jit(solution)/shard_map/ppermute | solution.py:35
  6.2 0.0 collective-permute-start.1
  6.2 2.6 %shard_map.114 = (bf16[1792,512]{1,0:T(8,128)(2,1)S(1)}, bf16[1792,512]{1,0:T(8,128)(2,1)S(1)}, bf16[512,1792]{1,0:T(8,128)(2,1)S(1)}) custom-call(bf16[1792,512]{1,0:T(8,128)(2,1)} %bitcast.22, bf16[1792,512]{1,0:T(8,128)(2,1)} %bitcast.23, bf16[512,1792]{1,0:T(8,128)(2,1)} %bitcast.24), custom_call_target="tpu_custom_call" | custom-call | bytes 11010048 | tf_op jit(solution)/shard_map/pallas_call | solution.py:279
  8.8 0.0 collective-permute-done.refs_0_.moved_ref
  8.8 0.1 collective-permute-start.2
  8.9 0.5 %collective-permute-start.4 = (bf16[16,1920]{1,0:T(8,128)(2,1)S(1)}, bf16[16,1920]{1,0:T(8,128)(2,1)S(1)}, u32[]{:S(2)}, u32[]{:S(2)}) collective-permute-start(bf16[16,1920]{1,0:T(8,128)(2,1)S(1)} %get-tuple-element.32.refs_4_), channel_id=1, source_target_pairs={{0,4},{4,0},{8,12},{12,8},{1,5},{5,1},{9,13},{13,9},{2,6},{6,2},{1... | collective-permute-start | bytes 184328 | tf_op jit(solution)/shard_map/ppermute | solution.py:35
  9.4 0.0 collective-permute-done.3.refs_5_
  9.4 0.1 collective-permute-start.5
  9.5 2.4 %collective-permute-done.1.refs_1_ = bf16[32,1792]{1,0:T(8,128)(2,1)S(1)} collective-permute-done((bf16[32,1792]{1,0:T(8,128)(2,1)S(1)}, bf16[32,1792]{1,0:T(8,128)(2,1)S(1)}, u32[]{:S(2)}, u32[]{:S(2)}) %collective-permute-start.1) | collective-permute-done | bytes 114720 | tf_op jit(solution)/shard_map/ppermute | solution.py:57
  11.9 0.0 collective-permute-done.4.refs_6_
  11.9 0.0 collective-permute-done.5.refs_7_
  11.9 0.1 collective-permute-start.6
  11.9 1.3 %collective-permute-done.6.refs_3_ = bf16[32,1792]{1,0:T(8,128)(2,1)S(1)} collective-permute-done((bf16[32,1792]{1,0:T(8,128)(2,1)S(1)}, bf16[32,1792]{1,0:T(8,128)(2,1)S(1)}, u32[]{:S(2)}, u32[]{:S(2)}) %collective-permute-start.6) | collective-permute-done | bytes 114720 | tf_op jit(solution)/shard_map/ppermute | solution.py:35
  13.3 1.4 %shard_map.115 = (bf16[40,1280]{1,0:T(8,128)(2,1)S(1)}, bf16[40,1280]{1,0:T(8,128)(2,1)S(1)}, bf16[96,80]{1,0:T(8,128)(2,1)S(1)}) custom-call(bf16[32,1792]{1,0:T(8,128)(2,1)S(1)} %collective-permute-done.refs_0_.moved_ref, bf16[32,1792]{1,0:T(8,128)(2,1)S(1)} %collective-permute-done.1.refs_1_, bf16[32,1792]{1,0:T(8,128)(2,1)S(1)} %collective-permute-done.2.refs_2_, ...), custom_call_target="tpu_custom_call" | custom-call | flops 367001600 | bytes 5505024 | tf_op jit(solution)/shard_map/pallas_call | solution.py:322
  14.7 1.6 %collective-permute-start.7 = (bf16[40,1280]{1,0:T(8,128)(2,1)S(1)}, bf16[40,1280]{1,0:T(8,128)(2,1)S(1)}, u32[]{:S(2)}, u32[]{:S(2)}) collective-permute-start(bf16[40,1280]{1,0:T(8,128)(2,1)S(1)} %get-tuple-element.42), channel_id=1, source_target_pairs={{0,1},{1,0},{2,3},{3,2},{4,6},{5,7},{6,4},{7,5},{8,9},{9,8},{10,11... | collective-permute-start | bytes 307208 | tf_op jit(solution)/shard_map/ppermute | solution.py:46
  16.3 0.5 %collective-permute-start.9 = (bf16[40,1280]{1,0:T(8,128)(2,1)S(1)}, bf16[40,1280]{1,0:T(8,128)(2,1)S(1)}, u32[]{:S(2)}, u32[]{:S(2)}) collective-permute-start(bf16[40,1280]{1,0:T(8,128)(2,1)S(1)} %get-tuple-element.43), channel_id=1, source_target_pairs={{0,1},{1,0},{2,3},{3,2},{4,6},{5,7},{6,4},{7,5},{8,9},{9,8},{10,11... | collective-permute-start | bytes 307208 | tf_op jit(solution)/shard_map/ppermute | solution.py:46
  16.8 3.7 %collective-permute-done.7 = bf16[40,1280]{1,0:T(8,128)(2,1)S(1)} collective-permute-done((bf16[40,1280]{1,0:T(8,128)(2,1)S(1)}, bf16[40,1280]{1,0:T(8,128)(2,1)S(1)}, u32[]{:S(2)}, u32[]{:S(2)}) %collective-permute-start.7) | collective-permute-done | bytes 102432 | tf_op jit(solution)/shard_map/ppermute | solution.py:46
  20.5 1.8 %collective-permute-start.8 = (bf16[40,1280]{1,0:T(8,128)(2,1)S(1)}, bf16[40,1280]{1,0:T(8,128)(2,1)S(1)}, u32[]{:S(2)}, u32[]{:S(2)}) collective-permute-start(bf16[40,1280]{1,0:T(8,128)(2,1)S(1)} %add_convert_fusion.1.a_ref.fa_ref), channel_id=1, source_target_pairs={{0,2},{1,3},{2,0},{3,1},{4,5},{5,4},{6,7},{7,6},{8,10},{9,11},{10,... | collective-permute-start | bytes 307208 | tf_op jit(solution)/shard_map/ppermute | solution.py:46
  22.3 0.4 %collective-permute-done.9 = bf16[40,1280]{1,0:T(8,128)(2,1)S(1)} collective-permute-done((bf16[40,1280]{1,0:T(8,128)(2,1)S(1)}, bf16[40,1280]{1,0:T(8,128)(2,1)S(1)}, u32[]{:S(2)}, u32[]{:S(2)}) %collective-permute-start.9) | collective-permute-done | bytes 102432 | tf_op jit(solution)/shard_map/ppermute | solution.py:46
  22.8 1.8 %collective-permute-start.10 = (bf16[40,1280]{1,0:T(8,128)(2,1)S(1)}, bf16[40,1280]{1,0:T(8,128)(2,1)S(1)}, u32[]{:S(2)}, u32[]{:S(2)}) collective-permute-start(bf16[40,1280]{1,0:T(8,128)(2,1)S(1)} %add_convert_fusion.ba_ref), channel_id=1, source_target_pairs={{0,2},{1,3},{2,0},{3,1},{4,5},{5,4},{6,7},{7,6},{8,10},{9,11},{10,... | collective-permute-start | bytes 307208 | tf_op jit(solution)/shard_map/ppermute | solution.py:46
  24.6 1.9 %collective-permute-done.8.b_ref.fb_ref = bf16[40,1280]{1,0:T(8,128)(2,1)S(1)} collective-permute-done((bf16[40,1280]{1,0:T(8,128)(2,1)S(1)}, bf16[40,1280]{1,0:T(8,128)(2,1)S(1)}, u32[]{:S(2)}, u32[]{:S(2)}) %collective-permute-start.8) | collective-permute-done | bytes 102432 | tf_op jit(solution)/shard_map/ppermute | solution.py:46
  26.4 0.4 %shard_map.117.out_ref = f32[40,1792]{1,0:T(8,128)S(1)} custom-call(bf16[40,1280]{1,0:T(8,128)(2,1)S(1)} %add_convert_fusion.1.a_ref.fa_ref, bf16[40,1280]{1,0:T(8,128)(2,1)S(1)} %collective-permute-done.8.b_ref.fb_ref, bf16[512,1792]{1,0:T(8,128)(2,1)S(1)} %get-tuple-element.36.refs_10_.w_d_ref), custom_call_target="tpu_custom_call" | custom-call | flops 73400320 | bytes 1835008 | tf_op jit(solution)/shard_map/pallas_call | solution.py:341
  26.9 1.6 %collective-permute-done.10.bb_ref = bf16[40,1280]{1,0:T(8,128)(2,1)S(1)} collective-permute-done((bf16[40,1280]{1,0:T(8,128)(2,1)S(1)}, bf16[40,1280]{1,0:T(8,128)(2,1)S(1)}, u32[]{:S(2)}, u32[]{:S(2)}) %collective-permute-start.10) | collective-permute-done | bytes 102432 | tf_op jit(solution)/shard_map/ppermute | solution.py:46
  28.4 1.4 %shard_map.118 = (bf16[2,24,1792]{2,1,0:T(8,128)(2,1)S(1)}, bf16[2,24,1792]{2,1,0:T(8,128)(2,1)S(1)}) custom-call(bf16[40,1280]{1,0:T(8,128)(2,1)S(1)} %add_convert_fusion.1.a_ref.fa_ref, bf16[40,1280]{1,0:T(8,128)(2,1)S(1)} %collective-permute-done.8.b_ref.fb_ref, bf16[40,1280]{1,0:T(8,128)(2,1)S(1)} %add_convert_fusion.ba_ref, ...), custom_call_target="tpu_custom_call" | custom-call | flops 146800640 | bytes 3670016 | tf_op jit(solution)/shard_map/pallas_call | solution.py:347
  29.8 0.1 collective-permute-start.11
  29.9 1.4 %collective-permute-done.11.other_ref = bf16[2,24,1792]{2,1,0:T(8,128)(2,1)S(1)} collective-permute-done((bf16[2,24,1792]{2,1,0:T(8,128)(2,1)S(1)}, bf16[2,24,1792]{2,1,0:T(8,128)(2,1)S(1)}, u32[]{:S(2)}, u32[]{:S(2)}) %collective-permute-start.11) | collective-permute-done | bytes 172064 | tf_op jit(solution)/shard_map/ppermute | solution.py:35
  31.3 2.0 %collective-permute-start.12 = (bf16[24,1792]{1,0:T(8,128)(2,1)S(1)}, bf16[24,1792]{1,0:T(8,128)(2,1)S(1)}, u32[]{:S(2)}, u32[]{:S(2)}) collective-permute-start(bf16[24,1792]{1,0:T(8,128)(2,1)S(1)} %fusion), channel_id=1, source_target_pairs={{0,8},{4,12},{8,0},{12,4},{1,9},{5,13},{9,1},{13,5},{2,10},{6,14},... | collective-permute-start | bytes 258056 | tf_op jit(solution)/shard_map/ppermute | solution.py:35
  33.3 0.3 shard_map.116.home_ref
  33.6 2.5 %collective-permute-done.12.refs_0_ = bf16[24,1792]{1,0:T(8,128)(2,1)S(1)} collective-permute-done((bf16[24,1792]{1,0:T(8,128)(2,1)S(1)}, bf16[24,1792]{1,0:T(8,128)(2,1)S(1)}, u32[]{:S(2)}, u32[]{:S(2)}) %collective-permute-start.12) | collective-permute-done | bytes 86048 | tf_op jit(solution)/shard_map/ppermute | solution.py:35
  36.2 0.9 %shard_map.119 = (bf16[16,1792]{1,0:T(8,128)(2,1)}, bf16[16,1792]{1,0:T(8,128)(2,1)}) custom-call(bf16[32,1792]{1,0:T(8,128)(2,1)S(1)} %collective-permute-done.refs_0_.moved_ref, bf16[2,32,24]{2,1,0:T(8,128)(2,1)S(1)} %shard_map.116.home_ref, bf16[2,24,1792]{2,1,0:T(8,128)(2,1)S(1)} %get-tuple-element.44.own_ref, ...), custom_call_target="tpu_custom_call" | custom-call | bytes 573440 | tf_op jit(solution)/shard_map/pallas_call | solution.py:366
  (12 shorter events, 0.1 us)
Async XLA Ops:
  1.6 7.2 %collective-permute-start = (bf16[32,1792]{1,0:T(8,128)(2,1)S(1)}, bf16[32,1792]{1,0:T(8,128)(2,1)S(1)}, u32[]{:S(2)}, u32[]{:S(2)}) collective-permute-start(bf16[32,1792]{1,0:T(8,128)(2,1)S(1)} %get-tuple-element.25), channel_id=1, source_target_pairs={{0,16},{4,20},{8,24},{12,28},{16,0},{20,4},{24,8},{28,12},{1,17},{... | collective-permute-start | bytes 344072 | tf_op jit(solution)/shard_map/ppermute | solution.py:57
  4.6 4.8 %collective-permute-start.3 = (bf16[16,1920]{1,0:T(8,128)(2,1)S(1)}, bf16[16,1920]{1,0:T(8,128)(2,1)S(1)}, u32[]{:S(2)}, u32[]{:S(2)}) collective-permute-start(bf16[16,1920]{1,0:T(8,128)(2,1)S(1)} %get-tuple-element.32.refs_4_), channel_id=1, source_target_pairs={{0,8},{4,12},{8,0},{12,4},{1,9},{5,13},{9,1},{13,5},{2,10},{6,14},... | collective-permute-start | bytes 184328 | tf_op jit(solution)/shard_map/ppermute | solution.py:35
  6.2 5.7 %collective-permute-start.1 = (bf16[32,1792]{1,0:T(8,128)(2,1)S(1)}, bf16[32,1792]{1,0:T(8,128)(2,1)S(1)}, u32[]{:S(2)}, u32[]{:S(2)}) collective-permute-start(bf16[32,1792]{1,0:T(8,128)(2,1)S(1)} %get-tuple-element.25), channel_id=1, source_target_pairs={{0,24},{4,28},{8,16},{12,20},{16,8},{20,12},{24,0},{28,4},{1,25},{... | collective-permute-start | bytes 344072 | tf_op jit(solution)/shard_map/ppermute | solution.py:57
  8.8 3.0 %collective-permute-start.2 = (bf16[32,1792]{1,0:T(8,128)(2,1)S(1)}, bf16[32,1792]{1,0:T(8,128)(2,1)S(1)}, u32[]{:S(2)}, u32[]{:S(2)}) collective-permute-start(bf16[32,1792]{1,0:T(8,128)(2,1)S(1)} %collective-permute-done.refs_0_.moved_ref), channel_id=1, source_target_pairs={{0,4},{4,0},{8,12},{12,8},{1,5},{5,1},{9,13},{13,9},{2,6},{6,2},{1... | collective-permute-start | bytes 344072 | tf_op jit(solution)/shard_map/ppermute | solution.py:35
  8.9 2.9 %collective-permute-start.4 = (bf16[16,1920]{1,0:T(8,128)(2,1)S(1)}, bf16[16,1920]{1,0:T(8,128)(2,1)S(1)}, u32[]{:S(2)}, u32[]{:S(2)}) collective-permute-start(bf16[16,1920]{1,0:T(8,128)(2,1)S(1)} %get-tuple-element.32.refs_4_), channel_id=1, source_target_pairs={{0,4},{4,0},{8,12},{12,8},{1,5},{5,1},{9,13},{13,9},{2,6},{6,2},{1... | collective-permute-start | bytes 184328 | tf_op jit(solution)/shard_map/ppermute | solution.py:35
  9.4 2.4 %collective-permute-start.5 = (bf16[16,1920]{1,0:T(8,128)(2,1)S(1)}, bf16[16,1920]{1,0:T(8,128)(2,1)S(1)}, u32[]{:S(2)}, u32[]{:S(2)}) collective-permute-start(bf16[16,1920]{1,0:T(8,128)(2,1)S(1)} %collective-permute-done.3.refs_5_), channel_id=1, source_target_pairs={{0,4},{4,0},{8,12},{12,8},{1,5},{5,1},{9,13},{13,9},{2,6},{6,2},{1... | collective-permute-start | bytes 184328 | tf_op jit(solution)/shard_map/ppermute | solution.py:35
  11.9 1.4 %collective-permute-start.6 = (bf16[32,1792]{1,0:T(8,128)(2,1)S(1)}, bf16[32,1792]{1,0:T(8,128)(2,1)S(1)}, u32[]{:S(2)}, u32[]{:S(2)}) collective-permute-start(bf16[32,1792]{1,0:T(8,128)(2,1)S(1)} %collective-permute-done.1.refs_1_), channel_id=1, source_target_pairs={{0,4},{4,0},{8,12},{12,8},{1,5},{5,1},{9,13},{13,9},{2,6},{6,2},{1... | collective-permute-start | bytes 344072 | tf_op jit(solution)/shard_map/ppermute | solution.py:35
  14.7 5.8 %collective-permute-start.7 = (bf16[40,1280]{1,0:T(8,128)(2,1)S(1)}, bf16[40,1280]{1,0:T(8,128)(2,1)S(1)}, u32[]{:S(2)}, u32[]{:S(2)}) collective-permute-start(bf16[40,1280]{1,0:T(8,128)(2,1)S(1)} %get-tuple-element.42), channel_id=1, source_target_pairs={{0,1},{1,0},{2,3},{3,2},{4,6},{5,7},{6,4},{7,5},{8,9},{9,8},{10,11... | collective-permute-start | bytes 307208 | tf_op jit(solution)/shard_map/ppermute | solution.py:46
  16.3 6.4 %collective-permute-start.9 = (bf16[40,1280]{1,0:T(8,128)(2,1)S(1)}, bf16[40,1280]{1,0:T(8,128)(2,1)S(1)}, u32[]{:S(2)}, u32[]{:S(2)}) collective-permute-start(bf16[40,1280]{1,0:T(8,128)(2,1)S(1)} %get-tuple-element.43), channel_id=1, source_target_pairs={{0,1},{1,0},{2,3},{3,2},{4,6},{5,7},{6,4},{7,5},{8,9},{9,8},{10,11... | collective-permute-start | bytes 307208 | tf_op jit(solution)/shard_map/ppermute | solution.py:46
  20.5 5.9 %collective-permute-start.8 = (bf16[40,1280]{1,0:T(8,128)(2,1)S(1)}, bf16[40,1280]{1,0:T(8,128)(2,1)S(1)}, u32[]{:S(2)}, u32[]{:S(2)}) collective-permute-start(bf16[40,1280]{1,0:T(8,128)(2,1)S(1)} %add_convert_fusion.1.a_ref.fa_ref), channel_id=1, source_target_pairs={{0,2},{1,3},{2,0},{3,1},{4,5},{5,4},{6,7},{7,6},{8,10},{9,11},{10,... | collective-permute-start | bytes 307208 | tf_op jit(solution)/shard_map/ppermute | solution.py:46
  22.8 5.7 %collective-permute-start.10 = (bf16[40,1280]{1,0:T(8,128)(2,1)S(1)}, bf16[40,1280]{1,0:T(8,128)(2,1)S(1)}, u32[]{:S(2)}, u32[]{:S(2)}) collective-permute-start(bf16[40,1280]{1,0:T(8,128)(2,1)S(1)} %add_convert_fusion.ba_ref), channel_id=1, source_target_pairs={{0,2},{1,3},{2,0},{3,1},{4,5},{5,4},{6,7},{7,6},{8,10},{9,11},{10,... | collective-permute-start | bytes 307208 | tf_op jit(solution)/shard_map/ppermute | solution.py:46
  28.4 4.9 %copy-start = (s32[1,16,1]{1,2,0:T(1,128)S(1)}, s32[1,16,1]{1,2,0:T(1,128)}, u32[]{:S(2)}) copy-start(s32[1,16,1]{1,2,0:T(1,128)} %param.13) | copy-start | bytes 196
  28.4 4.9 %copy-start.1 = (bf16[1,16,1]{1,2,0:T(2,128)(2,1)S(1)}, bf16[1,16,1]{1,2,0:T(2,128)(2,1)}, u32[]{:S(2)}) copy-start(bf16[1,16,1]{1,2,0:T(2,128)(2,1)} %param.14) | copy-start | bytes 100
  28.4 4.9 %copy-start.2 = (s32[1,16,1]{1,2,0:T(1,128)S(1)}, s32[1,16,1]{1,2,0:T(1,128)}, u32[]{:S(2)}) copy-start(s32[1,16,1]{1,2,0:T(1,128)} %param.15) | copy-start | bytes 196
  28.4 4.9 %copy-start.3 = (bf16[1,16,1]{1,2,0:T(2,128)(2,1)S(1)}, bf16[1,16,1]{1,2,0:T(2,128)(2,1)}, u32[]{:S(2)}) copy-start(bf16[1,16,1]{1,2,0:T(2,128)(2,1)} %param.16) | copy-start | bytes 100
  29.8 1.5 %collective-permute-start.11 = (bf16[2,24,1792]{2,1,0:T(8,128)(2,1)S(1)}, bf16[2,24,1792]{2,1,0:T(8,128)(2,1)S(1)}, u32[]{:S(2)}, u32[]{:S(2)}) collective-permute-start(bf16[2,24,1792]{2,1,0:T(8,128)(2,1)S(1)} %get-tuple-element.45), channel_id=1, source_target_pairs={{0,4},{4,0},{8,12},{12,8},{1,5},{5,1},{9,13},{13,9},{2,6},{6,2},{1... | collective-permute-start | bytes 516104 | tf_op jit(solution)/shard_map/ppermute | solution.py:35
  31.3 4.9 %collective-permute-start.12 = (bf16[24,1792]{1,0:T(8,128)(2,1)S(1)}, bf16[24,1792]{1,0:T(8,128)(2,1)S(1)}, u32[]{:S(2)}, u32[]{:S(2)}) collective-permute-start(bf16[24,1792]{1,0:T(8,128)(2,1)S(1)} %fusion), channel_id=1, source_target_pairs={{0,8},{4,12},{8,0},{12,4},{1,9},{5,13},{9,1},{13,5},{2,10},{6,14},... | collective-permute-start | bytes 258056 | tf_op jit(solution)/shard_map/ppermute | solution.py:35

commit v9 on v7

--- a/solution.py
+++ b/solution.py
@@ -194,41 +194,31 @@
     gate = jnp.dot(both, w_g_ref[...], preferred_element_type=F32)
     upper = jnp.dot(both, w_u_ref[...], preferred_element_type=F32)
     dhid = lax.dot_general(grads_b, w_d_ref[...], (((1,), (1,)), ((), ())), preferred_element_type=F32)
-    cut = part_f_ref.shape[1] - 2 * dhid.shape[1]
-    part_f_ref[...] = jnp.concatenate([gate[:rows], upper[:rows], dhid[:, :cut]], axis=1).astype(BF16)
-    part_b_ref[...] = jnp.concatenate([gate[rows:], upper[rows:], dhid[:, cut:]], axis=1).astype(BF16)
-
-
-def down_kernel(
-    groups,
-    rows,
-    fa_ref,
-    fb_ref,
-    ba_ref,
-    bb_ref,
-    slot_ref,
-    w_g_ref,
-    w_u_ref,
-    w_d_ref,
-    own_ref,
-    other_ref,
-):
-    total_f = fa_ref[...].astype(F32) + fb_ref[...].astype(F32)
-    total_b = ba_ref[...].astype(F32) + bb_ref[...].astype(F32)
-    units = w_d_ref.shape[0]
-    gate_f, upper_f = total_f[:, :units], total_f[:, units : 2 * units]
-    gate_b, upper_b = total_b[:, :units], total_b[:, units : 2 * units]
-    dhid = jnp.concatenate([total_f[:, 2 * units :], total_b[:, 2 * units :]], axis=1)
-    hidden = (gate_f * jax.nn.sigmoid(gate_f) * upper_f).astype(BF16)
-    sigma = jax.nn.sigmoid(gate_b)
-    slope = sigma * (1.0 + gate_b * (1.0 - sigma))
-    dgate = (dhid * upper_b * slope).astype(BF16)
-    dupper = (dhid * (gate_b * sigma)).astype(BF16)
+    part_f_ref[...] = jnp.concatenate([gate[:rows], upper[:rows]], axis=1).astype(BF16)
+    part_b_ref[...] = jnp.concatenate([gate[rows:], upper[rows:], dhid], axis=1).astype(BF16)
+
+
+def grad_kernel(a_ref, b_ref, w_g_ref, w_u_ref, grad_ref):
+    units = w_g_ref.shape[1]
+    total = a_ref[...].astype(F32) + b_ref[...].astype(F32)
+    gate, upper, dhid = [total[:, i * units : (i + 1) * units] for i in range(3)]
+    sigma = jax.nn.sigmoid(gate)
+    slope = sigma * (1.0 + gate * (1.0 - sigma))
+    dgate = (dhid * upper * slope).astype(BF16)
+    dupper = (dhid * (gate * sigma)).astype(BF16)
     turned = (((1,), (1,)), ((), ()))
-    out_f = jnp.dot(hidden, w_d_ref[...], preferred_element_type=F32)
     grad = lax.dot_general(dgate, w_g_ref[...], turned, preferred_element_type=F32)
     grad = grad + lax.dot_general(dupper, w_u_ref[...], turned, preferred_element_type=F32)
-    both = jnp.concatenate([out_f, grad], axis=0).astype(BF16)
+    grad_ref[...] = grad
+
+
+def down_kernel(groups, a_ref, b_ref, grad_ref, slot_ref, w_d_ref, own_ref, other_ref):
+    units = w_d_ref.shape[0]
+    total = a_ref[...].astype(F32) + b_ref[...].astype(F32)
+    gate, upper = total[:, :units], total[:, units:]
+    hidden = (gate * jax.nn.sigmoid(gate) * upper).astype(BF16)
+    out = jnp.dot(hidden, w_d_ref[...], preferred_element_type=F32)
+    both = jnp.concatenate([out, grad_ref[...]], axis=0).astype(BF16)
     full = jnp.dot(slot_ref[...], both, preferred_element_type=F32)
     slot_rows = own_ref.shape[1]
     for d in range(groups):
@@ -268,7 +258,6 @@
     topk = routes_forward.shape[2]
     capacity = min(held, max(6, held * topk // experts + 2))
     rows = -(-peers * capacity // 8) * 8
-    cut = hidden * 2 // 4
     slot_rows = -(-2 * capacity // 8) * 8
     weight_bytes = 6 * width * hidden
     w_g, w_u, w_d = pl.pallas_call(
@@ -317,8 +306,8 @@
     part_f, part_b, slot = kernel_call(
         functools.partial(up_kernel, groups, topk, rows, capacity, slot_rows),
         (
-            jax.ShapeDtypeStruct((rows, 2 * hidden + cut), BF16),
-            jax.ShapeDtypeStruct((rows, 3 * hidden - cut), BF16),
+            jax.ShapeDtypeStruct((rows, 2 * hidden), BF16),
+            jax.ShapeDtypeStruct((rows, 3 * hidden), BF16),
             jax.ShapeDtypeStruct((peers * slot_rows, 2 * rows), BF16),
         ),
         10 * rows * width * hidden,
@@ -333,12 +322,18 @@
             break
         part_f = (part_f.astype(F32) + came_f.astype(F32)).astype(BF16)
         part_b = (part_b.astype(F32) + came_b.astype(F32)).astype(BF16)
+    grad = kernel_call(
+        grad_kernel,
+        jax.ShapeDtypeStruct((rows, width), F32),
+        4 * rows * width * hidden,
+        4 * width * hidden,
+    )(part_b, came_b, w_g, w_u)
     own, other = kernel_call(
-        functools.partial(down_kernel, groups, rows),
+        functools.partial(down_kernel, groups),
         [jax.ShapeDtypeStruct((groups, slot_rows, width), BF16)] * 2,
-        6 * rows * width * hidden,
-        weight_bytes,
-    )(part_f, came_f, part_b, came_b, slot, w_g, w_u, w_d)
+        2 * rows * width * hidden,
+        2 * width * hidden,
+    )(part_f, came_f, grad, slot, w_d)
     other = swap(other, "expert", 1)
     came = []
     for d in range(1, groups):

time: 37.6 us -> 37.1 us (0.987)
  waiting for transfers between devices: 15.6 us -> 15.1 us
    ppermute x4, waiting for transfers between devices: 7.98 us -> 7.52 us  [mixed(): return lax.ppermute(x, ('expert', 'dp'), pairs)]
    pallas_call x1 -> x2, Pallas kernels: 1.73 us -> 1.75 us  [the longest x1 1.16 us: local(): kernel_call(grad_kernel, jax.ShapeDtypeStruct((rows, width), F32), 4 * ro...]
  transfers between devices with their start and end apart: 13 -> 13, of which waited for: 8 -> 7; matrix products, arithmetic and copies ran while one was open for 0% -> 0% of each run, Pallas kernels for 8% -> 11%
where the time goes in v9:
time: 37.1 us; the launch traced here: 36.9 us
  waiting for transfers between devices  15.1 us (41%)
  starting transfers between devices  12.9 us (35%)
  Pallas kernels  7.97 us (21%)
  between operations  0.75 us (2%)
    ppermute x4, waiting for transfers between devices, mixed(): return lax.ppermute(x, ('expert', 'dp'), pairs)  7.52 us
    ppermute x4, starting transfers between devices, mixed(): return lax.ppermute(x, ('expert', 'dp'), pairs)  5.61 us
    ppermute x7, waiting for transfers between devices, swap(): return lax.ppermute(x, axis, [(i, i ^ bit) for i in range(peers)])  5.26 us
    ppermute x7, starting transfers between devices, swap(): return lax.ppermute(x, axis, [(i, i ^ bit) for i in range(peers)])  4.31 us
    ppermute x2, starting transfers between devices, onward(): return lax.ppermute(x, ('pipe', 'expert'), pairs)  3.02 us
    pallas_call x1, Pallas kernels, local(): pl.pallas_call(fetch_kernel, out_shape=[pltpu.VMEM(w.shape[2:], BF16) for...  2.63 us
    ppermute x2, waiting for transfers between devices, onward(): return lax.ppermute(x, ('pipe', 'expert'), pairs)  2.36 us
    pallas_call x1, Pallas kernels, local(): kernel_call(functools.partial(up_kernel, groups, topk, rows, capacity, sl...  1.43 us
  transfers between devices with their start and end apart: 13, of which 7 were waited for; matrix products, arithmetic and copies ran while one was open for 0% of the time, Pallas kernels for 11%

profile of v9, /device:TPU:0, one launch (start us, length us, event | category | flops | bytes accessed | tf_op | source)
XLA Modules:
  0.0 36.9 jit_solution(4479072742200136872)
XLA Ops:
  0.6 1.0 %shard_map.113 = (bf16[32,1792]{1,0:T(8,128)(2,1)S(1)}, bf16[16,1920]{1,0:T(8,128)(2,1)S(1)}) custom-call(bf16[16,1792]{1,0:T(8,128)(2,1)} %bitcast.25, bf16[16,1792]{1,0:T(8,128)(2,1)} %bitcast.26, bf16[16,1792]{1,0:T(8,128)(2,1)} %bitcast.27, s32[1,16]{1,0:T(1,128)} %bitcast.14, bf16[1,16]{1,0:T(2,128)(2,1)} %bitcast.16, s32[1,16]{1,0:T(1,128)} %bitcast.18, ...), custom_call_target="tpu_custom_call" | custom-call | bytes 344064 | tf_op jit(solution)/shard_map/pallas_call | solution.py:277
  1.6 3.0 %collective-permute-start = (bf16[32,1792]{1,0:T(8,128)(2,1)S(1)}, bf16[32,1792]{1,0:T(8,128)(2,1)S(1)}, u32[]{:S(2)}, u32[]{:S(2)}) collective-permute-start(bf16[32,1792]{1,0:T(8,128)(2,1)S(1)} %get-tuple-element.25), channel_id=1, source_target_pairs={{0,16},{4,20},{8,24},{12,28},{16,0},{20,4},{24,8},{28,12},{1,17},{... | collective-permute-start | bytes 344072 | tf_op jit(solution)/shard_map/ppermute | solution.py:57
  4.6 1.5 %collective-permute-start.3 = (bf16[16,1920]{1,0:T(8,128)(2,1)S(1)}, bf16[16,1920]{1,0:T(8,128)(2,1)S(1)}, u32[]{:S(2)}, u32[]{:S(2)}) collective-permute-start(bf16[16,1920]{1,0:T(8,128)(2,1)S(1)} %get-tuple-element.32.refs_4_), channel_id=1, source_target_pairs={{0,8},{4,12},{8,0},{12,4},{1,9},{5,13},{9,1},{13,5},{2,10},{6,14},... | collective-permute-start | bytes 184328 | tf_op jit(solution)/shard_map/ppermute | solution.py:35
  6.2 0.0 collective-permute-start.1
  6.2 2.6 %shard_map.114 = (bf16[1792,512]{1,0:T(8,128)(2,1)S(1)}, bf16[1792,512]{1,0:T(8,128)(2,1)S(1)}, bf16[512,1792]{1,0:T(8,128)(2,1)S(1)}) custom-call(bf16[1792,512]{1,0:T(8,128)(2,1)} %bitcast.22, bf16[1792,512]{1,0:T(8,128)(2,1)} %bitcast.23, bf16[512,1792]{1,0:T(8,128)(2,1)} %bitcast.24), custom_call_target="tpu_custom_call" | custom-call | bytes 11010048 | tf_op jit(solution)/shard_map/pallas_call | solution.py:263
  8.8 0.1 collective-permute-start.2
  8.9 0.5 %collective-permute-start.4 = (bf16[16,1920]{1,0:T(8,128)(2,1)S(1)}, bf16[16,1920]{1,0:T(8,128)(2,1)S(1)}, u32[]{:S(2)}, u32[]{:S(2)}) collective-permute-start(bf16[16,1920]{1,0:T(8,128)(2,1)S(1)} %get-tuple-element.32.refs_4_), channel_id=1, source_target_pairs={{0,4},{4,0},{8,12},{12,8},{1,5},{5,1},{9,13},{13,9},{2,6},{6,2},{1... | collective-permute-start | bytes 184328 | tf_op jit(solution)/shard_map/ppermute | solution.py:35
  9.4 0.1 collective-permute-start.5
  9.5 2.4 %collective-permute-done.1.refs_1_ = bf16[32,1792]{1,0:T(8,128)(2,1)S(1)} collective-permute-done((bf16[32,1792]{1,0:T(8,128)(2,1)S(1)}, bf16[32,1792]{1,0:T(8,128)(2,1)S(1)}, u32[]{:S(2)}, u32[]{:S(2)}) %collective-permute-start.1) | collective-permute-done | bytes 114720 | tf_op jit(solution)/shard_map/ppermute | solution.py:57
  11.9 0.0 collective-permute-done.4.refs_6_
  11.9 0.1 collective-permute-start.6
  11.9 1.3 %collective-permute-done.6.refs_3_ = bf16[32,1792]{1,0:T(8,128)(2,1)S(1)} collective-permute-done((bf16[32,1792]{1,0:T(8,128)(2,1)S(1)}, bf16[32,1792]{1,0:T(8,128)(2,1)S(1)}, u32[]{:S(2)}, u32[]{:S(2)}) %collective-permute-start.6) | collective-permute-done | bytes 114720 | tf_op jit(solution)/shard_map/ppermute | solution.py:35
  13.3 1.4 %shard_map.115 = (bf16[40,1024]{1,0:T(8,128)(2,1)S(1)}, bf16[40,1536]{1,0:T(8,128)(2,1)S(1)}, bf16[96,80]{1,0:T(8,128)(2,1)S(1)}) custom-call(bf16[32,1792]{1,0:T(8,128)(2,1)S(1)} %collective-permute-done.refs_0_.moved_ref, bf16[32,1792]{1,0:T(8,128)(2,1)S(1)} %collective-permute-done.1.refs_1_, bf16[32,1792]{1,0:T(8,128)(2,1)S(1)} %collective-permute-done.2.refs_2_, ...), custom_call_target="tpu_custom_call" | custom-call | flops 367001600 | bytes 5505024 | tf_op jit(solution)/shard_map/pallas_call | solution.py:306
  14.7 1.6 %collective-permute-start.9 = (bf16[40,1536]{1,0:T(8,128)(2,1)S(1)}, bf16[40,1536]{1,0:T(8,128)(2,1)S(1)}, u32[]{:S(2)}, u32[]{:S(2)}) collective-permute-start(bf16[40,1536]{1,0:T(8,128)(2,1)S(1)} %get-tuple-element.43), channel_id=1, source_target_pairs={{0,1},{1,0},{2,3},{3,2},{4,6},{5,7},{6,4},{7,5},{8,9},{9,8},{10,11... | collective-permute-start | bytes 368648 | tf_op jit(solution)/shard_map/ppermute | solution.py:46
  16.3 0.5 %collective-permute-start.7 = (bf16[40,1024]{1,0:T(8,128)(2,1)S(1)}, bf16[40,1024]{1,0:T(8,128)(2,1)S(1)}, u32[]{:S(2)}, u32[]{:S(2)}) collective-permute-start(bf16[40,1024]{1,0:T(8,128)(2,1)S(1)} %get-tuple-element.42), channel_id=1, source_target_pairs={{0,1},{1,0},{2,3},{3,2},{4,6},{5,7},{6,4},{7,5},{8,9},{9,8},{10,11... | collective-permute-start | bytes 245768 | tf_op jit(solution)/shard_map/ppermute | solution.py:46
  16.8 4.1 %collective-permute-done.9 = bf16[40,1536]{1,0:T(8,128)(2,1)S(1)} collective-permute-done((bf16[40,1536]{1,0:T(8,128)(2,1)S(1)}, bf16[40,1536]{1,0:T(8,128)(2,1)S(1)}, u32[]{:S(2)}, u32[]{:S(2)}) %collective-permute-start.9) | collective-permute-done | bytes 122912 | tf_op jit(solution)/shard_map/ppermute | solution.py:46
  20.9 2.1 %collective-permute-start.10 = (bf16[40,1536]{1,0:T(8,128)(2,1)S(1)}, bf16[40,1536]{1,0:T(8,128)(2,1)S(1)}, u32[]{:S(2)}, u32[]{:S(2)}) collective-permute-start(bf16[40,1536]{1,0:T(8,128)(2,1)S(1)} %add_convert_fusion.a_ref), channel_id=1, source_target_pairs={{0,2},{1,3},{2,0},{3,1},{4,5},{5,4},{6,7},{7,6},{8,10},{9,11},{10,... | collective-permute-start | bytes 368648 | tf_op jit(solution)/shard_map/ppermute | solution.py:46
  23.0 1.4 %collective-permute-start.8 = (bf16[40,1024]{1,0:T(8,128)(2,1)S(1)}, bf16[40,1024]{1,0:T(8,128)(2,1)S(1)}, u32[]{:S(2)}, u32[]{:S(2)}) collective-permute-start(bf16[40,1024]{1,0:T(8,128)(2,1)S(1)} %add_convert_fusion.2.a_ref), channel_id=1, source_target_pairs={{0,2},{1,3},{2,0},{3,1},{4,5},{5,4},{6,7},{7,6},{8,10},{9,11},{10,... | collective-permute-start | bytes 245768 | tf_op jit(solution)/shard_map/ppermute | solution.py:46
  24.5 2.7 %collective-permute-done.10.b_ref = bf16[40,1536]{1,0:T(8,128)(2,1)S(1)} collective-permute-done((bf16[40,1536]{1,0:T(8,128)(2,1)S(1)}, bf16[40,1536]{1,0:T(8,128)(2,1)S(1)}, u32[]{:S(2)}, u32[]{:S(2)}) %collective-permute-start.10) | collective-permute-done | bytes 122912 | tf_op jit(solution)/shard_map/ppermute | solution.py:46
  27.2 1.2 %shard_map.117.grad_ref = f32[40,1792]{1,0:T(8,128)S(1)} custom-call(bf16[40,1536]{1,0:T(8,128)(2,1)S(1)} %add_convert_fusion.a_ref, bf16[40,1536]{1,0:T(8,128)(2,1)S(1)} %collective-permute-done.10.b_ref, bf16[1792,512]{1,0:T(8,128)(2,1)S(1)} %get-tuple-element.34.refs_8_.w_g_ref, bf16[1792,512]{1,0:T(8,128)(2,1)S(1)} %get-tuple-element.35.refs_9_.w_u_ref), custom_call_target="tpu_custom_call" | custom-call | flops 146800640 | bytes 3670016 | tf_op jit(solution)/shard_map/pallas_call | solution.py:325
  28.4 0.0 copy-start
  28.4 0.0 copy-start.1
  28.4 0.0 copy-start.2
  28.4 0.0 copy-start.3
  28.4 0.7 %collective-permute-done.8.b_ref = bf16[40,1024]{1,0:T(8,128)(2,1)S(1)} collective-permute-done((bf16[40,1024]{1,0:T(8,128)(2,1)S(1)}, bf16[40,1024]{1,0:T(8,128)(2,1)S(1)}, u32[]{:S(2)}, u32[]{:S(2)}) %collective-permute-start.8) | collective-permute-done | bytes 81952 | tf_op jit(solution)/shard_map/ppermute | solution.py:46
  29.1 0.6 %shard_map.118 = (bf16[2,24,1792]{2,1,0:T(8,128)(2,1)S(1)}, bf16[2,24,1792]{2,1,0:T(8,128)(2,1)S(1)}) custom-call(bf16[40,1024]{1,0:T(8,128)(2,1)S(1)} %add_convert_fusion.2.a_ref, bf16[40,1024]{1,0:T(8,128)(2,1)S(1)} %collective-permute-done.8.b_ref, f32[40,1792]{1,0:T(8,128)S(1)} %shard_map.117.grad_ref, bf16[96,80]{1,0:T(8,128)(2,1)S(1)} %get-tuple-element.37.slot_ref, ...), custom_call_target="tpu_custom_call" | custom-call | flops 73400320 | bytes 1835008 | tf_op jit(solution)/shard_map/pallas_call | solution.py:331
  29.7 0.1 collective-permute-start.11
  29.8 1.4 %collective-permute-done.11.other_ref = bf16[2,24,1792]{2,1,0:T(8,128)(2,1)S(1)} collective-permute-done((bf16[2,24,1792]{2,1,0:T(8,128)(2,1)S(1)}, bf16[2,24,1792]{2,1,0:T(8,128)(2,1)S(1)}, u32[]{:S(2)}, u32[]{:S(2)}) %collective-permute-start.11) | collective-permute-done | bytes 172064 | tf_op jit(solution)/shard_map/ppermute | solution.py:35
  31.2 2.0 %collective-permute-start.12 = (bf16[24,1792]{1,0:T(8,128)(2,1)S(1)}, bf16[24,1792]{1,0:T(8,128)(2,1)S(1)}, u32[]{:S(2)}, u32[]{:S(2)}) collective-permute-start(bf16[24,1792]{1,0:T(8,128)(2,1)S(1)} %fusion), channel_id=1, source_target_pairs={{0,8},{4,12},{8,0},{12,4},{1,9},{5,13},{9,1},{13,5},{2,10},{6,14},... | collective-permute-start | bytes 258056 | tf_op jit(solution)/shard_map/ppermute | solution.py:35
  33.2 0.3 shard_map.116.home_ref
  33.5 2.5 %collective-permute-done.12.refs_0_ = bf16[24,1792]{1,0:T(8,128)(2,1)S(1)} collective-permute-done((bf16[24,1792]{1,0:T(8,128)(2,1)S(1)}, bf16[24,1792]{1,0:T(8,128)(2,1)S(1)}, u32[]{:S(2)}, u32[]{:S(2)}) %collective-permute-start.12) | collective-permute-done | bytes 86048 | tf_op jit(solution)/shard_map/ppermute | solution.py:35
  36.1 0.9 %shard_map.119 = (bf16[16,1792]{1,0:T(8,128)(2,1)}, bf16[16,1792]{1,0:T(8,128)(2,1)}) custom-call(bf16[32,1792]{1,0:T(8,128)(2,1)S(1)} %collective-permute-done.refs_0_.moved_ref, bf16[2,32,24]{2,1,0:T(8,128)(2,1)S(1)} %shard_map.116.home_ref, bf16[2,24,1792]{2,1,0:T(8,128)(2,1)S(1)} %get-tuple-element.44.own_ref, ...), custom_call_target="tpu_custom_call" | custom-call | bytes 573440 | tf_op jit(solution)/shard_map/pallas_call | solution.py:350
  (12 shorter events, 0.1 us)
Async XLA Ops:
  1.6 7.2 %collective-permute-start = (bf16[32,1792]{1,0:T(8,128)(2,1)S(1)}, bf16[32,1792]{1,0:T(8,128)(2,1)S(1)}, u32[]{:S(2)}, u32[]{:S(2)}) collective-permute-start(bf16[32,1792]{1,0:T(8,128)(2,1)S(1)} %get-tuple-element.25), channel_id=1, source_target_pairs={{0,16},{4,20},{8,24},{12,28},{16,0},{20,4},{24,8},{28,12},{1,17},{... | collective-permute-start | bytes 344072 | tf_op jit(solution)/shard_map/ppermute | solution.py:57
  4.6 4.8 %collective-permute-start.3 = (bf16[16,1920]{1,0:T(8,128)(2,1)S(1)}, bf16[16,1920]{1,0:T(8,128)(2,1)S(1)}, u32[]{:S(2)}, u32[]{:S(2)}) collective-permute-start(bf16[16,1920]{1,0:T(8,128)(2,1)S(1)} %get-tuple-element.32.refs_4_), channel_id=1, source_target_pairs={{0,8},{4,12},{8,0},{12,4},{1,9},{5,13},{9,1},{13,5},{2,10},{6,14},... | collective-permute-start | bytes 184328 | tf_op jit(solution)/shard_map/ppermute | solution.py:35
  6.2 5.7 %collective-permute-start.1 = (bf16[32,1792]{1,0:T(8,128)(2,1)S(1)}, bf16[32,1792]{1,0:T(8,128)(2,1)S(1)}, u32[]{:S(2)}, u32[]{:S(2)}) collective-permute-start(bf16[32,1792]{1,0:T(8,128)(2,1)S(1)} %get-tuple-element.25), channel_id=1, source_target_pairs={{0,24},{4,28},{8,16},{12,20},{16,8},{20,12},{24,0},{28,4},{1,25},{... | collective-permute-start | bytes 344072 | tf_op jit(solution)/shard_map/ppermute | solution.py:57
  8.8 3.0 %collective-permute-start.2 = (bf16[32,1792]{1,0:T(8,128)(2,1)S(1)}, bf16[32,1792]{1,0:T(8,128)(2,1)S(1)}, u32[]{:S(2)}, u32[]{:S(2)}) collective-permute-start(bf16[32,1792]{1,0:T(8,128)(2,1)S(1)} %collective-permute-done.refs_0_.moved_ref), channel_id=1, source_target_pairs={{0,4},{4,0},{8,12},{12,8},{1,5},{5,1},{9,13},{13,9},{2,6},{6,2},{1... | collective-permute-start | bytes 344072 | tf_op jit(solution)/shard_map/ppermute | solution.py:35
  8.9 2.9 %collective-permute-start.4 = (bf16[16,1920]{1,0:T(8,128)(2,1)S(1)}, bf16[16,1920]{1,0:T(8,128)(2,1)S(1)}, u32[]{:S(2)}, u32[]{:S(2)}) collective-permute-start(bf16[16,1920]{1,0:T(8,128)(2,1)S(1)} %get-tuple-element.32.refs_4_), channel_id=1, source_target_pairs={{0,4},{4,0},{8,12},{12,8},{1,5},{5,1},{9,13},{13,9},{2,6},{6,2},{1... | collective-permute-start | bytes 184328 | tf_op jit(solution)/shard_map/ppermute | solution.py:35
  9.4 2.4 %collective-permute-start.5 = (bf16[16,1920]{1,0:T(8,128)(2,1)S(1)}, bf16[16,1920]{1,0:T(8,128)(2,1)S(1)}, u32[]{:S(2)}, u32[]{:S(2)}) collective-permute-start(bf16[16,1920]{1,0:T(8,128)(2,1)S(1)} %collective-permute-done.3.refs_5_), channel_id=1, source_target_pairs={{0,4},{4,0},{8,12},{12,8},{1,5},{5,1},{9,13},{13,9},{2,6},{6,2},{1... | collective-permute-start | bytes 184328 | tf_op jit(solution)/shard_map/ppermute | solution.py:35
  11.9 1.4 %collective-permute-start.6 = (bf16[32,1792]{1,0:T(8,128)(2,1)S(1)}, bf16[32,1792]{1,0:T(8,128)(2,1)S(1)}, u32[]{:S(2)}, u32[]{:S(2)}) collective-permute-start(bf16[32,1792]{1,0:T(8,128)(2,1)S(1)} %collective-permute-done.1.refs_1_), channel_id=1, source_target_pairs={{0,4},{4,0},{8,12},{12,8},{1,5},{5,1},{9,13},{13,9},{2,6},{6,2},{1... | collective-permute-start | bytes 344072 | tf_op jit(solution)/shard_map/ppermute | solution.py:35
  14.7 6.2 %collective-permute-start.9 = (bf16[40,1536]{1,0:T(8,128)(2,1)S(1)}, bf16[40,1536]{1,0:T(8,128)(2,1)S(1)}, u32[]{:S(2)}, u32[]{:S(2)}) collective-permute-start(bf16[40,1536]{1,0:T(8,128)(2,1)S(1)} %get-tuple-element.43), channel_id=1, source_target_pairs={{0,1},{1,0},{2,3},{3,2},{4,6},{5,7},{6,4},{7,5},{8,9},{9,8},{10,11... | collective-permute-start | bytes 368648 | tf_op jit(solution)/shard_map/ppermute | solution.py:46
  16.3 6.7 %collective-permute-start.7 = (bf16[40,1024]{1,0:T(8,128)(2,1)S(1)}, bf16[40,1024]{1,0:T(8,128)(2,1)S(1)}, u32[]{:S(2)}, u32[]{:S(2)}) collective-permute-start(bf16[40,1024]{1,0:T(8,128)(2,1)S(1)} %get-tuple-element.42), channel_id=1, source_target_pairs={{0,1},{1,0},{2,3},{3,2},{4,6},{5,7},{6,4},{7,5},{8,9},{9,8},{10,11... | collective-permute-start | bytes 245768 | tf_op jit(solution)/shard_map/ppermute | solution.py:46
  20.9 6.3 %collective-permute-start.10 = (bf16[40,1536]{1,0:T(8,128)(2,1)S(1)}, bf16[40,1536]{1,0:T(8,128)(2,1)S(1)}, u32[]{:S(2)}, u32[]{:S(2)}) collective-permute-start(bf16[40,1536]{1,0:T(8,128)(2,1)S(1)} %add_convert_fusion.a_ref), channel_id=1, source_target_pairs={{0,2},{1,3},{2,0},{3,1},{4,5},{5,4},{6,7},{7,6},{8,10},{9,11},{10,... | collective-permute-start | bytes 368648 | tf_op jit(solution)/shard_map/ppermute | solution.py:46
  23.0 6.1 %collective-permute-start.8 = (bf16[40,1024]{1,0:T(8,128)(2,1)S(1)}, bf16[40,1024]{1,0:T(8,128)(2,1)S(1)}, u32[]{:S(2)}, u32[]{:S(2)}) collective-permute-start(bf16[40,1024]{1,0:T(8,128)(2,1)S(1)} %add_convert_fusion.2.a_ref), channel_id=1, source_target_pairs={{0,2},{1,3},{2,0},{3,1},{4,5},{5,4},{6,7},{7,6},{8,10},{9,11},{10,... | collective-permute-start | bytes 245768 | tf_op jit(solution)/shard_map/ppermute | solution.py:46
  28.4 4.8 %copy-start = (s32[1,16,1]{1,2,0:T(1,128)S(1)}, s32[1,16,1]{1,2,0:T(1,128)}, u32[]{:S(2)}) copy-start(s32[1,16,1]{1,2,0:T(1,128)} %param.13) | copy-start | bytes 196
  28.4 4.8 %copy-start.1 = (bf16[1,16,1]{1,2,0:T(2,128)(2,1)S(1)}, bf16[1,16,1]{1,2,0:T(2,128)(2,1)}, u32[]{:S(2)}) copy-start(bf16[1,16,1]{1,2,0:T(2,128)(2,1)} %param.14) | copy-start | bytes 100
  28.4 4.8 %copy-start.2 = (s32[1,16,1]{1,2,0:T(1,128)S(1)}, s32[1,16,1]{1,2,0:T(1,128)}, u32[]{:S(2)}) copy-start(s32[1,16,1]{1,2,0:T(1,128)} %param.15) | copy-start | bytes 196
  28.4 4.8 %copy-start.3 = (bf16[1,16,1]{1,2,0:T(2,128)(2,1)S(1)}, bf16[1,16,1]{1,2,0:T(2,128)(2,1)}, u32[]{:S(2)}) copy-start(bf16[1,16,1]{1,2,0:T(2,128)(2,1)} %param.16) | copy-start | bytes 100
  29.7 1.5 %collective-permute-start.11 = (bf16[2,24,1792]{2,1,0:T(8,128)(2,1)S(1)}, bf16[2,24,1792]{2,1,0:T(8,128)(2,1)S(1)}, u32[]{:S(2)}, u32[]{:S(2)}) collective-permute-start(bf16[2,24,1792]{2,1,0:T(8,128)(2,1)S(1)} %get-tuple-element.45), channel_id=1, source_target_pairs={{0,4},{4,0},{8,12},{12,8},{1,5},{5,1},{9,13},{13,9},{2,6},{6,2},{1... | collective-permute-start | bytes 516104 | tf_op jit(solution)/shard_map/ppermute | solution.py:35
  31.2 4.8 %collective-permute-start.12 = (bf16[24,1792]{1,0:T(8,128)(2,1)S(1)}, bf16[24,1792]{1,0:T(8,128)(2,1)S(1)}, u32[]{:S(2)}, u32[]{:S(2)}) collective-permute-start(bf16[24,1792]{1,0:T(8,128)(2,1)S(1)} %fusion), channel_id=1, source_target_pairs={{0,8},{4,12},{8,0},{12,4},{1,9},{5,13},{9,1},{13,5},{2,10},{6,14},... | collective-permute-start | bytes 258056 | tf_op jit(solution)/shard_map/ppermute | solution.py:35

commit v10 on v9

--- a/solution.py
+++ b/solution.py
@@ -209,7 +209,7 @@
     turned = (((1,), (1,)), ((), ()))
     grad = lax.dot_general(dgate, w_g_ref[...], turned, preferred_element_type=F32)
     grad = grad + lax.dot_general(dupper, w_u_ref[...], turned, preferred_element_type=F32)
-    grad_ref[...] = grad
+    grad_ref[...] = grad.astype(BF16)
 
 
 def down_kernel(groups, a_ref, b_ref, grad_ref, slot_ref, w_d_ref, own_ref, other_ref):
@@ -218,7 +218,7 @@
     gate, upper = total[:, :units], total[:, units:]
     hidden = (gate * jax.nn.sigmoid(gate) * upper).astype(BF16)
     out = jnp.dot(hidden, w_d_ref[...], preferred_element_type=F32)
-    both = jnp.concatenate([out, grad_ref[...]], axis=0).astype(BF16)
+    both = jnp.concatenate([out, grad_ref[...].astype(F32)], axis=0).astype(BF16)
     full = jnp.dot(slot_ref[...], both, preferred_element_type=F32)
     slot_rows = own_ref.shape[1]
     for d in range(groups):
@@ -324,7 +324,7 @@
         part_b = (part_b.astype(F32) + came_b.astype(F32)).astype(BF16)
     grad = kernel_call(
         grad_kernel,
-        jax.ShapeDtypeStruct((rows, width), F32),
+        jax.ShapeDtypeStruct((rows, width), BF16),
         4 * rows * width * hidden,
         4 * width * hidden,
     )(part_b, came_b, w_g, w_u)

time: 37.1 us -> 37.1 us (level)
  no operation moved by 1% of the time
where the time goes in v10:
time: 37.1 us; the launch traced here: 36.9 us
  waiting for transfers between devices  15.1 us (41%)
  starting transfers between devices  12.9 us (35%)
  Pallas kernels  7.99 us (22%)
  between operations  0.76 us (2%)
    ppermute x4, waiting for transfers between devices, mixed(): return lax.ppermute(x, ('expert', 'dp'), pairs)  7.51 us
    ppermute x4, starting transfers between devices, mixed(): return lax.ppermute(x, ('expert', 'dp'), pairs)  5.61 us
    ppermute x7, waiting for transfers between devices, swap(): return lax.ppermute(x, axis, [(i, i ^ bit) for i in range(peers)])  5.26 us
    ppermute x7, starting transfers between devices, swap(): return lax.ppermute(x, axis, [(i, i ^ bit) for i in range(peers)])  4.3 us
    ppermute x2, starting transfers between devices, onward(): return lax.ppermute(x, ('pipe', 'expert'), pairs)  3.02 us
    pallas_call x1, Pallas kernels, local(): pl.pallas_call(fetch_kernel, out_shape=[pltpu.VMEM(w.shape[2:], BF16) for...  2.63 us
    ppermute x2, waiting for transfers between devices, onward(): return lax.ppermute(x, ('pipe', 'expert'), pairs)  2.36 us
    pallas_call x1, Pallas kernels, local(): kernel_call(functools.partial(up_kernel, groups, topk, rows, capacity, sl...  1.43 us
  transfers between devices with their start and end apart: 13, of which 7 were waited for; matrix products, arithmetic and copies ran while one was open for 0% of the time, Pallas kernels for 11%

profile of v10, /device:TPU:0, one launch (start us, length us, event | category | flops | bytes accessed | tf_op | source)
XLA Modules:
  0.0 36.9 jit_solution(16078826458628183074)
XLA Ops:
  0.6 1.0 %shard_map.113 = (bf16[32,1792]{1,0:T(8,128)(2,1)S(1)}, bf16[16,1920]{1,0:T(8,128)(2,1)S(1)}) custom-call(bf16[16,1792]{1,0:T(8,128)(2,1)} %bitcast.25, bf16[16,1792]{1,0:T(8,128)(2,1)} %bitcast.26, bf16[16,1792]{1,0:T(8,128)(2,1)} %bitcast.27, s32[1,16]{1,0:T(1,128)} %bitcast.14, bf16[1,16]{1,0:T(2,128)(2,1)} %bitcast.16, s32[1,16]{1,0:T(1,128)} %bitcast.18, ...), custom_call_target="tpu_custom_call" | custom-call | bytes 344064 | tf_op jit(solution)/shard_map/pallas_call | solution.py:277
  1.6 3.0 %collective-permute-start = (bf16[32,1792]{1,0:T(8,128)(2,1)S(1)}, bf16[32,1792]{1,0:T(8,128)(2,1)S(1)}, u32[]{:S(2)}, u32[]{:S(2)}) collective-permute-start(bf16[32,1792]{1,0:T(8,128)(2,1)S(1)} %get-tuple-element.25), channel_id=1, source_target_pairs={{0,16},{4,20},{8,24},{12,28},{16,0},{20,4},{24,8},{28,12},{1,17},{... | collective-permute-start | bytes 344072 | tf_op jit(solution)/shard_map/ppermute | solution.py:57
  4.6 1.5 %collective-permute-start.3 = (bf16[16,1920]{1,0:T(8,128)(2,1)S(1)}, bf16[16,1920]{1,0:T(8,128)(2,1)S(1)}, u32[]{:S(2)}, u32[]{:S(2)}) collective-permute-start(bf16[16,1920]{1,0:T(8,128)(2,1)S(1)} %get-tuple-element.32.refs_4_), channel_id=1, source_target_pairs={{0,8},{4,12},{8,0},{12,4},{1,9},{5,13},{9,1},{13,5},{2,10},{6,14},... | collective-permute-start | bytes 184328 | tf_op jit(solution)/shard_map/ppermute | solution.py:35
  6.2 0.0 collective-permute-start.1
  6.2 2.6 %shard_map.114 = (bf16[1792,512]{1,0:T(8,128)(2,1)S(1)}, bf16[1792,512]{1,0:T(8,128)(2,1)S(1)}, bf16[512,1792]{1,0:T(8,128)(2,1)S(1)}) custom-call(bf16[1792,512]{1,0:T(8,128)(2,1)} %bitcast.22, bf16[1792,512]{1,0:T(8,128)(2,1)} %bitcast.23, bf16[512,1792]{1,0:T(8,128)(2,1)} %bitcast.24), custom_call_target="tpu_custom_call" | custom-call | bytes 11010048 | tf_op jit(solution)/shard_map/pallas_call | solution.py:263
  8.8 0.1 collective-permute-start.2
  8.9 0.5 %collective-permute-start.4 = (bf16[16,1920]{1,0:T(8,128)(2,1)S(1)}, bf16[16,1920]{1,0:T(8,128)(2,1)S(1)}, u32[]{:S(2)}, u32[]{:S(2)}) collective-permute-start(bf16[16,1920]{1,0:T(8,128)(2,1)S(1)} %get-tuple-element.32.refs_4_), channel_id=1, source_target_pairs={{0,4},{4,0},{8,12},{12,8},{1,5},{5,1},{9,13},{13,9},{2,6},{6,2},{1... | collective-permute-start | bytes 184328 | tf_op jit(solution)/shard_map/ppermute | solution.py:35
  9.4 0.1 collective-permute-start.5
  9.5 2.4 %collective-permute-done.1.refs_1_ = bf16[32,1792]{1,0:T(8,128)(2,1)S(1)} collective-permute-done((bf16[32,1792]{1,0:T(8,128)(2,1)S(1)}, bf16[32,1792]{1,0:T(8,128)(2,1)S(1)}, u32[]{:S(2)}, u32[]{:S(2)}) %collective-permute-start.1) | collective-permute-done | bytes 114720 | tf_op jit(solution)/shard_map/ppermute | solution.py:57
  11.9 0.0 collective-permute-done.4.refs_6_
  11.9 0.1 collective-permute-start.6
  11.9 1.3 %collective-permute-done.6.refs_3_ = bf16[32,1792]{1,0:T(8,128)(2,1)S(1)} collective-permute-done((bf16[32,1792]{1,0:T(8,128)(2,1)S(1)}, bf16[32,1792]{1,0:T(8,128)(2,1)S(1)}, u32[]{:S(2)}, u32[]{:S(2)}) %collective-permute-start.6) | collective-permute-done | bytes 114720 | tf_op jit(solution)/shard_map/ppermute | solution.py:35
  13.3 1.4 %shard_map.115 = (bf16[40,1024]{1,0:T(8,128)(2,1)S(1)}, bf16[40,1536]{1,0:T(8,128)(2,1)S(1)}, bf16[96,80]{1,0:T(8,128)(2,1)S(1)}) custom-call(bf16[32,1792]{1,0:T(8,128)(2,1)S(1)} %collective-permute-done.refs_0_.moved_ref, bf16[32,1792]{1,0:T(8,128)(2,1)S(1)} %collective-permute-done.1.refs_1_, bf16[32,1792]{1,0:T(8,128)(2,1)S(1)} %collective-permute-done.2.refs_2_, ...), custom_call_target="tpu_custom_call" | custom-call | flops 367001600 | bytes 5505024 | tf_op jit(solution)/shard_map/pallas_call | solution.py:306
  14.7 1.6 %collective-permute-start.9 = (bf16[40,1536]{1,0:T(8,128)(2,1)S(1)}, bf16[40,1536]{1,0:T(8,128)(2,1)S(1)}, u32[]{:S(2)}, u32[]{:S(2)}) collective-permute-start(bf16[40,1536]{1,0:T(8,128)(2,1)S(1)} %get-tuple-element.43), channel_id=1, source_target_pairs={{0,1},{1,0},{2,3},{3,2},{4,6},{5,7},{6,4},{7,5},{8,9},{9,8},{10,11... | collective-permute-start | bytes 368648 | tf_op jit(solution)/shard_map/ppermute | solution.py:46
  16.3 0.5 %collective-permute-start.7 = (bf16[40,1024]{1,0:T(8,128)(2,1)S(1)}, bf16[40,1024]{1,0:T(8,128)(2,1)S(1)}, u32[]{:S(2)}, u32[]{:S(2)}) collective-permute-start(bf16[40,1024]{1,0:T(8,128)(2,1)S(1)} %get-tuple-element.42), channel_id=1, source_target_pairs={{0,1},{1,0},{2,3},{3,2},{4,6},{5,7},{6,4},{7,5},{8,9},{9,8},{10,11... | collective-permute-start | bytes 245768 | tf_op jit(solution)/shard_map/ppermute | solution.py:46
  16.8 4.1 %collective-permute-done.9 = bf16[40,1536]{1,0:T(8,128)(2,1)S(1)} collective-permute-done((bf16[40,1536]{1,0:T(8,128)(2,1)S(1)}, bf16[40,1536]{1,0:T(8,128)(2,1)S(1)}, u32[]{:S(2)}, u32[]{:S(2)}) %collective-permute-start.9) | collective-permute-done | bytes 122912 | tf_op jit(solution)/shard_map/ppermute | solution.py:46
  20.9 2.1 %collective-permute-start.10 = (bf16[40,1536]{1,0:T(8,128)(2,1)S(1)}, bf16[40,1536]{1,0:T(8,128)(2,1)S(1)}, u32[]{:S(2)}, u32[]{:S(2)}) collective-permute-start(bf16[40,1536]{1,0:T(8,128)(2,1)S(1)} %add_convert_fusion.a_ref), channel_id=1, source_target_pairs={{0,2},{1,3},{2,0},{3,1},{4,5},{5,4},{6,7},{7,6},{8,10},{9,11},{10,... | collective-permute-start | bytes 368648 | tf_op jit(solution)/shard_map/ppermute | solution.py:46
  23.0 1.4 %collective-permute-start.8 = (bf16[40,1024]{1,0:T(8,128)(2,1)S(1)}, bf16[40,1024]{1,0:T(8,128)(2,1)S(1)}, u32[]{:S(2)}, u32[]{:S(2)}) collective-permute-start(bf16[40,1024]{1,0:T(8,128)(2,1)S(1)} %add_convert_fusion.2.a_ref), channel_id=1, source_target_pairs={{0,2},{1,3},{2,0},{3,1},{4,5},{5,4},{6,7},{7,6},{8,10},{9,11},{10,... | collective-permute-start | bytes 245768 | tf_op jit(solution)/shard_map/ppermute | solution.py:46
  24.5 2.7 %collective-permute-done.10.b_ref = bf16[40,1536]{1,0:T(8,128)(2,1)S(1)} collective-permute-done((bf16[40,1536]{1,0:T(8,128)(2,1)S(1)}, bf16[40,1536]{1,0:T(8,128)(2,1)S(1)}, u32[]{:S(2)}, u32[]{:S(2)}) %collective-permute-start.10) | collective-permute-done | bytes 122912 | tf_op jit(solution)/shard_map/ppermute | solution.py:46
  27.2 1.2 %shard_map.117.grad_ref = bf16[40,1792]{1,0:T(8,128)(2,1)S(1)} custom-call(bf16[40,1536]{1,0:T(8,128)(2,1)S(1)} %add_convert_fusion.a_ref, bf16[40,1536]{1,0:T(8,128)(2,1)S(1)} %collective-permute-done.10.b_ref, bf16[1792,512]{1,0:T(8,128)(2,1)S(1)} %get-tuple-element.34.refs_8_.w_g_ref, bf16[1792,512]{1,0:T(8,128)(2,1)S(1)} %get-tuple-element.35.refs_9_.w_u_ref), custom_call_target="tpu_custom_call" | custom-call | flops 146800640 | bytes 3670016 | tf_op jit(solution)/shard_map/pallas_call | solution.py:325
  28.4 0.0 copy-start
  28.4 0.0 copy-start.1
  28.4 0.0 copy-start.2
  28.4 0.0 copy-start.3
  28.5 0.7 %collective-permute-done.8.b_ref = bf16[40,1024]{1,0:T(8,128)(2,1)S(1)} collective-permute-done((bf16[40,1024]{1,0:T(8,128)(2,1)S(1)}, bf16[40,1024]{1,0:T(8,128)(2,1)S(1)}, u32[]{:S(2)}, u32[]{:S(2)}) %collective-permute-start.8) | collective-permute-done | bytes 81952 | tf_op jit(solution)/shard_map/ppermute | solution.py:46
  29.1 0.6 %shard_map.118 = (bf16[2,24,1792]{2,1,0:T(8,128)(2,1)S(1)}, bf16[2,24,1792]{2,1,0:T(8,128)(2,1)S(1)}) custom-call(bf16[40,1024]{1,0:T(8,128)(2,1)S(1)} %add_convert_fusion.2.a_ref, bf16[40,1024]{1,0:T(8,128)(2,1)S(1)} %collective-permute-done.8.b_ref, bf16[40,1792]{1,0:T(8,128)(2,1)S(1)} %shard_map.117.grad_ref, ...), custom_call_target="tpu_custom_call" | custom-call | flops 73400320 | bytes 1835008 | tf_op jit(solution)/shard_map/pallas_call | solution.py:331
  29.7 0.1 collective-permute-start.11
  29.8 1.4 %collective-permute-done.11.other_ref = bf16[2,24,1792]{2,1,0:T(8,128)(2,1)S(1)} collective-permute-done((bf16[2,24,1792]{2,1,0:T(8,128)(2,1)S(1)}, bf16[2,24,1792]{2,1,0:T(8,128)(2,1)S(1)}, u32[]{:S(2)}, u32[]{:S(2)}) %collective-permute-start.11) | collective-permute-done | bytes 172064 | tf_op jit(solution)/shard_map/ppermute | solution.py:35
  31.2 2.0 %collective-permute-start.12 = (bf16[24,1792]{1,0:T(8,128)(2,1)S(1)}, bf16[24,1792]{1,0:T(8,128)(2,1)S(1)}, u32[]{:S(2)}, u32[]{:S(2)}) collective-permute-start(bf16[24,1792]{1,0:T(8,128)(2,1)S(1)} %fusion), channel_id=1, source_target_pairs={{0,8},{4,12},{8,0},{12,4},{1,9},{5,13},{9,1},{13,5},{2,10},{6,14},... | collective-permute-start | bytes 258056 | tf_op jit(solution)/shard_map/ppermute | solution.py:35
  33.2 0.3 shard_map.116.home_ref
  33.5 2.5 %collective-permute-done.12.refs_0_ = bf16[24,1792]{1,0:T(8,128)(2,1)S(1)} collective-permute-done((bf16[24,1792]{1,0:T(8,128)(2,1)S(1)}, bf16[24,1792]{1,0:T(8,128)(2,1)S(1)}, u32[]{:S(2)}, u32[]{:S(2)}) %collective-permute-start.12) | collective-permute-done | bytes 86048 | tf_op jit(solution)/shard_map/ppermute | solution.py:35
  36.1 0.9 %shard_map.119 = (bf16[16,1792]{1,0:T(8,128)(2,1)}, bf16[16,1792]{1,0:T(8,128)(2,1)}) custom-call(bf16[32,1792]{1,0:T(8,128)(2,1)S(1)} %collective-permute-done.refs_0_.moved_ref, bf16[2,32,24]{2,1,0:T(8,128)(2,1)S(1)} %shard_map.116.home_ref, bf16[2,24,1792]{2,1,0:T(8,128)(2,1)S(1)} %get-tuple-element.44.own_ref, ...), custom_call_target="tpu_custom_call" | custom-call | bytes 573440 | tf_op jit(solution)/shard_map/pallas_call | solution.py:350
  (12 shorter events, 0.1 us)
Async XLA Ops:
  1.6 7.2 %collective-permute-start = (bf16[32,1792]{1,0:T(8,128)(2,1)S(1)}, bf16[32,1792]{1,0:T(8,128)(2,1)S(1)}, u32[]{:S(2)}, u32[]{:S(2)}) collective-permute-start(bf16[32,1792]{1,0:T(8,128)(2,1)S(1)} %get-tuple-element.25), channel_id=1, source_target_pairs={{0,16},{4,20},{8,24},{12,28},{16,0},{20,4},{24,8},{28,12},{1,17},{... | collective-permute-start | bytes 344072 | tf_op jit(solution)/shard_map/ppermute | solution.py:57
  4.6 4.8 %collective-permute-start.3 = (bf16[16,1920]{1,0:T(8,128)(2,1)S(1)}, bf16[16,1920]{1,0:T(8,128)(2,1)S(1)}, u32[]{:S(2)}, u32[]{:S(2)}) collective-permute-start(bf16[16,1920]{1,0:T(8,128)(2,1)S(1)} %get-tuple-element.32.refs_4_), channel_id=1, source_target_pairs={{0,8},{4,12},{8,0},{12,4},{1,9},{5,13},{9,1},{13,5},{2,10},{6,14},... | collective-permute-start | bytes 184328 | tf_op jit(solution)/shard_map/ppermute | solution.py:35
  6.2 5.7 %collective-permute-start.1 = (bf16[32,1792]{1,0:T(8,128)(2,1)S(1)}, bf16[32,1792]{1,0:T(8,128)(2,1)S(1)}, u32[]{:S(2)}, u32[]{:S(2)}) collective-permute-start(bf16[32,1792]{1,0:T(8,128)(2,1)S(1)} %get-tuple-element.25), channel_id=1, source_target_pairs={{0,24},{4,28},{8,16},{12,20},{16,8},{20,12},{24,0},{28,4},{1,25},{... | collective-permute-start | bytes 344072 | tf_op jit(solution)/shard_map/ppermute | solution.py:57
  8.8 3.0 %collective-permute-start.2 = (bf16[32,1792]{1,0:T(8,128)(2,1)S(1)}, bf16[32,1792]{1,0:T(8,128)(2,1)S(1)}, u32[]{:S(2)}, u32[]{:S(2)}) collective-permute-start(bf16[32,1792]{1,0:T(8,128)(2,1)S(1)} %collective-permute-done.refs_0_.moved_ref), channel_id=1, source_target_pairs={{0,4},{4,0},{8,12},{12,8},{1,5},{5,1},{9,13},{13,9},{2,6},{6,2},{1... | collective-permute-start | bytes 344072 | tf_op jit(solution)/shard_map/ppermute | solution.py:35
  8.9 2.9 %collective-permute-start.4 = (bf16[16,1920]{1,0:T(8,128)(2,1)S(1)}, bf16[16,1920]{1,0:T(8,128)(2,1)S(1)}, u32[]{:S(2)}, u32[]{:S(2)}) collective-permute-start(bf16[16,1920]{1,0:T(8,128)(2,1)S(1)} %get-tuple-element.32.refs_4_), channel_id=1, source_target_pairs={{0,4},{4,0},{8,12},{12,8},{1,5},{5,1},{9,13},{13,9},{2,6},{6,2},{1... | collective-permute-start | bytes 184328 | tf_op jit(solution)/shard_map/ppermute | solution.py:35
  9.4 2.4 %collective-permute-start.5 = (bf16[16,1920]{1,0:T(8,128)(2,1)S(1)}, bf16[16,1920]{1,0:T(8,128)(2,1)S(1)}, u32[]{:S(2)}, u32[]{:S(2)}) collective-permute-start(bf16[16,1920]{1,0:T(8,128)(2,1)S(1)} %collective-permute-done.3.refs_5_), channel_id=1, source_target_pairs={{0,4},{4,0},{8,12},{12,8},{1,5},{5,1},{9,13},{13,9},{2,6},{6,2},{1... | collective-permute-start | bytes 184328 | tf_op jit(solution)/shard_map/ppermute | solution.py:35
  11.9 1.4 %collective-permute-start.6 = (bf16[32,1792]{1,0:T(8,128)(2,1)S(1)}, bf16[32,1792]{1,0:T(8,128)(2,1)S(1)}, u32[]{:S(2)}, u32[]{:S(2)}) collective-permute-start(bf16[32,1792]{1,0:T(8,128)(2,1)S(1)} %collective-permute-done.1.refs_1_), channel_id=1, source_target_pairs={{0,4},{4,0},{8,12},{12,8},{1,5},{5,1},{9,13},{13,9},{2,6},{6,2},{1... | collective-permute-start | bytes 344072 | tf_op jit(solution)/shard_map/ppermute | solution.py:35
  14.7 6.2 %collective-permute-start.9 = (bf16[40,1536]{1,0:T(8,128)(2,1)S(1)}, bf16[40,1536]{1,0:T(8,128)(2,1)S(1)}, u32[]{:S(2)}, u32[]{:S(2)}) collective-permute-start(bf16[40,1536]{1,0:T(8,128)(2,1)S(1)} %get-tuple-element.43), channel_id=1, source_target_pairs={{0,1},{1,0},{2,3},{3,2},{4,6},{5,7},{6,4},{7,5},{8,9},{9,8},{10,11... | collective-permute-start | bytes 368648 | tf_op jit(solution)/shard_map/ppermute | solution.py:46
  16.3 6.7 %collective-permute-start.7 = (bf16[40,1024]{1,0:T(8,128)(2,1)S(1)}, bf16[40,1024]{1,0:T(8,128)(2,1)S(1)}, u32[]{:S(2)}, u32[]{:S(2)}) collective-permute-start(bf16[40,1024]{1,0:T(8,128)(2,1)S(1)} %get-tuple-element.42), channel_id=1, source_target_pairs={{0,1},{1,0},{2,3},{3,2},{4,6},{5,7},{6,4},{7,5},{8,9},{9,8},{10,11... | collective-permute-start | bytes 245768 | tf_op jit(solution)/shard_map/ppermute | solution.py:46
  20.9 6.3 %collective-permute-start.10 = (bf16[40,1536]{1,0:T(8,128)(2,1)S(1)}, bf16[40,1536]{1,0:T(8,128)(2,1)S(1)}, u32[]{:S(2)}, u32[]{:S(2)}) collective-permute-start(bf16[40,1536]{1,0:T(8,128)(2,1)S(1)} %add_convert_fusion.a_ref), channel_id=1, source_target_pairs={{0,2},{1,3},{2,0},{3,1},{4,5},{5,4},{6,7},{7,6},{8,10},{9,11},{10,... | collective-permute-start | bytes 368648 | tf_op jit(solution)/shard_map/ppermute | solution.py:46
  23.0 6.1 %collective-permute-start.8 = (bf16[40,1024]{1,0:T(8,128)(2,1)S(1)}, bf16[40,1024]{1,0:T(8,128)(2,1)S(1)}, u32[]{:S(2)}, u32[]{:S(2)}) collective-permute-start(bf16[40,1024]{1,0:T(8,128)(2,1)S(1)} %add_convert_fusion.2.a_ref), channel_id=1, source_target_pairs={{0,2},{1,3},{2,0},{3,1},{4,5},{5,4},{6,7},{7,6},{8,10},{9,11},{10,... | collective-permute-start | bytes 245768 | tf_op jit(solution)/shard_map/ppermute | solution.py:46
  28.4 4.8 %copy-start = (s32[1,16,1]{1,2,0:T(1,128)S(1)}, s32[1,16,1]{1,2,0:T(1,128)}, u32[]{:S(2)}) copy-start(s32[1,16,1]{1,2,0:T(1,128)} %param.13) | copy-start | bytes 196
  28.4 4.8 %copy-start.1 = (bf16[1,16,1]{1,2,0:T(2,128)(2,1)S(1)}, bf16[1,16,1]{1,2,0:T(2,128)(2,1)}, u32[]{:S(2)}) copy-start(bf16[1,16,1]{1,2,0:T(2,128)(2,1)} %param.14) | copy-start | bytes 100
  28.4 4.8 %copy-start.2 = (s32[1,16,1]{1,2,0:T(1,128)S(1)}, s32[1,16,1]{1,2,0:T(1,128)}, u32[]{:S(2)}) copy-start(s32[1,16,1]{1,2,0:T(1,128)} %param.15) | copy-start | bytes 196
  28.4 4.8 %copy-start.3 = (bf16[1,16,1]{1,2,0:T(2,128)(2,1)S(1)}, bf16[1,16,1]{1,2,0:T(2,128)(2,1)}, u32[]{:S(2)}) copy-start(bf16[1,16,1]{1,2,0:T(2,128)(2,1)} %param.16) | copy-start | bytes 100
  29.7 1.5 %collective-permute-start.11 = (bf16[2,24,1792]{2,1,0:T(8,128)(2,1)S(1)}, bf16[2,24,1792]{2,1,0:T(8,128)(2,1)S(1)}, u32[]{:S(2)}, u32[]{:S(2)}) collective-permute-start(bf16[2,24,1792]{2,1,0:T(8,128)(2,1)S(1)} %get-tuple-element.45), channel_id=1, source_target_pairs={{0,4},{4,0},{8,12},{12,8},{1,5},{5,1},{9,13},{13,9},{2,6},{6,2},{1... | collective-permute-start | bytes 516104 | tf_op jit(solution)/shard_map/ppermute | solution.py:35
  31.2 4.8 %collective-permute-start.12 = (bf16[24,1792]{1,0:T(8,128)(2,1)S(1)}, bf16[24,1792]{1,0:T(8,128)(2,1)S(1)}, u32[]{:S(2)}, u32[]{:S(2)}) collective-permute-start(bf16[24,1792]{1,0:T(8,128)(2,1)S(1)} %fusion), channel_id=1, source_target_pairs={{0,8},{4,12},{8,0},{12,4},{1,9},{5,13},{9,1},{13,5},{2,10},{6,14},... | collective-permute-start | bytes 258056 | tf_op jit(solution)/shard_map/ppermute | solution.py:35
